TPU v7x, 256 devices: a whole 4x4x8 slice. The times are simulated.
256 devices in a mesh: section: 2 (over y_lo), dp: 4 (over y_hi, core), vocab: 32 (over z, x).
Axes of the slice: x: 4, y: 4 (y_hi: 2, y_lo: 2; y = y_hi * 2 + y_lo), z: 8, core: 2. Of those that a mesh axis runs over, the one named last changes fastest.
Arguments:
- stacked_rows: bfloat16 [2, 384, 4608], P('section', ('dp', 'vocab')), as said below
- tied_table: bfloat16 [131072, 4608], P(('section', 'dp', 'vocab')), as said below
- row_ids: int32 [2, 384], replicated, may hold values from 0 to 131071, as said below
Outputs:
- table_grad: bfloat16 [131072, 4608], P(('section', 'dp', 'vocab'))
- hidden_grad: bfloat16 [384, 4608], P(('dp', 'vocab'))
Inputs may be any that keep to these rules, and one draw needn't show every extreme that they name: `stacked_rows`: rows of slot 0 and slot 1 are real-valued draws. `tied_table`: Real-valued table rows. `row_ids`: token ids of the vocabulary; an id may recur.
All inputs are finite; a program needn't handle non-finite values.
Results may differ from a plain program's by a relative error of at most 0.007.
Values may be sent and summed in bfloat16 or wider, within the bound.
No kernel may reach another device: no remote copies, remote signals or barrier semaphores. Data moves between devices by JAX's collectives and lax.ppermute only.
A program may use at most 128 MiB of HBM per device.

v0:
```python
import math

import jax
import jax.numpy as jnp
from jax import lax
from jax.sharding import PartitionSpec as P

D = 4608


def shards(stacked_rows, tied_table, row_ids):
    factor = jnp.asarray(math.sqrt(D), jnp.float32).astype(jnp.bfloat16).astype(jnp.float32)
    shard_rows = tied_table.shape[0]
    section_index = lax.axis_index("section")
    owner = (section_index * lax.axis_size("dp") + lax.axis_index("dp")) * lax.axis_size(
        "vocab"
    ) + lax.axis_index("vocab")
    first_column = owner * shard_rows
    own_rows = stacked_rows[0]
    local_rows = own_rows.shape[0]
    section_total = local_rows * lax.axis_size("dp") * lax.axis_size("vocab")
    everything = lax.all_gather(own_rows, ("section", "dp", "vocab"), axis=0, tiled=True)
    cotangent = everything[:section_total]
    hidden = everything[section_total:]
    columns = first_column + lax.iota(jnp.int32, shard_rows)
    onehot = (row_ids[1][:, None] == columns[None, :]).astype(jnp.float32)
    logits = lax.dot_general(
        hidden, tied_table, (((1,), (1,)), ((), ())), preferred_element_type=jnp.float32
    )
    local_high = jnp.max(logits, axis=1, keepdims=True)
    highest = lax.pmax(local_high, ("section", "dp", "vocab"))
    expvals = jnp.exp(logits - highest)
    totals = lax.psum(jnp.sum(expvals, axis=1, keepdims=True), ("section", "dp", "vocab"))
    coefficient = (expvals / totals - onehot).astype(jnp.bfloat16)
    head_grad = lax.dot_general(
        coefficient, hidden, (((0,), (0,)), ((), ())), preferred_element_type=jnp.float32
    )
    local_ids = row_ids[0] - first_column
    inside = (local_ids >= 0) & (local_ids < shard_rows)
    segment_ids = jnp.where(inside, local_ids, shard_rows)
    embed_sums = jax.ops.segment_sum(cotangent.astype(jnp.float32), segment_ids, shard_rows + 1)[
        :shard_rows
    ]
    table_grad = (head_grad + factor * embed_sums).astype(jnp.bfloat16)
    section_part = lax.psum_scatter(
        jnp.dot(coefficient, tied_table, preferred_element_type=jnp.float32),
        ("dp", "vocab"),
        scatter_dimension=0,
        tiled=True,
    )
    hidden_sum = lax.psum(section_part, "section")
    return (table_grad, hidden_sum.astype(jnp.bfloat16))


def solution(mesh):
    placed = (P("section", ("dp", "vocab"), None), P(("section", "dp", "vocab"), None), P())
    return jax.shard_map(
        shards,
        mesh=mesh,
        in_specs=placed,
        out_specs=(P(("section", "dp", "vocab"), None), P(("dp", "vocab"), None)),
        check_vma=False,
    )
```

profile of v0, /device:TPU:8, one launch (start us, length us, event | category | flops | bytes accessed | tf_op | source)
XLA Modules:
  0.0 2224.1 jit_solution(15656668552202176900)
XLA Ops:
  7.2 0.0 all-gather.3.cloned.1.call-start
  7.2 1.4 copy.7
  8.6 0.0 all-gather.3.cloned.1.call-update
  8.7 0.0 all-reduce.3.cloned.1.call-start
  8.7 0.7 slice_reduce_fusion
  9.4 704.7 %all-gather.3.cloned.1.call-done = bf16[1,768,4608]{2,0,1:T(2,128)(2,1)} async-done(((bf16[1,3,4608]{2,0,1:T(2,128)(2,1)}), bf16[1,768,4608]{2,0,1:T(2,128)(2,1)}) %all-gather.3.cloned.1.call-update) | async-done | bytes 7077904 | tf_op jit(solution)/shard_map/all_gather | solution.py:22
  714.2 0.0 copy-start.1
  714.2 17.3 fusion.9
  731.5 0.0 copy-start
  731.5 3.0 copy-done
  734.4 0.0 copy-done.1
  734.5 2.1 fusion.10
  736.6 105.2 %pmax.7 = f32[384]{0:T(512)S(1)} all-reduce(f32[384]{0:T(512)S(1)} %get-tuple-element.4), channel_id=1, replica_groups=mesh['section'=2,'dp'=4,'vocab'=32] {'section','dp','vocab'}, use_global_device_ids=true, to_apply=%region_1.0 | all-reduce | flops 384 | bytes 3072 | tf_op jit(solution)/shard_map/pmax | solution.py:31
  841.8 0.3 fusion.6
  842.0 73.4 %psum.14 = f32[384]{0:T(512)S(1)} all-reduce(f32[384]{0:T(512)S(1)} %fusion.6), channel_id=1, replica_groups=mesh['section'=2,'dp'=4,'vocab'=32] {'section','dp','vocab'}, use_global_device_ids=true, to_apply=%region_3.0 | all-reduce | flops 384 | bytes 3072 | tf_op jit(solution)/shard_map/psum | solution.py:33
  915.4 0.0 copy-start.3
  915.4 0.0 copy-start.2
  915.4 7.5 fusion.8
  922.9 0.0 all-reduce.3.cloned.1.call-update
  922.9 0.0 copy-done.3
  922.9 0.6 dynamic-slice
  924.2 0.0 copy-done.2
  924.2 16.4 scatter_custom_fusion
  940.6 10.9 fusion.1
  951.6 1255.6 %all-reduce.3.cloned.1.call-done = f32[384,4608]{1,0:T(8,128)} async-done(((f32[384,4608]{1,0:T(8,128)}), f32[384,4608]{1,0:T(8,128)}) %all-reduce.3.cloned.1.call-update) | async-done | bytes 7077904
  2207.2 1.0 constant_dynamic-slice_fusion
  2208.1 9.1 psum.15
  (2 shorter events, 0.0 us)
Async XLA Ops:
  7.2 707.0 %all-gather.3.cloned.1.call-start = ((), (), s32[]{:S(2)}) async-start(), calls=%async_computation | async-start | bytes 14211072 | tf_op jit(solution)/shard_map/all_gather | solution.py:22
  8.7 2198.5 %all-reduce.3.cloned.1.call-start = ((), (), s32[]{:S(2)}) async-start(), calls=%async_computation.1 | async-start | bytes 14155776
  714.2 20.3 copy-start.1
  731.5 3.0 copy-start
  915.4 7.5 copy-start.3
  915.4 8.8 copy-start.2
Sparse Core Ops, SparseCore 0:
  10.5 703.6 all-gather.2
  923.0 1284.0 all-reduce.2
where the time goes:
time: 2230 us; the launch traced here: 2220 us
  waiting for transfers between devices  1960 us (88%)
  blocking collectives  188 us (8%)
  local copies, waits for them, and re-layouts  24 us (1%)
    unnamed x3, waiting for transfers between devices  1260 us
    all_gather x1, waiting for transfers between devices, shards(): lax.all_gather(own_rows, ('section', 'dp', 'vocab'), axis=0, tiled=True)  705 us
    pmax x1, blocking collectives, shards(): highest = lax.pmax(local_high, ('section', 'dp', 'vocab'))  105 us
    psum x1, blocking collectives, shards(): lax.psum(jnp.sum(expvals, axis=1, keepdims=True), ('section', 'dp', 'voca...  73.4 us
  transfers between devices with their start and end apart: 2, of which 2 were waited for; matrix products, arithmetic and copies ran while one was open for 1% of the time, Pallas kernels for 0%

commit v1 on v0

v1 whole, which is shorter than its diff:
```python
import math

import jax
import jax.numpy as jnp
from jax import lax
from jax.sharding import PartitionSpec as P

D = 4608
HALF = D // 2
AXES = ("section", "dp", "vocab")
SIZES = {"yl": 2, "yh": 2, "core": 2, "z": 8, "x": 4}


def place(device):
    vocab, dp, section = device % 32, device // 32 % 4, device // 128
    return {"yl": section, "yh": dp // 2, "core": dp % 2, "z": vocab // 4, "x": vocab % 4}


def groups(*axes):
    found = {}
    for device in range(256):
        at = place(device)
        key = tuple(at[a] for a in SIZES if a not in axes)
        found.setdefault(key, []).append((tuple(at[a] for a in axes), device))
    return [[device for _, device in sorted(members)] for members in found.values()]


def exchange(blocks, *axes):
    return lax.all_to_all(blocks, AXES, 0, 0, axis_index_groups=groups(*axes), tiled=True)


def other_core(array):
    pairs = [pair for a, b in groups("core") for pair in ((a, b), (b, a))]
    return lax.ppermute(array, AXES, pairs)


def by_core(ids):
    return ids.reshape(2, 2, 8, 4, 3).transpose(1, 0, 3, 2, 4).reshape(2, 192)


def shards(stacked_rows, tied_table, row_ids):
    factor = jnp.asarray(math.sqrt(D), jnp.float32).astype(jnp.bfloat16)
    shard_rows = tied_table.shape[0]
    core = lax.axis_index("dp") % 2
    owner = (lax.axis_index("section") * 4 + lax.axis_index("dp")) * 32 + lax.axis_index("vocab")
    columns = owner * shard_rows + lax.iota(jnp.int32, shard_rows)
    table = (tied_table[:, :HALF], tied_table[:, HALF:])

    with jax.named_scope("rows_lz"):
        own = stacked_rows[0].reshape(3, 2, HALF).transpose(1, 0, 2)
        blocks = jnp.broadcast_to(own[:, None], (2, 8, 3, HALF)).reshape(16, 3, HALF)
        got = exchange(blocks, "yl", "z").reshape(2, 24, HALF)
    with jax.named_scope("cotangent"):
        cotangent = lax.all_gather(
            got[0], AXES, axis_index_groups=groups("yl", "core", "yh", "x"), axis=0, tiled=True
        ).reshape(2, 384, HALF)
    with jax.named_scope("hidden_xy"):
        mine = exchange(jnp.broadcast_to(got[1], (16, 24, HALF)), "yl", "yh", "x").reshape(2, 192, HALF)
    with jax.named_scope("hidden_core"):
        hidden = jnp.concatenate([mine, other_core(mine)], axis=1)

    with jax.named_scope("logits"):
        logits = sum(
            lax.dot_general(hidden[i], table[i], (((1,), (1,)), ((), ())), preferred_element_type=jnp.float32)
            for i in range(2)
        )
    with jax.named_scope("stats"):
        high = jnp.max(logits, axis=1)
        total = jnp.sum(jnp.exp(logits - high[:, None]), axis=1)
        stats = jnp.stack([high, total]).reshape(2, 2, 192)
        stats = jnp.where(core == 0, stats, stats[:, ::-1]).reshape(1, 2, 384)

        def combine(parts):
            top = jnp.max(parts[:, 0], axis=0)
            return jnp.stack([top, jnp.sum(parts[:, 1] * jnp.exp(parts[:, 0] - top), axis=0)])[None]

        stats = combine(exchange(jnp.broadcast_to(stats, (32, 2, 384)), "yl", "yh", "x", "core"))
        stats = combine(exchange(jnp.broadcast_to(stats, (8, 2, 384)), "z"))
        stats = stats.reshape(2, 2, 192)
        stats = jnp.where(core == 0, stats, stats[:, ::-1]).reshape(2, 384)

    with jax.named_scope("coefficient"):
        targets = by_core(row_ids[1])
        targets = jnp.where(core == 0, targets, targets[::-1]).reshape(384)
        onehot = (targets[:, None] == columns[None, :]).astype(jnp.float32)
        coefficient = (jnp.exp(logits - stats[0][:, None]) / stats[1][:, None] - onehot).astype(jnp.bfloat16)

    with jax.named_scope("hidden_grad"):
        partial = jnp.stack(
            [jnp.dot(coefficient, table[i], preferred_element_type=jnp.float32) for i in range(2)]
        )
        theirs = other_core(partial[:, 192:].astype(jnp.bfloat16))
        chip = (partial[:, :192] + theirs.astype(jnp.float32)).astype(jnp.bfloat16)
        plane = exchange(chip.reshape(16, 24, HALF), "yl", "yh", "x")
        plane = jnp.sum(plane.astype(jnp.float32), axis=0).astype(jnp.bfloat16).reshape(1, 8, 3, HALF)
        last = exchange(jnp.broadcast_to(plane, (2, 8, 3, HALF)).reshape(16, 3, HALF), "yl", "z")
        last = jnp.sum(last.reshape(2, 8, 3, HALF).astype(jnp.float32), axis=1)
        hidden_grad = last.transpose(1, 0, 2).reshape(3, D).astype(jnp.bfloat16)

    with jax.named_scope("table_grad"):
        inputs = by_core(row_ids[0]).reshape(384)
        placed = jnp.where(inputs[:, None] == columns[None, :], factor, jnp.zeros((), jnp.bfloat16))
        left = jnp.concatenate([coefficient, placed], axis=0)
        right = jnp.concatenate([hidden, cotangent], axis=1)
        table_grad = jnp.concatenate(
            [
                lax.dot_general(left, right[i], (((0,), (0,)), ((), ())), preferred_element_type=jnp.float32)
                for i in range(2)
            ],
            axis=1,
        ).astype(jnp.bfloat16)
    return (table_grad, hidden_grad)


def solution(mesh):
    placed = (P("section", ("dp", "vocab"), None), P(("section", "dp", "vocab"), None), P())
    return jax.shard_map(
        shards,
        mesh=mesh,
        in_specs=placed,
        out_specs=(P(("section", "dp", "vocab"), None), P(("dp", "vocab"), None)),
        check_vma=False,
    )
```

time: 2230 us -> 202 us (0.09)
  waiting for transfers between devices: 1960 us -> 64.2 us
  blocking collectives: 188 us -> 48.5 us
  starting transfers between devices: 0.08 us -> 22.7 us
    unnamed x3 -> x1, waiting for transfers between devices: 1260 us -> 0.02 us
    all_gather x1, waiting for transfers between devices: 705 us -> 43.2 us  [shards(): lax.all_gather(got[0], AXES, axis_index_groups=groups('yl', 'core', 'yh',...]
    pmax x1 -> x0, blocking collectives: 105 us -> none  [shards(): highest = lax.pmax(local_high, ('section', 'dp', 'vocab'))]
    psum x2 -> x0, blocking collectives: 82.4 us -> none  [the longest x1 73.4 us: shards(): lax.psum(jnp.sum(expvals, axis=1, keepdims=True), ('section', 'dp', 'voca...]
    all_to_all x0 -> x2, blocking collectives: none -> 48.5 us  [exchange(): lax.all_to_all(blocks, AXES, 0, 0, axis_index_groups=groups(*axes), tiled...]
    all_to_all x0 -> x4, starting transfers between devices: none -> 22.7 us  [exchange(): lax.all_to_all(blocks, AXES, 0, 0, axis_index_groups=groups(*axes), tiled...]
  transfers between devices with their start and end apart: 2 -> 7, of which waited for: 2 -> 5; matrix products, arithmetic and copies ran while one was open for 1% -> 22% of each run, Pallas kernels for 0% -> 0%
where the time goes in v1:
time: 202 us; the launch traced here: 200 us
  waiting for transfers between devices  64.2 us (32%)
  blocking collectives  48.5 us (24%)
  starting transfers between devices  22.7 us (11%)
  matrix products  18.4 us (9%)
  other arithmetic  16.3 us (8%)
  local copies, waits for them, and re-layouts  15.6 us (8%)
  between operations  14.3 us (7%)
    all_to_all x2, blocking collectives, exchange(): lax.all_to_all(blocks, AXES, 0, 0, axis_index_groups=groups(*axes), tiled...  48.5 us
    all_gather x1, waiting for transfers between devices, shards(): lax.all_gather(got[0], AXES, axis_index_groups=groups('yl', 'core', 'yh',...  43.2 us
    all_to_all x4, starting transfers between devices, exchange(): lax.all_to_all(blocks, AXES, 0, 0, axis_index_groups=groups(*axes), tiled...  22.7 us
    all_to_all x4, waiting for transfers between devices, exchange(): lax.all_to_all(blocks, AXES, 0, 0, axis_index_groups=groups(*axes), tiled...  20.3 us
    dot_general x2, matrix products, shards(): lax.dot_general(left, right[i], (((0,), (0,)), ((), ())), preferred_eleme...  6.87 us
    dot_general x2, matrix products, shards(): lax.dot_general(hidden[i], table[i], (((1,), (1,)), ((), ())), preferred_...  5.9 us
    dot_general x2, matrix products, shards(): jnp.dot(coefficient, table[i], preferred_element_type=jnp.float32)  5.66 us
    concatenate x1, other arithmetic, shards(): jnp.concatenate([lax.dot_general(left, right[i], (((0,), (0,)), ((), ()))...  4.88 us
  transfers between devices with their start and end apart: 7, of which 5 were waited for; matrix products, arithmetic and copies ran while one was open for 22% of the time, Pallas kernels for 0%

profile of v1, /device:TPU:8, one launch (start us, length us, event | category | flops | bytes accessed | tf_op | source)
XLA Modules:
  0.0 200.0 jit_solution(8127401710833989698)
XLA Ops:
  7.2 0.8 squeeze.43
  8.2 19.7 %all_to_all.30 = bf16[16,3,2304]{2,1,0:T(4,128)(2,1)S(1)} all-to-all(bf16[16,3,2304]{2,1,0:T(4,128)(2,1)S(1)} %bitcast.69), channel_id=1, replica_groups={{0,4,8,12,16,20,24,28,128,132,136,140,144,148,152,156},{1,5,9,13,17,21,..., dimensions={0} | all-to-all | bytes 442368 | tf_op jit(solution)/shard_map/rows_lz/all_to_all | solution.py:29
  27.8 0.8 fusion.33
  28.6 0.1 squeeze.44
  28.7 0.1 broadcast_in_dim.21
  28.8 28.8 %all_to_all.31 = bf16[16,24,2304]{2,1,0:T(8,128)(2,1)S(1)} all-to-all(bf16[16,24,2304]{2,1,0:T(8,128)(2,1)S(1)} %broadcast_in_dim.21), channel_id=1, replica_groups={{0,1,2,3,64,65,66,67,128,129,130,131,192,193,194,195},{4,5,6,7,68,69,70..., dimensions={0} | all-to-all | bytes 3538944 | tf_op jit(solution)/shard_map/hidden_xy/all_to_all | solution.py:29
  57.7 1.2 squeeze.51
  58.8 1.5 copy.24
  60.3 1.0 reshape.67
  61.3 1.6 squeeze.53
  63.0 1.2 copy-done.5
  64.3 2.8 %fusion.5 = f32[384,512]{1,0:T(8,128)S(1)} fusion(bf16[512,4608]{1,0:T(8,128)(2,1)} %param.4, bf16[2,192,2304]{2,1,0:T(8,128)(2,1)S(1)} %collective-permute-done, bf16[2,192,2304]{2,1,0:T(8,128)(2,1)S(1)} %bitcast.64), kind=kOutput, calls=%fused_computation.18 | convolution fusion | flops 909508608 | bytes 6684672 | tf_op jit(solution)/shard_map/logits/dot_general | solution.py:64
  67.1 3.1 %fusion.36 = (f32[384]{0:T(512)S(1)}, f32[384,512]{1,0:T(8,128)S(1)}) fusion(f32[384,512]{1,0:T(8,128)S(1)} %fusion.5, bf16[512,4608]{1,0:T(8,128)(2,1)} %param.4, bf16[2,192,2304]{2,1,0:T(8,128)(2,1)S(1)} %bitcast.65, bf16[2,192,2304]{2,1,0:T(8,128)(2,1)} %copy-done.5), kind=kOutput, calls=%fused_computation.64 | convolution fusion | flops 909901440 | bytes 7472640 | tf_op jit(solution)/shard_map/logits/dot_general | solution.py:64
  70.2 0.1 stack.36
  70.3 0.3 exponential_reduce_fusion
  70.6 0.1 stack.37
  70.8 0.1 broadcast_in_dim.22
  70.9 0.7 broadcast_in_dim.46
  71.5 5.3 %all-to-all-start.2 = ((f32[32,2,384]{2,1,0:T(2,128)}), f32[32,2,384]{2,1,0:T(2,128)S(1)}, u32[]{:S(2)}, u32[]{:S(2)}) async-start(f32[32,2,384]{2,1,0:T(2,128)} %broadcast_in_dim.46), calls=%async_computation.2 | async-start | bytes 196608 | tf_op jit(solution)/shard_map/stats/all_to_all | solution.py:29
  76.9 6.5 %all-to-all-done.2 = f32[32,2,384]{2,1,0:T(2,128)S(1)} async-done(((f32[32,2,384]{2,1,0:T(2,128)}), f32[32,2,384]{2,1,0:T(2,128)S(1)}, u32[]{:S(2)}, u32[]{:S(2)}) %all-to-all-start.2) | async-done | bytes 98336 | tf_op jit(solution)/shard_map/stats/all_to_all | solution.py:29
  83.4 0.1 slice_reduce_fusion.3
  83.6 0.6 broadcast_in_dim.47
  84.2 5.3 %all-to-all-start.3 = ((f32[8,2,384]{2,1,0:T(2,128)}), f32[8,2,384]{2,1,0:T(2,128)S(1)}, u32[]{:S(2)}, u32[]{:S(2)}) async-start(f32[8,2,384]{2,1,0:T(2,128)} %broadcast_in_dim.47), calls=%async_computation.3 | async-start | bytes 49152 | tf_op jit(solution)/shard_map/stats/all_to_all | solution.py:29
  89.6 7.7 %all-to-all-done.3 = f32[8,2,384]{2,1,0:T(2,128)S(1)} async-done(((f32[8,2,384]{2,1,0:T(2,128)}), f32[8,2,384]{2,1,0:T(2,128)S(1)}, u32[]{:S(2)}, u32[]{:S(2)}) %all-to-all-start.3) | async-done | bytes 24608 | tf_op jit(solution)/shard_map/stats/all_to_all | solution.py:29
  97.3 0.1 stack.42
  97.5 0.1 stack.43
  97.8 0.3 subtract_convert_fusion
  98.1 2.9 %convolution_bitcast_fusion = f32[1,384,2304]{2,1,0:T(8,128)S(1)} fusion(bf16[384,512]{1,0:T(8,128)(2,1)S(1)} %subtract_convert_fusion, bf16[512,4608]{1,0:T(8,128)(2,1)} %param.4), kind=kOutput, calls=%fused_computation.4 | convolution fusion | flops 905969664 | bytes 6291456 | tf_op jit(solution)/shard_map/hidden_grad/dot_general | solution.py:90
  101.0 2.8 %convolution_bitcast_fusion.1 = f32[1,384,2304]{2,1,0:T(8,128)S(1)} fusion(bf16[384,512]{1,0:T(8,128)(2,1)S(1)} %subtract_convert_fusion, bf16[512,4608]{1,0:T(8,128)(2,1)} %param.4), kind=kOutput, calls=%fused_computation.5 | convolution fusion | flops 905969664 | bytes 6291456 | tf_op jit(solution)/shard_map/hidden_grad/dot_general | solution.py:90
  103.8 1.7 fusion.3
  105.5 0.7 copy-done
  106.2 0.9 squeeze.52
  107.1 1.5 copy.25
  108.5 1.0 eq.40
  109.6 0.6 collective-permute-done.1
  110.2 3.6 %fusion.2 = bf16[2,192,2304]{2,1,0:T(8,128)(2,1)} fusion(f32[1,384,2304]{2,1,0:T(8,128)} %copy-done, f32[1,384,2304]{2,1,0:T(8,128)S(1)} %convolution_bitcast_fusion, bf16[2,192,2304]{2,1,0:T(8,128)(2,1)} %collective-permute-done.1), kind=kLoop, calls=%fused_computation.10 | loop fusion | flops 3538944 | bytes 10616832 | tf_op jit(solution)/shard_map/hidden_grad/convert_element_type | solution.py:93
  113.9 5.3 %all-to-all-start.4 = ((bf16[16,24,2304]{2,1,0:T(8,128)(2,1)}), bf16[16,24,2304]{2,1,0:T(8,128)(2,1)S(1)}, u32[]{:S(2)}, u32[]{:S(2)}) async-start(bf16[16,24,2304]{2,1,0:T(8,128)(2,1)} %bitcast.67), calls=%async_computation.4 | async-start | bytes 3538944 | tf_op jit(solution)/shard_map/hidden_grad/all_to_all | solution.py:29
  119.1 0.9 compare_select_fusion
  120.0 43.2 %all-gather.2.cloned.1.call-done = bf16[768,2304]{1,0:T(8,128)(2,1)} async-done(((bf16[24,2304]{1,0:T(8,128)(2,1)}), bf16[768,2304]{1,0:T(8,128)(2,1)}) %all-gather.2.cloned.1.call-update) | async-done | bytes 3538960 | tf_op jit(solution)/shard_map/cotangent/all_gather | solution.py:54
  163.3 3.4 %pad_maximum_fusion = bf16[2,768,2304]{2,1,0:T(8,128)(2,1)S(1)} fusion(bf16[2,384,2304]{2,1,0:T(8,128)(2,1)} %bitcast.68, bf16[2,192,2304]{2,1,0:T(8,128)(2,1)} %copy-done.5, bf16[2,192,2304]{2,1,0:T(8,128)(2,1)S(1)} %bitcast.66), kind=kLoop, calls=%fused_computation | loop fusion | flops 21233664 | bytes 14155776 | tf_op jit(solution)/shard_map/table_grad/concatenate | solution.py:104
  166.7 3.4 %convolution_convert_fusion.1 = bf16[512,2304]{1,0:T(8,128)(2,1)} fusion(bf16[2,768,2304]{2,1,0:T(8,128)(2,1)S(1)} %pad_maximum_fusion, bf16[384,512]{1,0:T(8,128)(2,1)S(1)} %copy-done.6, bf16[384,512]{1,0:T(8,128)(2,1)S(1)} %copy-done.4), kind=kOutput, calls=%fused_computation.7 | convolution fusion | flops 1814691840 | bytes 6684672 | tf_op jit(solution)/shard_map/table_grad/dot_general | solution.py:107
  170.1 3.4 %convolution_convert_fusion = bf16[512,2304]{1,0:T(8,128)(2,1)} fusion(bf16[2,768,2304]{2,1,0:T(8,128)(2,1)S(1)} %pad_maximum_fusion, bf16[384,512]{1,0:T(8,128)(2,1)S(1)} %copy-done.6, bf16[384,512]{1,0:T(8,128)(2,1)S(1)} %copy-done.4), kind=kOutput, calls=%fused_computation.6 | convolution fusion | flops 1814691840 | bytes 6684672 | tf_op jit(solution)/shard_map/table_grad/dot_general | solution.py:107
  173.6 0.2 reduce_sum.51
  173.9 0.8 broadcast_in_dim.51
  174.7 6.8 %all-to-all-start.5 = ((bf16[16,3,2304]{2,1,0:T(4,128)(2,1)}), bf16[16,3,2304]{2,1,0:T(4,128)(2,1)S(1)}, u32[]{:S(2)}, u32[]{:S(2)}) async-start(bf16[16,3,2304]{2,1,0:T(4,128)(2,1)} %bitcast.15), calls=%async_computation.5 | async-start | bytes 589824 | tf_op jit(solution)/shard_map/hidden_grad/all_to_all | solution.py:29
  181.5 4.9 %pad_maximum_fusion.1 = bf16[512,4608]{1,0:T(8,128)(2,1)} fusion(bf16[512,2304]{1,0:T(8,128)(2,1)} %convolution_convert_fusion, bf16[512,2304]{1,0:T(8,128)(2,1)} %convolution_convert_fusion.1), kind=kLoop, calls=%fused_computation.3 | loop fusion | flops 9437184 | bytes 9437184 | tf_op jit(solution)/shard_map/table_grad/concatenate | solution.py:105
  186.3 6.1 %all-to-all-done.5 = bf16[16,3,2304]{2,1,0:T(4,128)(2,1)S(1)} async-done(((bf16[16,3,2304]{2,1,0:T(4,128)(2,1)}), bf16[16,3,2304]{2,1,0:T(4,128)(2,1)S(1)}, u32[]{:S(2)}, u32[]{:S(2)}) %all-to-all-start.5) | async-done | bytes 221216 | tf_op jit(solution)/shard_map/hidden_grad/all_to_all | solution.py:29
  192.4 0.7 bitcast_reduce_fusion
  (45 shorter events, 0.9 us)
Async XLA Ops:
  7.2 156.1 %all-gather.2.cloned.1.call-start = ((), (), s32[]{:S(2)}) async-start(), calls=%async_computation.6 | async-start | bytes 3649536 | tf_op jit(solution)/shard_map/cotangent/all_gather | solution.py:54
  8.1 49.6 %copy-start.7 = (s32[2,384]{1,0:T(2,128)S(1)}, s32[2,384]{1,0:T(2,128)}, u32[]{:S(2)}) copy-start(s32[2,384]{1,0:T(2,128)} %param.5) | copy-start | bytes 9220
  57.6 9.4 %copy-start.1 = (bf16[16,24,2304]{2,1,0:T(8,128)(2,1)}, bf16[16,24,2304]{2,1,0:T(8,128)(2,1)S(1)}, u32[]{:S(2)}) copy-start(bf16[16,24,2304]{2,1,0:T(8,128)(2,1)S(1)} %all_to_all.31) | copy-start | bytes 5308420
  57.6 5.4 %collective-permute-start = (bf16[2,192,2304]{2,1,0:T(8,128)(2,1)S(1)}, bf16[2,192,2304]{2,1,0:T(8,128)(2,1)S(1)}, u32[]{:S(2)}, u32[]{:S(2)}) collective-permute-start(bf16[2,192,2304]{2,1,0:T(8,128)(2,1)S(1)} %bitcast.63), channel_id=1, source_target_pairs={{0,32},{32,0},{1,33},{33,1},{2,34},{34,2},{3,35},{35,3},{4,36},{36... | collective-permute-start | bytes 5308424 | tf_op jit(solution)/shard_map/hidden_core/ppermute | solution.py:34
  63.0 1.3 copy-start.5
  71.5 11.9 %all-to-all-start.2 = ((f32[32,2,384]{2,1,0:T(2,128)}), f32[32,2,384]{2,1,0:T(2,128)S(1)}, u32[]{:S(2)}, u32[]{:S(2)}) async-start(f32[32,2,384]{2,1,0:T(2,128)} %broadcast_in_dim.46), calls=%async_computation.2 | async-start | bytes 196608 | tf_op jit(solution)/shard_map/stats/all_to_all | solution.py:29
  84.2 13.1 %all-to-all-start.3 = ((f32[8,2,384]{2,1,0:T(2,128)}), f32[8,2,384]{2,1,0:T(2,128)S(1)}, u32[]{:S(2)}, u32[]{:S(2)}) async-start(f32[8,2,384]{2,1,0:T(2,128)} %broadcast_in_dim.47), calls=%async_computation.3 | async-start | bytes 49152 | tf_op jit(solution)/shard_map/stats/all_to_all | solution.py:29
  98.1 2.9 %copy-start.3 = (bf16[384,512]{1,0:T(8,128)(2,1)}, bf16[384,512]{1,0:T(8,128)(2,1)S(1)}, u32[]{:S(2)}) copy-start(bf16[384,512]{1,0:T(8,128)(2,1)S(1)} %subtract_convert_fusion) | copy-start | bytes 1179652
  103.8 2.4 %copy-start = (f32[1,384,2304]{2,1,0:T(8,128)}, f32[1,384,2304]{2,1,0:T(8,128)S(1)}, u32[]{:S(2)}) copy-start(f32[1,384,2304]{2,1,0:T(8,128)S(1)} %convolution_bitcast_fusion.1) | copy-start | bytes 10616836
  106.2 4.0 %collective-permute-start.1 = (bf16[2,192,2304]{2,1,0:T(8,128)(2,1)}, bf16[2,192,2304]{2,1,0:T(8,128)(2,1)}, u32[]{:S(2)}, u32[]{:S(2)}) collective-permute-start(bf16[2,192,2304]{2,1,0:T(8,128)(2,1)} %fusion.3), channel_id=1, source_target_pairs={{0,32},{32,0},{1,33},{33,1},{2,34},{34,2},{3,35},{35,3},{4,36},{36... | collective-permute-start | bytes 5308424 | tf_op jit(solution)/shard_map/hidden_grad/ppermute | solution.py:34
  113.8 49.4 %copy-start.2 = (bf16[16,24,2304]{2,1,0:T(8,128)(2,1)S(1)}, bf16[16,24,2304]{2,1,0:T(8,128)(2,1)}, u32[]{:S(2)}) copy-start(bf16[16,24,2304]{2,1,0:T(8,128)(2,1)} %copy-done.1) | copy-start | bytes 5308420
  113.9 59.7 %all-to-all-start.4 = ((bf16[16,24,2304]{2,1,0:T(8,128)(2,1)}), bf16[16,24,2304]{2,1,0:T(8,128)(2,1)S(1)}, u32[]{:S(2)}, u32[]{:S(2)}) async-start(bf16[16,24,2304]{2,1,0:T(8,128)(2,1)} %bitcast.67), calls=%async_computation.4 | async-start | bytes 3538944 | tf_op jit(solution)/shard_map/hidden_grad/all_to_all | solution.py:29
  163.3 3.4 %copy-start.4 = (bf16[384,512]{1,0:T(8,128)(2,1)S(1)}, bf16[384,512]{1,0:T(8,128)(2,1)}, u32[]{:S(2)}) copy-start(bf16[384,512]{1,0:T(8,128)(2,1)} %copy-done.3) | copy-start | bytes 1179652
  163.3 3.4 %copy-start.6 = (bf16[384,512]{1,0:T(8,128)(2,1)S(1)}, bf16[384,512]{1,0:T(8,128)(2,1)}, u32[]{:S(2)}) copy-start(bf16[384,512]{1,0:T(8,128)(2,1)} %compare_select_fusion) | copy-start | bytes 1179652
  174.7 17.7 %all-to-all-start.5 = ((bf16[16,3,2304]{2,1,0:T(4,128)(2,1)}), bf16[16,3,2304]{2,1,0:T(4,128)(2,1)S(1)}, u32[]{:S(2)}, u32[]{:S(2)}) async-start(bf16[16,3,2304]{2,1,0:T(4,128)(2,1)} %bitcast.15), calls=%async_computation.5 | async-start | bytes 589824 | tf_op jit(solution)/shard_map/hidden_grad/all_to_all | solution.py:29
Sparse Core Ops, SparseCore 0:
  63.1 100.0 all-gather.1

commit v2 on v1

v2 whole, which is shorter than its diff:
```python
import math

import jax
import jax.numpy as jnp
from jax import lax
from jax.experimental import pallas as pl
from jax.experimental.pallas import tpu as pltpu
from jax.sharding import PartitionSpec as P

D = 4608
HALF = D // 2
ROWS = 384
CORE_ROWS = 192
CHUNK = 768
PER_HALF = HALF // CHUNK
AXES = ("section", "dp", "vocab")
SIZES = {"yl": 2, "yh": 2, "core": 2, "z": 8, "x": 4}
FACTOR = float(jnp.bfloat16(math.sqrt(D)))


def place(device):
    vocab, dp, section = device % 32, device // 32 % 4, device // 128
    return {"yl": section, "yh": dp // 2, "core": dp % 2, "z": vocab // 4, "x": vocab % 4}


def device_at(at):
    return (at["yl"] * 4 + at["yh"] * 2 + at["core"]) * 32 + at["z"] * 4 + at["x"]


def groups(*axes):
    found = {}
    for device in range(256):
        at = place(device)
        key = tuple(at[a] for a in SIZES if a not in axes)
        found.setdefault(key, []).append((tuple(at[a] for a in axes), device))
    return [[device for _, device in sorted(members)] for members in found.values()]


def exchange(blocks, *axes):
    return lax.all_to_all(blocks, AXES, 0, 0, axis_index_groups=groups(*axes), tiled=True)


def other_core(array):
    pairs = [pair for a, b in groups("core") for pair in ((a, b), (b, a))]
    return lax.ppermute(array, AXES, pairs)


def from_x(array, offset):
    pairs = []
    for device in range(256):
        at = place(device)
        pairs.append((device_at(dict(at, x=(at["x"] + offset) % 4)), device))
    return lax.ppermute(array, AXES, pairs)


def from_y(array, offset):
    pairs = []
    for device in range(256):
        at = place(device)
        y = (at["yh"] * 2 + at["yl"] + offset) % 4
        pairs.append((device_at(dict(at, yh=y // 2, yl=y % 2)), device))
    return lax.ppermute(array, AXES, pairs)


def natural_row(yh, core, z, x, j):
    return ((yh * 2 + core) * 32 + z * 4 + x) * 3 + j


def params(**more):
    return pltpu.CompilerParams(vmem_limit_bytes=14 * 2**20, **more)


def pick(condition, a, b):
    return jnp.where(condition, a, b)


def hold_kernel(source, held, arrived):
    copy = pltpu.make_async_copy(source, held, arrived)
    copy.start()
    copy.wait()


def hold(array):
    return pl.pallas_call(
        hold_kernel,
        in_specs=[pl.BlockSpec(memory_space=pltpu.MemorySpace.HBM)],
        out_specs=pl.BlockSpec(memory_space=pltpu.VMEM),
        out_shape=pltpu.VMEM(array.shape, array.dtype),
        scratch_shapes=[pltpu.SemaphoreType.DMA],
        compiler_params=params(),
        name="hold",
    )(array)


def ids_onehot(ids, first, order, value):
    column = first + lax.broadcasted_iota(jnp.int32, (512, ROWS), 0)
    plain = jnp.where(column == ids, jnp.float32(value), jnp.float32(0)).astype(jnp.bfloat16)
    natural = lax.broadcasted_iota(jnp.int32, (ROWS, order.shape[1]), 0)
    move = jnp.where(natural == order, jnp.float32(1), jnp.float32(0)).astype(jnp.bfloat16)
    return jnp.dot(plain, move, preferred_element_type=jnp.float32)


SCALARS = pl.BlockSpec(memory_space=pltpu.SMEM)
BLOCK = pl.BlockSpec(memory_space=pltpu.VMEM)


def stats_kernel(at, mine, other, out):
    rows = []
    for logits in (mine, other):
        turned = logits[...].T
        high = jnp.max(turned, axis=0, keepdims=True)
        rows.append((high, jnp.sum(jnp.exp(turned - high), axis=0, keepdims=True)))
    first = at[0] == 0
    both = [pick(first, rows[i][k], rows[1 - i][k]) for k in range(2) for i in range(2)]
    out[...] = jnp.broadcast_to(jnp.concatenate(both, axis=0)[None], out.shape)


def merged(parts):
    high = jnp.max(parts[:, 0:2, :], axis=0)
    total = jnp.sum(parts[:, 2:4, :] * jnp.exp(parts[:, 0:2, :] - high), axis=0)
    return high, total


def merge_kernel(parts, out):
    out[...] = jnp.broadcast_to(jnp.concatenate(merged(parts[...]), axis=0)[None], out.shape)


def coefficient_kernel(at, mine, other, parts, ids, orders, out_mine, out_other, turned_mine, turned_other):
    high, total = merged(parts[...])
    scale = 1.0 / total
    first = at[0] == 0
    for i, (logits, out, turned) in enumerate(((mine, out_mine, turned_mine), (other, out_other, turned_other))):
        top = pick(first, high[i : i + 1], high[1 - i : 2 - i])
        factor = pick(first, scale[i : i + 1], scale[1 - i : 2 - i])
        onehot = ids_onehot(ids[1:2, :], at[2], orders[i : i + 1, :], 1.0)
        values = jnp.exp(logits[...].T - top) * factor - onehot
        turned[...] = values.astype(jnp.bfloat16)
        out[...] = values.T.astype(jnp.bfloat16)


def small_call(kernel, name, outs, *args):
    return pl.pallas_call(
        kernel,
        in_specs=[SCALARS if a.ndim == 1 else BLOCK for a in args],
        out_specs=[BLOCK] * len(outs),
        out_shape=[jax.ShapeDtypeStruct(*out) for out in outs],
        compiler_params=params(),
        name=name,
    )(*args)


def table_grad_kernel(at, coef_mine, coef_other, ids, orders, mine, other, a0, a1, a2, a3, b0, b1, b2, b3, out, placed):
    part, step = pl.program_id(0), pl.program_id(1)

    @pl.when(step == 0)
    def _():
        order = jnp.where(part == 0, orders[0:1, :], orders[1:2, :])
        placed[...] = ids_onehot(ids[0:1, :], at[2], order, FACTOR).astype(jnp.bfloat16)

    even = part == 0
    cotangent = jnp.concatenate(
        [
            pick(even, a0[...], a1[...]),
            pick(even, a2[...], a3[...]),
            pick(even, b0[...], b1[...]),
            pick(even, b2[...], b3[...]),
        ],
        axis=0,
    )
    total = jnp.dot(placed[...], cotangent, preferred_element_type=jnp.float32)
    total += jnp.dot(coef_mine[...], mine[0], preferred_element_type=jnp.float32)
    total += jnp.dot(coef_other[...], other[0], preferred_element_type=jnp.float32)
    out[...] = total.astype(jnp.bfloat16)


def table_grad_call(at, coef_mine, coef_other, ids, orders, mine, other, own, far):
    whole = lambda *shape: pl.BlockSpec(shape, lambda p, k, at: (0,) * len(shape))
    side = lambda p, at: lax.bitwise_xor(at[1], p)
    block = pl.BlockSpec((1, CORE_ROWS, CHUNK), lambda p, k, at: (side(p, at), 0, k))
    early = pl.BlockSpec((96, CHUNK), lambda p, k, at: (0, k * (1 - p) + (PER_HALF - 1) * p))
    late = pl.BlockSpec((96, CHUNK), lambda p, k, at: (0, k * p))
    return pl.pallas_call(
        table_grad_kernel,
        grid_spec=pltpu.PrefetchScalarGridSpec(
            num_scalar_prefetch=1,
            grid=(2, PER_HALF),
            in_specs=[whole(512, CORE_ROWS)] * 2 + [whole(2, ROWS), whole(2, ROWS), block, block]
            + [early, late, early, late] * 2,
            out_specs=pl.BlockSpec((512, CHUNK), lambda p, k, at: (0, side(p, at) * PER_HALF + k)),
            scratch_shapes=[pltpu.VMEM((512, ROWS), jnp.bfloat16)],
        ),
        out_shape=jax.ShapeDtypeStruct((512, D), jnp.bfloat16),
        compiler_params=params(),
        cost_estimate=pl.CostEstimate(flops=4 * ROWS * 512 * D, bytes_accessed=13_000_000, transcendentals=0),
        name="table_grad",
    )(at, coef_mine, coef_other, ids, orders, mine, other, *own, *far)


def shards(stacked_rows, tied_table, row_ids):
    section, dp, vocab = (lax.axis_index(a) for a in AXES)
    core, yh, x = dp % 2, dp // 2, vocab % 4
    first_column = ((section * 4 + dp) * 32 + vocab) * tied_table.shape[0]
    at = jnp.stack([core, section, first_column]).astype(jnp.int32)

    with jax.named_scope("orders"):
        i = lax.iota(jnp.int32, ROWS)
        c, yy, xx, z, j = i // 192, i // 96 % 2, i // 24 % 4, i // 3 % 8, i % 3
        moved_x = (x + xx) % 4
        y_of = lambda part: (yh * 2 + section + 2 * yy + part) % 4
        head_orders = natural_row(yy, lax.bitwise_xor(core, c), z, xx, j).reshape(2, CORE_ROWS)
        input_orders = jnp.stack(
            [natural_row(y_of(part) // 2, lax.bitwise_xor(core, c), z, moved_x, j) for part in range(2)]
        )

    with jax.named_scope("rows_lz"):
        own = stacked_rows[0].reshape(3, 2, HALF).transpose(1, 0, 2)
        blocks = jnp.broadcast_to(own[:, None], (2, 8, 3, HALF)).reshape(16, 3, HALF)
        got = exchange(blocks, "yl", "z").reshape(2, 24, HALF)
    with jax.named_scope("cotangent_x"):
        line = [got[0]] + [from_x(got[0], offset) for offset in (1, 2, 3)]
    with jax.named_scope("hidden_xy"):
        mine = exchange(jnp.broadcast_to(got[1], (16, 24, HALF)), "yl", "yh", "x").reshape(2, CORE_ROWS, HALF)
        line = jnp.concatenate(line, axis=0)
        mine, line, table, at, head_orders, input_orders = lax.optimization_barrier(
            (mine, line, tied_table, at, head_orders, input_orders)
        )
        table = hold(table)
    with jax.named_scope("hidden_core"):
        other = other_core(mine)
    with jax.named_scope("cotangent_y"):
        own = [line] + [from_y(line, offset) for offset in (1, 2, 3)]
    with jax.named_scope("logits"):
        logits = [
            sum(
                lax.dot_general(
                    rows[i], half, (((1,), (1,)), ((), ())), preferred_element_type=jnp.float32
                )
                for i, half in enumerate((table[:, :HALF], table[:, HALF:]))
            )
            for rows in (mine, other)
        ]
    with jax.named_scope("stats"):
        (stats,) = small_call(stats_kernel, "stats", [((32, 4, CORE_ROWS), jnp.float32)], at, *logits)
        stats = exchange(stats, "yl", "yh", "x", "core")
        (stats,) = small_call(merge_kernel, "merge", [((8, 4, CORE_ROWS), jnp.float32)], stats)
        stats = exchange(stats, "z")
    with jax.named_scope("coefficient"):
        *coefficient, turned_mine, turned_other = small_call(
            coefficient_kernel,
            "coefficient",
            [((CORE_ROWS, 512), jnp.bfloat16)] * 2 + [((512, CORE_ROWS), jnp.bfloat16)] * 2,
            at,
            *logits,
            stats,
            row_ids,
            head_orders,
        )
        *coefficient, own = lax.optimization_barrier((*coefficient, own))
    with jax.named_scope("hidden_grad"):
        halves = (table[:, :HALF], table[:, HALF:])
        product = lambda rows, half: jnp.dot(rows, half, preferred_element_type=jnp.float32)
        theirs = [other_core(product(coefficient[1], half).astype(jnp.bfloat16)) for half in halves]
        ours = lax.optimization_barrier([product(coefficient[0], half) for half in halves])
        chip = jnp.stack([(a + b).astype(jnp.bfloat16) for a, b in zip(ours, theirs)])
        chip, turned_mine, turned_other = lax.optimization_barrier((chip, turned_mine, turned_other))
    with jax.named_scope("table_grad"):
        far = [other_core(piece) for piece in own]
        table_grad = table_grad_call(at, turned_mine, turned_other, row_ids, input_orders, mine, other, own, far)
    with jax.named_scope("hidden_grad"):
        plane = exchange(chip.reshape(16, 24, HALF), "yl", "yh", "x")
        plane, table_grad = lax.optimization_barrier((plane, table_grad))
        plane = jnp.sum(plane.astype(jnp.float32), axis=0).astype(jnp.bfloat16).reshape(1, 8, 3, HALF)
        last = exchange(jnp.broadcast_to(plane, (2, 8, 3, HALF)).reshape(16, 3, HALF), "yl", "z")
        last = jnp.sum(last.reshape(2, 8, 3, HALF).astype(jnp.float32), axis=1)
        hidden_grad = last.transpose(1, 0, 2).reshape(3, D).astype(jnp.bfloat16)
    return (table_grad, hidden_grad)


def solution(mesh):
    placed = (P("section", ("dp", "vocab"), None), P(("section", "dp", "vocab"), None), P())
    return jax.shard_map(
        shards,
        mesh=mesh,
        in_specs=placed,
        out_specs=(P(("section", "dp", "vocab"), None), P(("dp", "vocab"), None)),
        check_vma=False,
    )
```

time: 202 us -> 156 us (0.77)
  waiting for transfers between devices: 64.2 us -> 35.6 us
  between operations: 14.3 us -> 0.86 us
  matrix products: 18.4 us -> 6.2 us
  other arithmetic: 16.3 us -> 4.41 us
  blocking collectives: 48.5 us -> 60.2 us
  Pallas kernels: 0 us -> 11.6 us
  local copies, waits for them, and re-layouts: 15.6 us -> 10.1 us
  starting transfers between devices: 22.7 us -> 25.8 us
    all_gather x1 -> x0, waiting for transfers between devices: 43.2 us -> none  [shards(): lax.all_gather(got[0], AXES, axis_index_groups=groups('yl', 'core', 'yh',...]
    ppermute x0 -> x6, waiting for transfers between devices: none -> 20.1 us  [the longest x3 20.1 us: from_x(): return lax.ppermute(array, AXES, pairs)]
    dot_general x6 -> x8, matrix products: 18.4 us -> 6.2 us  [the longest x4 3.65 us: shards(): lax.dot_general(rows[i], half, (((1,), (1,)), ((), ())), preferred_elemen...]
    all_to_all x2 -> x4, blocking collectives: 48.5 us -> 60.2 us  [exchange(): lax.all_to_all(blocks, AXES, 0, 0, axis_index_groups=groups(*axes), tiled...]
    pallas_call x0 -> x5, Pallas kernels: none -> 11.6 us  [the longest x1 9.09 us: table_grad_call(): pl.pallas_call(table_grad_kernel, grid_spec=pltpu.PrefetchScalarGridSpec(...]
    ppermute x0 -> x6, starting transfers between devices: none -> 9.24 us  [the longest x3 4.78 us: from_y(): return lax.ppermute(array, AXES, pairs)]
    all_to_all x4 -> x2, waiting for transfers between devices: 20.3 us -> 12 us  [exchange(): lax.all_to_all(blocks, AXES, 0, 0, axis_index_groups=groups(*axes), tiled...]
    concatenate x2 -> x1, other arithmetic: 8.3 us -> 0.03 us  [shards(): line = jnp.concatenate(line, axis=0)]
  transfers between devices with their start and end apart: 7 -> 15, of which waited for: 5 -> 9; matrix products, arithmetic and copies ran while one was open for 22% -> 4% of each run, Pallas kernels for 0% -> 7%
where the time goes in v2:
time: 156 us; the launch traced here: 155 us
  blocking collectives  60.2 us (39%)
  waiting for transfers between devices  35.6 us (23%)
  starting transfers between devices  25.8 us (17%)
  Pallas kernels  11.6 us (7%)
  local copies, waits for them, and re-layouts  10.1 us (6%)
  matrix products  6.2 us (4%)
  other arithmetic  4.41 us (3%)
    all_to_all x4, blocking collectives, exchange(): lax.all_to_all(blocks, AXES, 0, 0, axis_index_groups=groups(*axes), tiled...  60.2 us
    ppermute x3, waiting for transfers between devices, from_x(): return lax.ppermute(array, AXES, pairs)  20.1 us
    all_to_all x2, starting transfers between devices, exchange(): lax.all_to_all(blocks, AXES, 0, 0, axis_index_groups=groups(*axes), tiled...  14.6 us
    all_to_all x2, waiting for transfers between devices, exchange(): lax.all_to_all(blocks, AXES, 0, 0, axis_index_groups=groups(*axes), tiled...  12 us
    pallas_call x1, Pallas kernels, table_grad_call(): pl.pallas_call(table_grad_kernel, grid_spec=pltpu.PrefetchScalarGridSpec(...  9.09 us
    unnamed x16, local copies, waits for them, and re-layouts  7.42 us
    ppermute x3, starting transfers between devices, from_y(): return lax.ppermute(array, AXES, pairs)  4.78 us
    ppermute x3, starting transfers between devices, from_x(): return lax.ppermute(array, AXES, pairs)  4.47 us
  transfers between devices with their start and end apart: 15, of which 9 were waited for; matrix products, arithmetic and copies ran while one was open for 4% of the time, Pallas kernels for 7%

profile of v2, /device:TPU:8, one launch (start us, length us, event | category | flops | bytes accessed | tf_op | source)
XLA Modules:
  0.0 154.8 jit_solution(8619049397703073674)
XLA Ops:
  0.6 0.8 squeeze.24
  1.6 19.7 %all_to_all.30 = bf16[16,3,2304]{2,1,0:T(4,128)(2,1)S(1)} all-to-all(bf16[16,3,2304]{2,1,0:T(4,128)(2,1)S(1)} %bitcast.38), channel_id=1, replica_groups={{0,4,8,12,16,20,24,28,128,132,136,140,144,148,152,156},{1,5,9,13,17,21,..., dimensions={0} | all-to-all | bytes 442368 | tf_op jit(solution)/shard_map/rows_lz/all_to_all | solution.py:40
  21.4 1.3 broadcast_in_dim.17
  22.7 7.5 %all-to-all-start.1 = ((bf16[16,24,2304]{2,1,0:T(8,128)(2,1)}), bf16[16,24,2304]{2,1,0:T(8,128)(2,1)S(1)}, u32[]{:S(2)}, u32[]{:S(2)}) async-start(bf16[16,24,2304]{2,1,0:T(8,128)(2,1)} %broadcast_in_dim.17), calls=%async_computation.1 | async-start | bytes 3538944 | tf_op jit(solution)/shard_map/hidden_xy/all_to_all | solution.py:40
  30.5 2.8 %collective-permute-start = (bf16[24,2304]{1,0:T(8,128)(2,1)S(1)}, bf16[24,2304]{1,0:T(8,128)(2,1)S(1)}, u32[]{:S(2)}, u32[]{:S(2)}) collective-permute-start(bf16[24,2304]{1,0:T(8,128)(2,1)S(1)} %squeeze.26), channel_id=1, source_target_pairs={{1,0},{2,1},{3,2},{0,3},{5,4},{6,5},{7,6},{4,7},{9,8},{10,9},{11,1... | collective-permute-start | bytes 331784 | tf_op jit(solution)/shard_map/cotangent_x/ppermute | solution.py:53
  33.3 0.9 collective-permute-start.1
  34.1 0.9 collective-permute-start.2
  35.1 17.8 %collective-permute-done = bf16[24,2304]{1,0:T(8,128)(2,1)S(1)} collective-permute-done((bf16[24,2304]{1,0:T(8,128)(2,1)S(1)}, bf16[24,2304]{1,0:T(8,128)(2,1)S(1)}, u32[]{:S(2)}, u32[]{:S(2)}) %collective-permute-start) | collective-permute-done | bytes 110624 | tf_op jit(solution)/shard_map/cotangent_x/ppermute | solution.py:53
  52.8 1.6 %collective-permute-done.1 = bf16[24,2304]{1,0:T(8,128)(2,1)S(1)} collective-permute-done((bf16[24,2304]{1,0:T(8,128)(2,1)S(1)}, bf16[24,2304]{1,0:T(8,128)(2,1)S(1)}, u32[]{:S(2)}, u32[]{:S(2)}) %collective-permute-start.1) | collective-permute-done | bytes 110624 | tf_op jit(solution)/shard_map/cotangent_x/ppermute | solution.py:53
  54.4 0.7 collective-permute-done.2
  55.3 0.6 collective-permute-start.4
  55.9 2.4 %collective-permute-start.5 = (bf16[96,2304]{1,0:T(8,128)(2,1)S(1)}, bf16[96,2304]{1,0:T(8,128)(2,1)S(1)}, u32[]{:S(2)}, u32[]{:S(2)}) collective-permute-start(bf16[96,2304]{1,0:T(8,128)(2,1)S(1)} %pad_maximum_fusion.1.a0), channel_id=1, source_target_pairs={{64,0},{65,1},{66,2},{67,3},{68,4},{69,5},{70,6},{71,7},{72,8},{73... | collective-permute-start | bytes 1327112 | tf_op jit(solution)/shard_map/cotangent_y/ppermute | solution.py:62
  58.3 1.8 %collective-permute-start.6 = (bf16[96,2304]{1,0:T(8,128)(2,1)S(1)}, bf16[96,2304]{1,0:T(8,128)(2,1)S(1)}, u32[]{:S(2)}, u32[]{:S(2)}) collective-permute-start(bf16[96,2304]{1,0:T(8,128)(2,1)S(1)} %pad_maximum_fusion.1.a0), channel_id=1, source_target_pairs={{192,0},{193,1},{194,2},{195,3},{196,4},{197,5},{198,6},{199,7},{2... | collective-permute-start | bytes 1327112 | tf_op jit(solution)/shard_map/cotangent_y/ppermute | solution.py:62
  60.1 2.3 %copy-done = bf16[512,4608]{1,0:T(8,128)(2,1)S(1)} copy-done((bf16[512,4608]{1,0:T(8,128)(2,1)S(1)}, bf16[512,4608]{1,0:T(8,128)(2,1)}, u32[]{:S(2)}) %copy-start) | copy-done | bytes 4718616
  62.4 0.3 hold.1
  62.7 0.9 fusion.5
  63.7 0.9 fusion.14.mine
  64.6 0.9 fusion.3
  65.5 0.3 copy-done.2
  65.8 0.9 fusion.17.other
  66.7 1.0 stats.1
  67.8 12.8 %all_to_all.31.parts = f32[32,4,192]{2,1,0:T(4,128)S(1)} all-to-all(f32[32,4,192]{2,1,0:T(4,128)S(1)} %stats.1), channel_id=1, replica_groups={{0,32,1,33,2,34,3,35,64,96,65,97,66,98,67,99,128,160,129,161,130,162,13..., dimensions={0} | all-to-all | bytes 196608 | tf_op jit(solution)/shard_map/stats/all_to_all | solution.py:40
  80.7 13.8 %all_to_all.32.parts = f32[8,4,192]{2,1,0:T(4,128)S(1)} all-to-all(f32[8,4,192]{2,1,0:T(4,128)S(1)} %merge.1), channel_id=1, replica_groups={{0,4,8,12,16,20,24,28},{1,5,9,13,17,21,25,29},{2,6,10,14,18,22,26,30},{..., dimensions={0} | all-to-all | bytes 49152 | tf_op jit(solution)/shard_map/stats/all_to_all | solution.py:40
  94.5 1.1 coefficient.1
  95.6 0.7 copy-done.4
  96.4 0.7 copy-done.6
  97.1 0.6 convolution_convert_fusion.1
  97.8 0.6 convolution_convert_fusion
  98.4 0.8 collective-permute-start.8
  99.2 0.6 fusion.1
  99.8 0.6 fusion.8
  100.7 0.8 collective-permute-done.8
  101.7 1.4 pad_maximum_fusion
  103.0 7.0 %all-to-all-start.4 = ((bf16[16,24,2304]{2,1,0:T(8,128)(2,1)}), bf16[16,24,2304]{2,1,0:T(8,128)(2,1)}, u32[]{:S(2)}, u32[]{:S(2)}) async-start(bf16[16,24,2304]{2,1,0:T(8,128)(2,1)} %bitcast.37), calls=%async_computation.4 | async-start | bytes 3538944 | tf_op jit(solution)/shard_map/hidden_grad/all_to_all | solution.py:40
  110.1 0.5 collective-permute-start.11
  110.7 0.4 collective-permute-start.9
  111.1 0.8 collective-permute-done.10.b1
  111.9 0.6 collective-permute-done.11.b2
  112.5 0.6 collective-permute-done.12.b3
  113.1 0.6 collective-permute-done.9.b0
  113.8 1.5 copy-done.3
  115.3 0.9 copy-done.5
  116.2 0.9 copy-done.7
  117.2 9.1 %table_grad.1 = bf16[512,4608]{1,0:T(8,128)(2,1)} custom-call(s32[3]{0:T(128)S(1)} %pad_add_fusion.1.at, bf16[512,192]{1,0:T(8,128)(2,1)S(1)} %copy-done.5, bf16[512,192]{1,0:T(8,128)(2,1)S(1)} %copy-done.7, s32[2,384]{1,0:T(2,128)S(1)} %copy-done.1, s32[2,384]{1,0:T(2,128)S(1)} %pad_add_fusion.orders, bf16[2,192,2304]{2,1,0:T(8,128)(2,1)S(1)} %bitcast.36, ...), custom_call_target="tpu_custom_call" | custom-call | flops 3623878656 | bytes 13000000 | tf_op jit(solution)/shard_map/table_grad/table_grad/pallas_call | solution.py:182
  126.2 12.0 %all-to-all-done.4 = bf16[16,24,2304]{2,1,0:T(8,128)(2,1)} async-done(((bf16[16,24,2304]{2,1,0:T(8,128)(2,1)}), bf16[16,24,2304]{2,1,0:T(8,128)(2,1)}, u32[]{:S(2)}, u32[]{:S(2)}) %all-to-all-start.4) | async-done | bytes 1769504 | tf_op jit(solution)/shard_map/hidden_grad/all_to_all | solution.py:40
  138.2 1.7 %reduce_sum.21 = bf16[24,2304]{1,0:T(8,128)(2,1)S(1)} reduce(bf16[16,24,2304]{2,1,0:T(8,128)(2,1)} %all-to-all-done.4, bf16[]{:T(256)} %constant.160.clone.1), dimensions={0}, to_apply=%region_0.1 | reduce | flops 829440 | bytes 1880066 | tf_op jit(solution)/shard_map/hidden_grad/reduce_sum | solution.py:272
  140.1 13.9 %all_to_all.33 = bf16[16,3,2304]{2,1,0:T(4,128)(2,1)S(1)} all-to-all(bf16[16,3,2304]{2,1,0:T(4,128)(2,1)S(1)} %bitcast.39), channel_id=1, replica_groups={{0,4,8,12,16,20,24,28,128,132,136,140,144,148,152,156},{1,5,9,13,17,21,..., dimensions={0} | all-to-all | bytes 442368 | tf_op jit(solution)/shard_map/hidden_grad/all_to_all | solution.py:40
  154.0 0.7 bitcast_reduce_fusion
  (34 shorter events, 1.5 us)
Async XLA Ops:
  22.7 32.4 %all-to-all-start.1 = ((bf16[16,24,2304]{2,1,0:T(8,128)(2,1)}), bf16[16,24,2304]{2,1,0:T(8,128)(2,1)S(1)}, u32[]{:S(2)}, u32[]{:S(2)}) async-start(bf16[16,24,2304]{2,1,0:T(8,128)(2,1)} %broadcast_in_dim.17), calls=%async_computation.1 | async-start | bytes 3538944 | tf_op jit(solution)/shard_map/hidden_xy/all_to_all | solution.py:40
  30.5 22.3 %collective-permute-start = (bf16[24,2304]{1,0:T(8,128)(2,1)S(1)}, bf16[24,2304]{1,0:T(8,128)(2,1)S(1)}, u32[]{:S(2)}, u32[]{:S(2)}) collective-permute-start(bf16[24,2304]{1,0:T(8,128)(2,1)S(1)} %squeeze.26), channel_id=1, source_target_pairs={{1,0},{2,1},{3,2},{0,3},{5,4},{6,5},{7,6},{4,7},{9,8},{10,9},{11,1... | collective-permute-start | bytes 331784 | tf_op jit(solution)/shard_map/cotangent_x/ppermute | solution.py:53
  33.3 21.1 %collective-permute-start.1 = (bf16[24,2304]{1,0:T(8,128)(2,1)S(1)}, bf16[24,2304]{1,0:T(8,128)(2,1)S(1)}, u32[]{:S(2)}, u32[]{:S(2)}) collective-permute-start(bf16[24,2304]{1,0:T(8,128)(2,1)S(1)} %squeeze.26), channel_id=1, source_target_pairs={{2,0},{3,1},{0,2},{1,3},{6,4},{7,5},{4,6},{5,7},{10,8},{11,9},{8,1... | collective-permute-start | bytes 331784 | tf_op jit(solution)/shard_map/cotangent_x/ppermute | solution.py:53
  34.1 21.0 %collective-permute-start.2 = (bf16[24,2304]{1,0:T(8,128)(2,1)S(1)}, bf16[24,2304]{1,0:T(8,128)(2,1)S(1)}, u32[]{:S(2)}, u32[]{:S(2)}) collective-permute-start(bf16[24,2304]{1,0:T(8,128)(2,1)S(1)} %squeeze.26), channel_id=1, source_target_pairs={{3,0},{0,1},{1,2},{2,3},{7,4},{4,5},{5,6},{6,7},{11,8},{8,9},{9,10... | collective-permute-start | bytes 331784 | tf_op jit(solution)/shard_map/cotangent_x/ppermute | solution.py:53
  55.2 9.4 %collective-permute-start.3 = (bf16[2,192,2304]{2,1,0:T(8,128)(2,1)S(1)}, bf16[2,192,2304]{2,1,0:T(8,128)(2,1)S(1)}, u32[]{:S(2)}, u32[]{:S(2)}) collective-permute-start(bf16[2,192,2304]{2,1,0:T(8,128)(2,1)S(1)} %bitcast.33), channel_id=1, source_target_pairs={{0,32},{32,0},{1,33},{33,1},{2,34},{34,2},{3,35},{35,3},{4,36},{36... | collective-permute-start | bytes 5308424 | tf_op jit(solution)/shard_map/hidden_core/ppermute | solution.py:45
  55.3 41.8 %collective-permute-start.4 = (bf16[96,2304]{1,0:T(8,128)(2,1)S(1)}, bf16[96,2304]{1,0:T(8,128)(2,1)S(1)}, u32[]{:S(2)}, u32[]{:S(2)}) collective-permute-start(bf16[96,2304]{1,0:T(8,128)(2,1)S(1)} %pad_maximum_fusion.1.a0), channel_id=1, source_target_pairs={{128,0},{129,1},{130,2},{131,3},{132,4},{133,5},{134,6},{135,7},{1... | collective-permute-start | bytes 1327112 | tf_op jit(solution)/shard_map/cotangent_y/ppermute | solution.py:62
  55.9 41.1 %collective-permute-start.5 = (bf16[96,2304]{1,0:T(8,128)(2,1)S(1)}, bf16[96,2304]{1,0:T(8,128)(2,1)S(1)}, u32[]{:S(2)}, u32[]{:S(2)}) collective-permute-start(bf16[96,2304]{1,0:T(8,128)(2,1)S(1)} %pad_maximum_fusion.1.a0), channel_id=1, source_target_pairs={{64,0},{65,1},{66,2},{67,3},{68,4},{69,5},{70,6},{71,7},{72,8},{73... | collective-permute-start | bytes 1327112 | tf_op jit(solution)/shard_map/cotangent_y/ppermute | solution.py:62
  58.3 38.8 %collective-permute-start.6 = (bf16[96,2304]{1,0:T(8,128)(2,1)S(1)}, bf16[96,2304]{1,0:T(8,128)(2,1)S(1)}, u32[]{:S(2)}, u32[]{:S(2)}) collective-permute-start(bf16[96,2304]{1,0:T(8,128)(2,1)S(1)} %pad_maximum_fusion.1.a0), channel_id=1, source_target_pairs={{192,0},{193,1},{194,2},{195,3},{196,4},{197,5},{198,6},{199,7},{2... | collective-permute-start | bytes 1327112 | tf_op jit(solution)/shard_map/cotangent_y/ppermute | solution.py:62
  60.1 2.3 %copy-start = (bf16[512,4608]{1,0:T(8,128)(2,1)S(1)}, bf16[512,4608]{1,0:T(8,128)(2,1)}, u32[]{:S(2)}) copy-start(bf16[512,4608]{1,0:T(8,128)(2,1)} %source) | copy-start | bytes 14155780
  64.6 1.2 copy-start.2
  65.8 28.7 %copy-start.1 = (s32[2,384]{1,0:T(2,128)S(1)}, s32[2,384]{1,0:T(2,128)}, u32[]{:S(2)}) copy-start(s32[2,384]{1,0:T(2,128)} %ids.3) | copy-start | bytes 9220
  95.6 0.7 copy-start.4
  96.4 0.7 copy-start.6
  97.7 2.8 %collective-permute-start.7 = (bf16[192,2304]{1,0:T(8,128)(2,1)S(1)}, bf16[192,2304]{1,0:T(8,128)(2,1)S(1)}, u32[]{:S(2)}, u32[]{:S(2)}) collective-permute-start(bf16[192,2304]{1,0:T(8,128)(2,1)S(1)} %convolution_convert_fusion.1), channel_id=1, source_target_pairs={{0,32},{32,0},{1,33},{33,1},{2,34},{34,2},{3,35},{35,3},{4,36},{36... | collective-permute-start | bytes 2654216 | tf_op jit(solution)/shard_map/hidden_grad/ppermute | solution.py:45
  98.4 3.0 %collective-permute-start.8 = (bf16[192,2304]{1,0:T(8,128)(2,1)S(1)}, bf16[192,2304]{1,0:T(8,128)(2,1)S(1)}, u32[]{:S(2)}, u32[]{:S(2)}) collective-permute-start(bf16[192,2304]{1,0:T(8,128)(2,1)S(1)} %convolution_convert_fusion), channel_id=1, source_target_pairs={{0,32},{32,0},{1,33},{33,1},{2,34},{34,2},{3,35},{35,3},{4,36},{36... | collective-permute-start | bytes 2654216 | tf_op jit(solution)/shard_map/hidden_grad/ppermute | solution.py:45
  103.0 35.2 %all-to-all-start.4 = ((bf16[16,24,2304]{2,1,0:T(8,128)(2,1)}), bf16[16,24,2304]{2,1,0:T(8,128)(2,1)}, u32[]{:S(2)}, u32[]{:S(2)}) async-start(bf16[16,24,2304]{2,1,0:T(8,128)(2,1)} %bitcast.37), calls=%async_computation.4 | async-start | bytes 3538944 | tf_op jit(solution)/shard_map/hidden_grad/all_to_all | solution.py:40
  110.1 1.8 %collective-permute-start.10 = (bf16[96,2304]{1,0:T(8,128)(2,1)S(1)}, bf16[96,2304]{1,0:T(8,128)(2,1)S(1)}, u32[]{:S(2)}, u32[]{:S(2)}) collective-permute-start(bf16[96,2304]{1,0:T(8,128)(2,1)S(1)} %collective-permute-done.4.a1), channel_id=1, source_target_pairs={{0,32},{32,0},{1,33},{33,1},{2,34},{34,2},{3,35},{35,3},{4,36},{36... | collective-permute-start | bytes 1327112 | tf_op jit(solution)/shard_map/table_grad/ppermute | solution.py:45
  110.1 2.4 %collective-permute-start.11 = (bf16[96,2304]{1,0:T(8,128)(2,1)S(1)}, bf16[96,2304]{1,0:T(8,128)(2,1)S(1)}, u32[]{:S(2)}, u32[]{:S(2)}) collective-permute-start(bf16[96,2304]{1,0:T(8,128)(2,1)S(1)} %collective-permute-done.5.a2), channel_id=1, source_target_pairs={{0,32},{32,0},{1,33},{33,1},{2,34},{34,2},{3,35},{35,3},{4,36},{36... | collective-permute-start | bytes 1327112 | tf_op jit(solution)/shard_map/table_grad/ppermute | solution.py:45
  110.6 2.5 %collective-permute-start.12 = (bf16[96,2304]{1,0:T(8,128)(2,1)S(1)}, bf16[96,2304]{1,0:T(8,128)(2,1)S(1)}, u32[]{:S(2)}, u32[]{:S(2)}) collective-permute-start(bf16[96,2304]{1,0:T(8,128)(2,1)S(1)} %collective-permute-done.6.a3), channel_id=1, source_target_pairs={{0,32},{32,0},{1,33},{33,1},{2,34},{34,2},{3,35},{35,3},{4,36},{36... | collective-permute-start | bytes 1327112 | tf_op jit(solution)/shard_map/table_grad/ppermute | solution.py:45
  110.7 3.1 %collective-permute-start.9 = (bf16[96,2304]{1,0:T(8,128)(2,1)S(1)}, bf16[96,2304]{1,0:T(8,128)(2,1)S(1)}, u32[]{:S(2)}, u32[]{:S(2)}) collective-permute-start(bf16[96,2304]{1,0:T(8,128)(2,1)S(1)} %pad_maximum_fusion.1.a0), channel_id=1, source_target_pairs={{0,32},{32,0},{1,33},{33,1},{2,34},{34,2},{3,35},{35,3},{4,36},{36... | collective-permute-start | bytes 1327112 | tf_op jit(solution)/shard_map/table_grad/ppermute | solution.py:45
  113.8 1.5 copy-start.3
  115.3 0.9 copy-start.5
  116.2 0.9 copy-start.7

commit v3 on v2

--- a/solution.py
+++ b/solution.py
@@ -11,7 +11,7 @@
 HALF = D // 2
 ROWS = 384
 CORE_ROWS = 192
-CHUNK = 768
+CHUNK = 1152
 PER_HALF = HALF // CHUNK
 AXES = ("section", "dp", "vocab")
 SIZES = {"yl": 2, "yh": 2, "core": 2, "z": 8, "x": 4}
@@ -72,6 +72,10 @@
 
 def pick(condition, a, b):
     return jnp.where(condition, a, b)
+
+
+def in_hbm(array):
+    return pltpu.with_memory_space_constraint(array, pltpu.MemorySpace.HBM)
 
 
 def hold_kernel(source, held, arrived):
@@ -89,7 +93,7 @@
         scratch_shapes=[pltpu.SemaphoreType.DMA],
         compiler_params=params(),
         name="hold",
-    )(array)
+    )(in_hbm(array))
 
 
 def ids_onehot(ids, first, order, value):
@@ -100,6 +104,7 @@
     return jnp.dot(plain, move, preferred_element_type=jnp.float32)
 
 
+HBM = pltpu.MemorySpace.HBM
 SCALARS = pl.BlockSpec(memory_space=pltpu.SMEM)
 BLOCK = pl.BlockSpec(memory_space=pltpu.VMEM)
 
@@ -125,39 +130,56 @@
     out[...] = jnp.broadcast_to(jnp.concatenate(merged(parts[...]), axis=0)[None], out.shape)
 
 
-def coefficient_kernel(at, mine, other, parts, ids, orders, out_mine, out_other, turned_mine, turned_other):
+def coefficient_kernel(at, mine, other, parts, head_mine, head_other, out_mine, out_other, turned_mine, turned_other, kept, sent):
     high, total = merged(parts[...])
     scale = 1.0 / total
     first = at[0] == 0
-    for i, (logits, out, turned) in enumerate(((mine, out_mine, turned_mine), (other, out_other, turned_other))):
+    copies = []
+    sides = ((mine, head_mine, out_mine, turned_mine), (other, head_other, out_other, turned_other))
+    for i, (logits, onehot, out, turned) in enumerate(sides):
         top = pick(first, high[i : i + 1], high[1 - i : 2 - i])
         factor = pick(first, scale[i : i + 1], scale[1 - i : 2 - i])
-        onehot = ids_onehot(ids[1:2, :], at[2], orders[i : i + 1, :], 1.0)
-        values = jnp.exp(logits[...].T - top) * factor - onehot
-        turned[...] = values.astype(jnp.bfloat16)
+        values = jnp.exp(logits[...].T - top) * factor - onehot[...].astype(jnp.float32)
+        kept[i] = values.astype(jnp.bfloat16)
+        copy = pltpu.make_async_copy(kept.at[i], turned, sent.at[i])
+        copy.start()
+        copies.append(copy)
         out[...] = values.T.astype(jnp.bfloat16)
-
-
-def small_call(kernel, name, outs, *args):
+    for copy in copies:
+        copy.wait()
+
+
+def onehots_kernel(at, ids, head_orders, input_orders, head_mine, head_other, placed):
+    for i, out in enumerate((head_mine, head_other)):
+        out[...] = ids_onehot(ids[1:2, :], at[2], head_orders[i : i + 1, :], 1.0).astype(jnp.bfloat16)
+    for i in range(2):
+        placed[i] = ids_onehot(ids[0:1, :], at[2], input_orders[i : i + 1, :], FACTOR).astype(jnp.bfloat16)
+
+
+def plane_kernel(blocks, out):
+    total = blocks[0].astype(jnp.float32)
+    for i in range(1, blocks.shape[0]):
+        total += blocks[i].astype(jnp.float32)
+    for k in range(8):
+        rows = total[3 * k : 3 * k + 3].astype(jnp.bfloat16)
+        out[k] = rows
+        out[8 + k] = rows
+
+
+def small_call(kernel, name, outs, *args, far_outs=(), scratch=()):
     return pl.pallas_call(
         kernel,
         in_specs=[SCALARS if a.ndim == 1 else BLOCK for a in args],
-        out_specs=[BLOCK] * len(outs),
-        out_shape=[jax.ShapeDtypeStruct(*out) for out in outs],
+        out_specs=[BLOCK] * len(outs) + [pl.BlockSpec(memory_space=HBM)] * len(far_outs),
+        out_shape=[jax.ShapeDtypeStruct(*out) for out in outs] + [HBM(*out) for out in far_outs],
+        scratch_shapes=scratch,
         compiler_params=params(),
         name=name,
     )(*args)
 
 
-def table_grad_kernel(at, coef_mine, coef_other, ids, orders, mine, other, a0, a1, a2, a3, b0, b1, b2, b3, out, placed):
-    part, step = pl.program_id(0), pl.program_id(1)
-
-    @pl.when(step == 0)
-    def _():
-        order = jnp.where(part == 0, orders[0:1, :], orders[1:2, :])
-        placed[...] = ids_onehot(ids[0:1, :], at[2], order, FACTOR).astype(jnp.bfloat16)
-
-    even = part == 0
+def table_grad_kernel(at, coef_mine, coef_other, placed, mine, other, a0, a1, a2, a3, b0, b1, b2, b3, out):
+    even = pl.program_id(0) == 0
     cotangent = jnp.concatenate(
         [
             pick(even, a0[...], a1[...]),
@@ -167,13 +189,13 @@
         ],
         axis=0,
     )
-    total = jnp.dot(placed[...], cotangent, preferred_element_type=jnp.float32)
+    total = jnp.dot(placed[0], cotangent, preferred_element_type=jnp.float32)
     total += jnp.dot(coef_mine[...], mine[0], preferred_element_type=jnp.float32)
     total += jnp.dot(coef_other[...], other[0], preferred_element_type=jnp.float32)
     out[...] = total.astype(jnp.bfloat16)
 
 
-def table_grad_call(at, coef_mine, coef_other, ids, orders, mine, other, own, far):
+def table_grad_call(at, coef_mine, coef_other, placed, mine, other, own, far):
     whole = lambda *shape: pl.BlockSpec(shape, lambda p, k, at: (0,) * len(shape))
     side = lambda p, at: lax.bitwise_xor(at[1], p)
     block = pl.BlockSpec((1, CORE_ROWS, CHUNK), lambda p, k, at: (side(p, at), 0, k))
@@ -184,16 +206,16 @@
         grid_spec=pltpu.PrefetchScalarGridSpec(
             num_scalar_prefetch=1,
             grid=(2, PER_HALF),
-            in_specs=[whole(512, CORE_ROWS)] * 2 + [whole(2, ROWS), whole(2, ROWS), block, block]
+            in_specs=[whole(512, CORE_ROWS)] * 2
+            + [pl.BlockSpec((1, 512, ROWS), lambda p, k, at: (p, 0, 0)), block, block]
             + [early, late, early, late] * 2,
             out_specs=pl.BlockSpec((512, CHUNK), lambda p, k, at: (0, side(p, at) * PER_HALF + k)),
-            scratch_shapes=[pltpu.VMEM((512, ROWS), jnp.bfloat16)],
         ),
         out_shape=jax.ShapeDtypeStruct((512, D), jnp.bfloat16),
         compiler_params=params(),
         cost_estimate=pl.CostEstimate(flops=4 * ROWS * 512 * D, bytes_accessed=13_000_000, transcendentals=0),
         name="table_grad",
-    )(at, coef_mine, coef_other, ids, orders, mine, other, *own, *far)
+    )(at, *(in_hbm(a) for a in (coef_mine, coef_other, placed, mine, other, *own, *far)))
 
 
 def shards(stacked_rows, tied_table, row_ids):
@@ -221,8 +243,17 @@
     with jax.named_scope("hidden_xy"):
         mine = exchange(jnp.broadcast_to(got[1], (16, 24, HALF)), "yl", "yh", "x").reshape(2, CORE_ROWS, HALF)
         line = jnp.concatenate(line, axis=0)
-        mine, line, table, at, head_orders, input_orders = lax.optimization_barrier(
-            (mine, line, tied_table, at, head_orders, input_orders)
+        head_mine, head_other, placed = small_call(
+            onehots_kernel,
+            "onehots",
+            [((512, CORE_ROWS), jnp.bfloat16)] * 2 + [((2, 512, ROWS), jnp.bfloat16)],
+            at,
+            row_ids,
+            head_orders,
+            input_orders,
+        )
+        mine, line, table, at, head_mine, head_other, placed = lax.optimization_barrier(
+            (mine, line, tied_table, at, head_mine, head_other, placed)
         )
         table = hold(table)
     with jax.named_scope("hidden_core"):
@@ -240,37 +271,41 @@
             for rows in (mine, other)
         ]
     with jax.named_scope("stats"):
-        (stats,) = small_call(stats_kernel, "stats", [((32, 4, CORE_ROWS), jnp.float32)], at, *logits)
-        stats = exchange(stats, "yl", "yh", "x", "core")
-        (stats,) = small_call(merge_kernel, "merge", [((8, 4, CORE_ROWS), jnp.float32)], stats)
-        stats = exchange(stats, "z")
+        (stats,) = small_call(stats_kernel, "stats", [((16, 4, CORE_ROWS), jnp.float32)], at, *logits)
+        stats = exchange(stats, "z", "core")
+        (stats,) = small_call(merge_kernel, "merge", [((16, 4, CORE_ROWS), jnp.float32)], stats)
+        stats, own = lax.optimization_barrier((stats, own))
+        far = [other_core(piece) for piece in own]
+        stats = exchange(stats, "yl", "yh", "x")
     with jax.named_scope("coefficient"):
         *coefficient, turned_mine, turned_other = small_call(
             coefficient_kernel,
             "coefficient",
-            [((CORE_ROWS, 512), jnp.bfloat16)] * 2 + [((512, CORE_ROWS), jnp.bfloat16)] * 2,
+            [((CORE_ROWS, 512), jnp.bfloat16)] * 2,
             at,
             *logits,
             stats,
-            row_ids,
-            head_orders,
-        )
-        *coefficient, own = lax.optimization_barrier((*coefficient, own))
+            head_mine,
+            head_other,
+            far_outs=[((512, CORE_ROWS), jnp.bfloat16)] * 2,
+            scratch=[pltpu.VMEM((2, 512, CORE_ROWS), jnp.bfloat16), pltpu.SemaphoreType.DMA((2,))],
+        )
+        *coefficient, own, far = lax.optimization_barrier((*coefficient, own, far))
     with jax.named_scope("hidden_grad"):
         halves = (table[:, :HALF], table[:, HALF:])
         product = lambda rows, half: jnp.dot(rows, half, preferred_element_type=jnp.float32)
         theirs = [other_core(product(coefficient[1], half).astype(jnp.bfloat16)) for half in halves]
         ours = lax.optimization_barrier([product(coefficient[0], half) for half in halves])
         chip = jnp.stack([(a + b).astype(jnp.bfloat16) for a, b in zip(ours, theirs)])
-        chip, turned_mine, turned_other = lax.optimization_barrier((chip, turned_mine, turned_other))
-    with jax.named_scope("table_grad"):
-        far = [other_core(piece) for piece in own]
-        table_grad = table_grad_call(at, turned_mine, turned_other, row_ids, input_orders, mine, other, own, far)
     with jax.named_scope("hidden_grad"):
         plane = exchange(chip.reshape(16, 24, HALF), "yl", "yh", "x")
-        plane, table_grad = lax.optimization_barrier((plane, table_grad))
-        plane = jnp.sum(plane.astype(jnp.float32), axis=0).astype(jnp.bfloat16).reshape(1, 8, 3, HALF)
-        last = exchange(jnp.broadcast_to(plane, (2, 8, 3, HALF)).reshape(16, 3, HALF), "yl", "z")
+        plane, turned_mine, turned_other, own, far = lax.optimization_barrier(
+            (plane, turned_mine, turned_other, own, far)
+        )
+        (plane,) = small_call(plane_kernel, "plane_sum", [((16, 3, HALF), jnp.bfloat16)], plane)
+        last = exchange(plane, "yl", "z")
+        table_grad = table_grad_call(at, turned_mine, turned_other, placed, mine, other, own, far)
+        last, table_grad = lax.optimization_barrier((last, table_grad))
         last = jnp.sum(last.reshape(2, 8, 3, HALF).astype(jnp.float32), axis=1)
         hidden_grad = last.transpose(1, 0, 2).reshape(3, D).astype(jnp.bfloat16)
     return (table_grad, hidden_grad)

time: 156 us -> 148 us (0.949)
  waiting for transfers between devices: 35.6 us -> 17.8 us
  blocking collectives: 60.2 us -> 72.3 us
  Pallas kernels: 11.6 us -> 18.1 us
  local copies, waits for them, and re-layouts: 10.1 us -> 3.74 us
  other arithmetic: 4.41 us -> 1.47 us
    all_to_all x4, blocking collectives: 60.2 us -> 72.3 us  [exchange(): lax.all_to_all(blocks, AXES, 0, 0, axis_index_groups=groups(*axes), tiled...]
    all_to_all x2, waiting for transfers between devices: 12 us -> 0.01 us  [exchange(): lax.all_to_all(blocks, AXES, 0, 0, axis_index_groups=groups(*axes), tiled...]
    unnamed x16 -> x24, local copies, waits for them, and re-layouts: 7.42 us -> 1.21 us
    ppermute x3, waiting for transfers between devices: 20.1 us -> 16.9 us  [from_x(): return lax.ppermute(array, AXES, pairs)]
    pallas_call x3 -> x5, Pallas kernels: 2.19 us -> 5.27 us  [small_call(): pl.pallas_call(kernel, in_specs=[SCALARS if a.ndim == 1 else BLOCK for a...]
    ppermute x7, waiting for transfers between devices: 3.49 us -> 0.95 us  [other_core(): return lax.ppermute(array, AXES, pairs)]
    pallas_call x1, Pallas kernels: 0.32 us -> 2.34 us  [hold(): pl.pallas_call(hold_kernel, in_specs=[pl.BlockSpec(memory_space=pltpu.Mem...]
    reduce_sum x1 -> x0, other arithmetic: 1.72 us -> none  [shards(): jnp.sum(plane.astype(jnp.float32), axis=0).astype(jnp.bfloat16)]
  transfers between devices with their start and end apart: 15 -> 15, of which waited for: 9 -> 3; matrix products, arithmetic and copies ran while one was open for 4% -> 4% of each run, Pallas kernels for 7% -> 12%
where the time goes in v3:
time: 148 us
  blocking collectives  72.3 us (49%)
  starting transfers between devices  26.9 us (18%)
  Pallas kernels  18.1 us (12%)
  waiting for transfers between devices  17.8 us (12%)
  matrix products  6.23 us (4%)
  local copies, waits for them, and re-layouts  3.74 us (3%)
    all_to_all x4, blocking collectives, exchange(): lax.all_to_all(blocks, AXES, 0, 0, axis_index_groups=groups(*axes), tiled...  72.3 us
    ppermute x3, waiting for transfers between devices, from_x(): return lax.ppermute(array, AXES, pairs)  16.9 us
    all_to_all x2, starting transfers between devices, exchange(): lax.all_to_all(blocks, AXES, 0, 0, axis_index_groups=groups(*axes), tiled...  14.5 us
    pallas_call x1, Pallas kernels, table_grad_call(): pl.pallas_call(table_grad_kernel, grid_spec=pltpu.PrefetchScalarGridSpec(...  10.4 us
    ppermute x3, starting transfers between devices, from_x(): return lax.ppermute(array, AXES, pairs)  5.68 us
    pallas_call x5, Pallas kernels, small_call(): pl.pallas_call(kernel, in_specs=[SCALARS if a.ndim == 1 else BLOCK for a...  5.27 us
    ppermute x3, starting transfers between devices, from_y(): return lax.ppermute(array, AXES, pairs)  4.78 us
    dot_general x4, matrix products, shards(): lax.dot_general(rows[i], half, (((1,), (1,)), ((), ())), preferred_elemen...  3.65 us
  transfers between devices with their start and end apart: 15, of which 3 were waited for; matrix products, arithmetic and copies ran while one was open for 4% of the time, Pallas kernels for 12%

profile of v3, /device:TPU:8, one launch (start us, length us, event | category | flops | bytes accessed | tf_op | source)
XLA Modules:
  0.0 147.5 jit_solution(10892678302190717166)
XLA Ops:
  0.6 0.8 squeeze.24
  1.5 0.1 broadcast_in_dim.4
  1.6 19.7 %all_to_all.30 = bf16[16,3,2304]{2,1,0:T(4,128)(2,1)S(1)} all-to-all(bf16[16,3,2304]{2,1,0:T(4,128)(2,1)S(1)} %bitcast.37), channel_id=1, replica_groups={{0,4,8,12,16,20,24,28,128,132,136,140,144,148,152,156},{1,5,9,13,17,21,..., dimensions={0} | all-to-all | bytes 442368 | tf_op jit(solution)/shard_map/rows_lz/all_to_all | solution.py:40
  21.2 0.1 fusion.47
  21.3 0.1 squeeze.25
  21.4 1.3 broadcast_in_dim.10
  22.7 7.7 %all-to-all-start.1 = ((bf16[16,24,2304]{2,1,0:T(8,128)(2,1)}), bf16[16,24,2304]{2,1,0:T(8,128)(2,1)S(1)}, u32[]{:S(2)}, u32[]{:S(2)}) async-start(bf16[16,24,2304]{2,1,0:T(8,128)(2,1)} %broadcast_in_dim.10), calls=%async_computation.1 | async-start | bytes 3538944 | tf_op jit(solution)/shard_map/hidden_xy/all_to_all | solution.py:40
  30.6 0.1 squeeze.26
  30.7 1.5 %collective-permute-start.2 = (bf16[24,2304]{1,0:T(8,128)(2,1)S(1)}, bf16[24,2304]{1,0:T(8,128)(2,1)S(1)}, u32[]{:S(2)}, u32[]{:S(2)}) collective-permute-start(bf16[24,2304]{1,0:T(8,128)(2,1)S(1)} %squeeze.26), channel_id=1, source_target_pairs={{3,0},{0,1},{1,2},{2,3},{7,4},{4,5},{5,6},{6,7},{11,8},{8,9},{9,10... | collective-permute-start | bytes 331784 | tf_op jit(solution)/shard_map/cotangent_x/ppermute | solution.py:53
  32.2 2.7 %collective-permute-start.1 = (bf16[24,2304]{1,0:T(8,128)(2,1)S(1)}, bf16[24,2304]{1,0:T(8,128)(2,1)S(1)}, u32[]{:S(2)}, u32[]{:S(2)}) collective-permute-start(bf16[24,2304]{1,0:T(8,128)(2,1)S(1)} %squeeze.26), channel_id=1, source_target_pairs={{2,0},{3,1},{0,2},{1,3},{6,4},{7,5},{4,6},{5,7},{10,8},{11,9},{8,1... | collective-permute-start | bytes 331784 | tf_op jit(solution)/shard_map/cotangent_x/ppermute | solution.py:53
  34.9 1.5 collective-permute-start
  36.4 1.5 onehots.1
  37.9 0.9 copy-done.1
  38.8 15.3 %collective-permute-done.2 = bf16[24,2304]{1,0:T(8,128)(2,1)S(1)} collective-permute-done((bf16[24,2304]{1,0:T(8,128)(2,1)S(1)}, bf16[24,2304]{1,0:T(8,128)(2,1)S(1)}, u32[]{:S(2)}, u32[]{:S(2)}) %collective-permute-start.2) | collective-permute-done | bytes 110624 | tf_op jit(solution)/shard_map/cotangent_x/ppermute | solution.py:53
  54.1 1.6 %collective-permute-done.1 = bf16[24,2304]{1,0:T(8,128)(2,1)S(1)} collective-permute-done((bf16[24,2304]{1,0:T(8,128)(2,1)S(1)}, bf16[24,2304]{1,0:T(8,128)(2,1)S(1)}, u32[]{:S(2)}, u32[]{:S(2)}) %collective-permute-start.1) | collective-permute-done | bytes 110624 | tf_op jit(solution)/shard_map/cotangent_x/ppermute | solution.py:53
  55.7 0.1 collective-permute-start.3
  55.8 1.5 %collective-permute-start.6 = (bf16[96,2304]{1,0:T(8,128)(2,1)S(1)}, bf16[96,2304]{1,0:T(8,128)(2,1)S(1)}, u32[]{:S(2)}, u32[]{:S(2)}) collective-permute-start(bf16[96,2304]{1,0:T(8,128)(2,1)S(1)} %pad_maximum_fusion.1.a0), channel_id=1, source_target_pairs={{192,0},{193,1},{194,2},{195,3},{196,4},{197,5},{198,6},{199,7},{2... | collective-permute-start | bytes 1327112 | tf_op jit(solution)/shard_map/cotangent_y/ppermute | solution.py:62
  57.4 1.2 collective-permute-start.5
  58.5 2.1 %collective-permute-start.4 = (bf16[96,2304]{1,0:T(8,128)(2,1)S(1)}, bf16[96,2304]{1,0:T(8,128)(2,1)S(1)}, u32[]{:S(2)}, u32[]{:S(2)}) collective-permute-start(bf16[96,2304]{1,0:T(8,128)(2,1)S(1)} %pad_maximum_fusion.1.a0), channel_id=1, source_target_pairs={{128,0},{129,1},{130,2},{131,3},{132,4},{133,5},{134,6},{135,7},{1... | collective-permute-start | bytes 1327112 | tf_op jit(solution)/shard_map/cotangent_y/ppermute | solution.py:62
  60.6 2.3 %hold.1 = bf16[512,4608]{1,0:T(8,128)(2,1)S(1)} custom-call(bf16[512,4608]{1,0:T(8,128)(2,1)} %source), custom_call_target="tpu_custom_call" | custom-call | tf_op jit(solution)/shard_map/hidden_xy/hold/pallas_call | solution.py:88
  63.0 0.9 fusion.5
  63.9 0.9 fusion.14.mine
  64.8 0.9 fusion.3
  65.7 0.3 copy-done.4
  66.0 0.9 fusion.17.other
  66.9 1.0 stats.1
  68.0 14.0 %all_to_all.31.parts = f32[16,4,192]{2,1,0:T(4,128)S(1)} all-to-all(f32[16,4,192]{2,1,0:T(4,128)S(1)} %stats.1), channel_id=1, replica_groups={{0,32,4,36,8,40,12,44,16,48,20,52,24,56,28,60},{1,33,5,37,9,41,13,45,17..., dimensions={0} | all-to-all | bytes 98304 | tf_op jit(solution)/shard_map/stats/all_to_all | solution.py:40
  82.1 0.4 collective-permute-start.7
  82.6 0.2 collective-permute-start.8
  82.7 0.3 collective-permute-start.9
  83.1 0.2 collective-permute-start.10
  83.2 10.6 %all_to_all.32.parts = f32[16,4,192]{2,1,0:T(4,128)S(1)} all-to-all(f32[16,4,192]{2,1,0:T(4,128)S(1)} %merge.1), channel_id=1, replica_groups={{0,1,2,3,64,65,66,67,128,129,130,131,192,193,194,195},{4,5,6,7,68,69,70..., dimensions={0} | all-to-all | bytes 98304 | tf_op jit(solution)/shard_map/stats/all_to_all | solution.py:40
  93.8 1.7 %coefficient.1 = (bf16[192,512]{1,0:T(8,128)(2,1)S(1)}, bf16[192,512]{1,0:T(8,128)(2,1)S(1)}, bf16[512,192]{1,0:T(8,128)(2,1)}, bf16[512,192]{1,0:T(8,128)(2,1)}) custom-call(s32[3]{0:T(128)S(1)} %pad_add_fusion.1.at, f32[192,512]{1,0:T(8,128)S(1)} %fusion.14.mine, f32[192,512]{1,0:T(8,128)S(1)} %fusion.17.other, f32[16,4,192]{2,1,0:T(4,128)S(1)} %all_to_all.32.parts, ...), custom_call_target="tpu_custom_call" | custom-call | tf_op jit(solution)/shard_map/coefficient/coefficient/pallas_call | solution.py:170
  95.6 0.6 convolution_convert_fusion.1
  96.3 0.1 collective-permute-start.11
  96.4 0.6 convolution_convert_fusion
  97.1 0.6 collective-permute-start.12
  97.7 0.6 fusion.1
  98.3 0.6 fusion.8
  99.0 0.1 fusion.20
  99.1 0.9 collective-permute-done.12
  100.1 0.2 fusion.21
  100.3 0.2 pad_maximum_fusion
  100.4 28.0 %all_to_all.33.blocks = bf16[16,24,2304]{2,1,0:T(8,128)(2,1)S(1)} all-to-all(bf16[16,24,2304]{2,1,0:T(8,128)(2,1)S(1)} %bitcast.32), channel_id=1, replica_groups={{0,1,2,3,64,65,66,67,128,129,130,131,192,193,194,195},{4,5,6,7,68,69,70..., dimensions={0} | all-to-all | bytes 3538944 | tf_op jit(solution)/shard_map/hidden_grad/all_to_all | solution.py:40
  128.5 1.0 plane_sum.1
  129.5 6.9 %all-to-all-start.5 = ((bf16[16,3,2304]{2,1,0:T(4,128)(2,1)}), bf16[16,3,2304]{2,1,0:T(4,128)(2,1)S(1)}, u32[]{:S(2)}, u32[]{:S(2)}) async-start(bf16[16,3,2304]{2,1,0:T(4,128)(2,1)} %plane_sum.1), calls=%async_computation.5 | async-start | bytes 589824 | tf_op jit(solution)/shard_map/hidden_grad/all_to_all | solution.py:40
  136.3 10.4 %table_grad.1 = bf16[512,4608]{1,0:T(8,128)(2,1)} custom-call(s32[3]{0:T(128)S(1)} %pad_add_fusion.1.at, bf16[512,192]{1,0:T(8,128)(2,1)} %get-tuple-element.77.coef_mine, bf16[512,192]{1,0:T(8,128)(2,1)} %get-tuple-element.78.coef_other, bf16[2,512,384]{2,1,0:T(8,128)(2,1)} %copy-done.1, bf16[2,192,2304]{2,1,0:T(8,128)(2,1)} %bitcast.36, ...), custom_call_target="tpu_custom_call" | custom-call | flops 3623878656 | bytes 13000000 | tf_op jit(solution)/shard_map/hidden_grad/table_grad/pallas_call | solution.py:204
  146.8 0.7 bitcast_reduce_fusion
  (41 shorter events, 0.4 us)
Async XLA Ops:
  22.7 13.7 %copy-start = (s32[2,384]{1,0:T(2,128)S(1)}, s32[2,384]{1,0:T(2,128)}, u32[]{:S(2)}) copy-start(s32[2,384]{1,0:T(2,128)} %ids.1) | copy-start | bytes 9220
  22.7 33.0 %all-to-all-start.1 = ((bf16[16,24,2304]{2,1,0:T(8,128)(2,1)}), bf16[16,24,2304]{2,1,0:T(8,128)(2,1)S(1)}, u32[]{:S(2)}, u32[]{:S(2)}) async-start(bf16[16,24,2304]{2,1,0:T(8,128)(2,1)} %broadcast_in_dim.10), calls=%async_computation.1 | async-start | bytes 3538944 | tf_op jit(solution)/shard_map/hidden_xy/all_to_all | solution.py:40
  30.7 23.4 %collective-permute-start.2 = (bf16[24,2304]{1,0:T(8,128)(2,1)S(1)}, bf16[24,2304]{1,0:T(8,128)(2,1)S(1)}, u32[]{:S(2)}, u32[]{:S(2)}) collective-permute-start(bf16[24,2304]{1,0:T(8,128)(2,1)S(1)} %squeeze.26), channel_id=1, source_target_pairs={{3,0},{0,1},{1,2},{2,3},{7,4},{4,5},{5,6},{6,7},{11,8},{8,9},{9,10... | collective-permute-start | bytes 331784 | tf_op jit(solution)/shard_map/cotangent_x/ppermute | solution.py:53
  32.2 23.5 %collective-permute-start.1 = (bf16[24,2304]{1,0:T(8,128)(2,1)S(1)}, bf16[24,2304]{1,0:T(8,128)(2,1)S(1)}, u32[]{:S(2)}, u32[]{:S(2)}) collective-permute-start(bf16[24,2304]{1,0:T(8,128)(2,1)S(1)} %squeeze.26), channel_id=1, source_target_pairs={{2,0},{3,1},{0,2},{1,3},{6,4},{7,5},{4,6},{5,7},{10,8},{11,9},{8,1... | collective-permute-start | bytes 331784 | tf_op jit(solution)/shard_map/cotangent_x/ppermute | solution.py:53
  34.9 20.8 %collective-permute-start = (bf16[24,2304]{1,0:T(8,128)(2,1)S(1)}, bf16[24,2304]{1,0:T(8,128)(2,1)S(1)}, u32[]{:S(2)}, u32[]{:S(2)}) collective-permute-start(bf16[24,2304]{1,0:T(8,128)(2,1)S(1)} %squeeze.26), channel_id=1, source_target_pairs={{1,0},{2,1},{3,2},{0,3},{5,4},{6,5},{7,6},{4,7},{9,8},{10,9},{11,1... | collective-permute-start | bytes 331784 | tf_op jit(solution)/shard_map/cotangent_x/ppermute | solution.py:53
  37.9 0.9 copy-start.1
  55.7 26.4 %copy-start.3 = (bf16[96,2304]{1,0:T(8,128)(2,1)}, bf16[96,2304]{1,0:T(8,128)(2,1)S(1)}, u32[]{:S(2)}) copy-start(bf16[96,2304]{1,0:T(8,128)(2,1)S(1)} %pad_maximum_fusion.1.a0) | copy-start | bytes 1327108
  55.7 8.2 %copy-start.2 = (bf16[16,24,2304]{2,1,0:T(8,128)(2,1)}, bf16[16,24,2304]{2,1,0:T(8,128)(2,1)S(1)}, u32[]{:S(2)}) copy-start(bf16[16,24,2304]{2,1,0:T(8,128)(2,1)S(1)} %all-to-all-done.1) | copy-start | bytes 5308420
  55.7 9.1 %collective-permute-start.3 = (bf16[2,192,2304]{2,1,0:T(8,128)(2,1)S(1)}, bf16[2,192,2304]{2,1,0:T(8,128)(2,1)S(1)}, u32[]{:S(2)}, u32[]{:S(2)}) collective-permute-start(bf16[2,192,2304]{2,1,0:T(8,128)(2,1)S(1)} %bitcast.33), channel_id=1, source_target_pairs={{0,32},{32,0},{1,33},{33,1},{2,34},{34,2},{3,35},{35,3},{4,36},{36... | collective-permute-start | bytes 5308424 | tf_op jit(solution)/shard_map/hidden_core/ppermute | solution.py:45
  55.8 26.2 %collective-permute-start.6 = (bf16[96,2304]{1,0:T(8,128)(2,1)S(1)}, bf16[96,2304]{1,0:T(8,128)(2,1)S(1)}, u32[]{:S(2)}, u32[]{:S(2)}) collective-permute-start(bf16[96,2304]{1,0:T(8,128)(2,1)S(1)} %pad_maximum_fusion.1.a0), channel_id=1, source_target_pairs={{192,0},{193,1},{194,2},{195,3},{196,4},{197,5},{198,6},{199,7},{2... | collective-permute-start | bytes 1327112 | tf_op jit(solution)/shard_map/cotangent_y/ppermute | solution.py:62
  57.4 24.7 %collective-permute-start.5 = (bf16[96,2304]{1,0:T(8,128)(2,1)S(1)}, bf16[96,2304]{1,0:T(8,128)(2,1)S(1)}, u32[]{:S(2)}, u32[]{:S(2)}) collective-permute-start(bf16[96,2304]{1,0:T(8,128)(2,1)S(1)} %pad_maximum_fusion.1.a0), channel_id=1, source_target_pairs={{64,0},{65,1},{66,2},{67,3},{68,4},{69,5},{70,6},{71,7},{72,8},{73... | collective-permute-start | bytes 1327112 | tf_op jit(solution)/shard_map/cotangent_y/ppermute | solution.py:62
  58.5 23.6 %collective-permute-start.4 = (bf16[96,2304]{1,0:T(8,128)(2,1)S(1)}, bf16[96,2304]{1,0:T(8,128)(2,1)S(1)}, u32[]{:S(2)}, u32[]{:S(2)}) collective-permute-start(bf16[96,2304]{1,0:T(8,128)(2,1)S(1)} %pad_maximum_fusion.1.a0), channel_id=1, source_target_pairs={{128,0},{129,1},{130,2},{131,3},{132,4},{133,5},{134,6},{135,7},{1... | collective-permute-start | bytes 1327112 | tf_op jit(solution)/shard_map/cotangent_y/ppermute | solution.py:62
  64.8 1.2 copy-start.4
  82.1 14.2 %copy-start.5 = (bf16[96,2304]{1,0:T(8,128)(2,1)}, bf16[96,2304]{1,0:T(8,128)(2,1)S(1)}, u32[]{:S(2)}) copy-start(bf16[96,2304]{1,0:T(8,128)(2,1)S(1)} %collective-permute-done.6.a3) | copy-start | bytes 1327108
  82.1 14.2 %copy-start.6 = (bf16[96,2304]{1,0:T(8,128)(2,1)}, bf16[96,2304]{1,0:T(8,128)(2,1)S(1)}, u32[]{:S(2)}) copy-start(bf16[96,2304]{1,0:T(8,128)(2,1)S(1)} %collective-permute-done.5.a2) | copy-start | bytes 1327108
  82.1 14.2 %copy-start.7 = (bf16[96,2304]{1,0:T(8,128)(2,1)}, bf16[96,2304]{1,0:T(8,128)(2,1)S(1)}, u32[]{:S(2)}) copy-start(bf16[96,2304]{1,0:T(8,128)(2,1)S(1)} %collective-permute-done.4.a1) | copy-start | bytes 1327108
  82.1 13.4 %collective-permute-start.7 = (bf16[96,2304]{1,0:T(8,128)(2,1)S(1)}, bf16[96,2304]{1,0:T(8,128)(2,1)S(1)}, u32[]{:S(2)}, u32[]{:S(2)}) collective-permute-start(bf16[96,2304]{1,0:T(8,128)(2,1)S(1)} %pad_maximum_fusion.1.a0), channel_id=1, source_target_pairs={{0,32},{32,0},{1,33},{33,1},{2,34},{34,2},{3,35},{35,3},{4,36},{36... | collective-permute-start | bytes 1327112 | tf_op jit(solution)/shard_map/stats/ppermute | solution.py:45
  82.6 13.0 %collective-permute-start.8 = (bf16[96,2304]{1,0:T(8,128)(2,1)S(1)}, bf16[96,2304]{1,0:T(8,128)(2,1)S(1)}, u32[]{:S(2)}, u32[]{:S(2)}) collective-permute-start(bf16[96,2304]{1,0:T(8,128)(2,1)S(1)} %collective-permute-done.4.a1), channel_id=1, source_target_pairs={{0,32},{32,0},{1,33},{33,1},{2,34},{34,2},{3,35},{35,3},{4,36},{36... | collective-permute-start | bytes 1327112 | tf_op jit(solution)/shard_map/stats/ppermute | solution.py:45
  82.7 12.8 %collective-permute-start.9 = (bf16[96,2304]{1,0:T(8,128)(2,1)S(1)}, bf16[96,2304]{1,0:T(8,128)(2,1)S(1)}, u32[]{:S(2)}, u32[]{:S(2)}) collective-permute-start(bf16[96,2304]{1,0:T(8,128)(2,1)S(1)} %collective-permute-done.5.a2), channel_id=1, source_target_pairs={{0,32},{32,0},{1,33},{33,1},{2,34},{34,2},{3,35},{35,3},{4,36},{36... | collective-permute-start | bytes 1327112 | tf_op jit(solution)/shard_map/stats/ppermute | solution.py:45
  83.1 12.5 %collective-permute-start.10 = (bf16[96,2304]{1,0:T(8,128)(2,1)S(1)}, bf16[96,2304]{1,0:T(8,128)(2,1)S(1)}, u32[]{:S(2)}, u32[]{:S(2)}) collective-permute-start(bf16[96,2304]{1,0:T(8,128)(2,1)S(1)} %collective-permute-done.6.a3), channel_id=1, source_target_pairs={{0,32},{32,0},{1,33},{33,1},{2,34},{34,2},{3,35},{35,3},{4,36},{36... | collective-permute-start | bytes 1327112 | tf_op jit(solution)/shard_map/stats/ppermute | solution.py:45
  95.5 1.5 %copy-start.8 = (bf16[96,2304]{1,0:T(8,128)(2,1)}, bf16[96,2304]{1,0:T(8,128)(2,1)S(1)}, u32[]{:S(2)}) copy-start(bf16[96,2304]{1,0:T(8,128)(2,1)S(1)} %collective-permute-done.7.b0) | copy-start | bytes 1327108
  95.6 1.5 %copy-start.9 = (bf16[96,2304]{1,0:T(8,128)(2,1)}, bf16[96,2304]{1,0:T(8,128)(2,1)S(1)}, u32[]{:S(2)}) copy-start(bf16[96,2304]{1,0:T(8,128)(2,1)S(1)} %collective-permute-done.8.b1) | copy-start | bytes 1327108
  95.6 1.5 %copy-start.10 = (bf16[96,2304]{1,0:T(8,128)(2,1)}, bf16[96,2304]{1,0:T(8,128)(2,1)S(1)}, u32[]{:S(2)}) copy-start(bf16[96,2304]{1,0:T(8,128)(2,1)S(1)} %collective-permute-done.9.b2) | copy-start | bytes 1327108
  95.6 1.5 %copy-start.11 = (bf16[96,2304]{1,0:T(8,128)(2,1)}, bf16[96,2304]{1,0:T(8,128)(2,1)S(1)}, u32[]{:S(2)}) copy-start(bf16[96,2304]{1,0:T(8,128)(2,1)S(1)} %collective-permute-done.10.b3) | copy-start | bytes 1327108
  96.3 2.7 %collective-permute-start.11 = (bf16[192,2304]{1,0:T(8,128)(2,1)S(1)}, bf16[192,2304]{1,0:T(8,128)(2,1)S(1)}, u32[]{:S(2)}, u32[]{:S(2)}) collective-permute-start(bf16[192,2304]{1,0:T(8,128)(2,1)S(1)} %convolution_convert_fusion.1), channel_id=1, source_target_pairs={{0,32},{32,0},{1,33},{33,1},{2,34},{34,2},{3,35},{35,3},{4,36},{36... | collective-permute-start | bytes 2654216 | tf_op jit(solution)/shard_map/hidden_grad/ppermute | solution.py:45
  97.1 3.0 %collective-permute-start.12 = (bf16[192,2304]{1,0:T(8,128)(2,1)S(1)}, bf16[192,2304]{1,0:T(8,128)(2,1)S(1)}, u32[]{:S(2)}, u32[]{:S(2)}) collective-permute-start(bf16[192,2304]{1,0:T(8,128)(2,1)S(1)} %convolution_convert_fusion), channel_id=1, source_target_pairs={{0,32},{32,0},{1,33},{33,1},{2,34},{34,2},{3,35},{35,3},{4,36},{36... | collective-permute-start | bytes 2654216 | tf_op jit(solution)/shard_map/hidden_grad/ppermute | solution.py:45
  129.5 17.3 %all-to-all-start.5 = ((bf16[16,3,2304]{2,1,0:T(4,128)(2,1)}), bf16[16,3,2304]{2,1,0:T(4,128)(2,1)S(1)}, u32[]{:S(2)}, u32[]{:S(2)}) async-start(bf16[16,3,2304]{2,1,0:T(4,128)(2,1)} %plane_sum.1), calls=%async_computation.5 | async-start | bytes 589824 | tf_op jit(solution)/shard_map/hidden_grad/all_to_all | solution.py:40

commit v4 on v3

--- a/solution.py
+++ b/solution.py
@@ -11,7 +11,7 @@
 HALF = D // 2
 ROWS = 384
 CORE_ROWS = 192
-CHUNK = 1152
+CHUNK = 768
 PER_HALF = HALF // CHUNK
 AXES = ("section", "dp", "vocab")
 SIZES = {"yl": 2, "yh": 2, "core": 2, "z": 8, "x": 4}
@@ -109,6 +109,13 @@
 BLOCK = pl.BlockSpec(memory_space=pltpu.VMEM)
 
 
+def first_kernel(rows, out):
+    for i in range(2):
+        half = rows[0, :, i * HALF : (i + 1) * HALF]
+        for k in range(8):
+            out[8 * i + k] = half
+
+
 def stats_kernel(at, mine, other, out):
     rows = []
     for logits in (mine, other):
@@ -130,23 +137,23 @@
     out[...] = jnp.broadcast_to(jnp.concatenate(merged(parts[...]), axis=0)[None], out.shape)
 
 
-def coefficient_kernel(at, mine, other, parts, head_mine, head_other, out_mine, out_other, turned_mine, turned_other, kept, sent):
+def coefficient_kernel(at, mine, other, parts, head_mine, head_other, out_mine, out_other):
     high, total = merged(parts[...])
     scale = 1.0 / total
     first = at[0] == 0
-    copies = []
-    sides = ((mine, head_mine, out_mine, turned_mine), (other, head_other, out_other, turned_other))
-    for i, (logits, onehot, out, turned) in enumerate(sides):
+    sides = ((mine, head_mine, out_mine), (other, head_other, out_other))
+    for i, (logits, onehot, out) in enumerate(sides):
         top = pick(first, high[i : i + 1], high[1 - i : 2 - i])
         factor = pick(first, scale[i : i + 1], scale[1 - i : 2 - i])
         values = jnp.exp(logits[...].T - top) * factor - onehot[...].astype(jnp.float32)
-        kept[i] = values.astype(jnp.bfloat16)
-        copy = pltpu.make_async_copy(kept.at[i], turned, sent.at[i])
-        copy.start()
-        copies.append(copy)
         out[...] = values.T.astype(jnp.bfloat16)
-    for copy in copies:
-        copy.wait()
+
+
+def turn_kernel(mine, other, turned, kept, sent):
+    kept[...] = jnp.concatenate([mine[...], other[...]], axis=0).T
+    copy = pltpu.make_async_copy(kept, turned, sent)
+    copy.start()
+    copy.wait()
 
 
 def onehots_kernel(at, ids, head_orders, input_orders, head_mine, head_other, placed):
@@ -178,44 +185,77 @@
     )(*args)
 
 
-def table_grad_kernel(at, coef_mine, coef_other, placed, mine, other, a0, a1, a2, a3, b0, b1, b2, b3, out):
-    even = pl.program_id(0) == 0
-    cotangent = jnp.concatenate(
-        [
-            pick(even, a0[...], a1[...]),
-            pick(even, a2[...], a3[...]),
-            pick(even, b0[...], b1[...]),
-            pick(even, b2[...], b3[...]),
-        ],
-        axis=0,
-    )
-    total = jnp.dot(placed[0], cotangent, preferred_element_type=jnp.float32)
-    total += jnp.dot(coef_mine[...], mine[0], preferred_element_type=jnp.float32)
-    total += jnp.dot(coef_other[...], other[0], preferred_element_type=jnp.float32)
-    out[...] = total.astype(jnp.bfloat16)
-
-
-def table_grad_call(at, coef_mine, coef_other, placed, mine, other, own, far):
-    whole = lambda *shape: pl.BlockSpec(shape, lambda p, k, at: (0,) * len(shape))
-    side = lambda p, at: lax.bitwise_xor(at[1], p)
-    block = pl.BlockSpec((1, CORE_ROWS, CHUNK), lambda p, k, at: (side(p, at), 0, k))
-    early = pl.BlockSpec((96, CHUNK), lambda p, k, at: (0, k * (1 - p) + (PER_HALF - 1) * p))
-    late = pl.BlockSpec((96, CHUNK), lambda p, k, at: (0, k * p))
+def table_grad_kernel(at, turned, placed, mine, other, *refs):
+    own, far, (out, left, right, done, left_sem, right_sem, done_sem) = refs[:4], refs[4:8], refs[8:]
+    lefts = []
+    for part in range(2):
+        for i, source in enumerate((turned, placed.at[part])):
+            target = left.at[part, :, i * ROWS : (i + 1) * ROWS]
+            lefts.append(pltpu.make_async_copy(source, target, left_sem.at[part, i]))
+
+    def load(step):
+        part, slot = step // PER_HALF, step % 2
+        side = lax.bitwise_xor(at[1], part)
+        columns = pl.ds(step % PER_HALF * CHUNK, CHUNK)
+        sources = [mine.at[side, :, columns], other.at[side, :, columns]]
+        sources += [rows[i].at[:, columns] for rows in (own, far) for i in (part, part + 2)]
+        copies, begin = [], 0
+        for i, source in enumerate(sources):
+            rows = CORE_ROWS if i < 2 else 96
+            copies.append(
+                pltpu.make_async_copy(source, right.at[slot, begin : begin + rows, :], right_sem.at[slot, i])
+            )
+            begin += rows
+        return copies
+
+    def store(step):
+        part, slot = step // PER_HALF, step % 2
+        side = lax.bitwise_xor(at[1], part)
+        begin = pl.multiple_of((side * PER_HALF + step % PER_HALF) * CHUNK, CHUNK)
+        return pltpu.make_async_copy(done.at[slot], out.at[:, pl.ds(begin, CHUNK)], done_sem.at[slot])
+
+    steps = 2 * PER_HALF
+    loads, stores = [load(step) for step in range(steps)], [store(step) for step in range(steps)]
+    for copy in lefts[:2] + loads[0] + lefts[2:]:
+        copy.start()
+    for step in range(steps):
+        if step + 1 < steps:
+            for copy in loads[step + 1]:
+                copy.start()
+        part, slot = step // PER_HALF, step % 2
+        if step % PER_HALF == 0:
+            for copy in lefts[2 * part : 2 * part + 2]:
+                copy.wait()
+        for copy in loads[step]:
+            copy.wait()
+        if step >= 2:
+            stores[step - 2].wait()
+        total = jnp.dot(left[part], right[slot], preferred_element_type=jnp.float32)
+        done[slot] = total.astype(jnp.bfloat16)
+        stores[step].start()
+    for copy in stores[-2:]:
+        copy.wait()
+
+
+def table_grad_call(at, turned, placed, mine, other, own, far):
+    arrays = [in_hbm(a) for a in (turned, placed, mine, other, *own, *far)]
     return pl.pallas_call(
         table_grad_kernel,
-        grid_spec=pltpu.PrefetchScalarGridSpec(
-            num_scalar_prefetch=1,
-            grid=(2, PER_HALF),
-            in_specs=[whole(512, CORE_ROWS)] * 2
-            + [pl.BlockSpec((1, 512, ROWS), lambda p, k, at: (p, 0, 0)), block, block]
-            + [early, late, early, late] * 2,
-            out_specs=pl.BlockSpec((512, CHUNK), lambda p, k, at: (0, side(p, at) * PER_HALF + k)),
-        ),
+        in_specs=[SCALARS] + [pl.BlockSpec(memory_space=HBM)] * len(arrays),
+        out_specs=pl.BlockSpec(memory_space=HBM),
         out_shape=jax.ShapeDtypeStruct((512, D), jnp.bfloat16),
+        scratch_shapes=[
+            pltpu.VMEM((2, 512, 2 * ROWS), jnp.bfloat16),
+            pltpu.VMEM((2, 2 * ROWS, CHUNK), jnp.bfloat16),
+            pltpu.VMEM((2, 512, CHUNK), jnp.bfloat16),
+            pltpu.SemaphoreType.DMA((2, 2)),
+            pltpu.SemaphoreType.DMA((2, 6)),
+            pltpu.SemaphoreType.DMA((2,)),
+        ],
         compiler_params=params(),
         cost_estimate=pl.CostEstimate(flops=4 * ROWS * 512 * D, bytes_accessed=13_000_000, transcendentals=0),
         name="table_grad",
-    )(at, *(in_hbm(a) for a in (coef_mine, coef_other, placed, mine, other, *own, *far)))
+    )(at, *arrays)
 
 
 def shards(stacked_rows, tied_table, row_ids):
@@ -235,8 +275,7 @@
         )
 
     with jax.named_scope("rows_lz"):
-        own = stacked_rows[0].reshape(3, 2, HALF).transpose(1, 0, 2)
-        blocks = jnp.broadcast_to(own[:, None], (2, 8, 3, HALF)).reshape(16, 3, HALF)
+        (blocks,) = small_call(first_kernel, "first_blocks", [((16, 3, HALF), jnp.bfloat16)], stacked_rows)
         got = exchange(blocks, "yl", "z").reshape(2, 24, HALF)
     with jax.named_scope("cotangent_x"):
         line = [got[0]] + [from_x(got[0], offset) for offset in (1, 2, 3)]
@@ -278,7 +317,7 @@
         far = [other_core(piece) for piece in own]
         stats = exchange(stats, "yl", "yh", "x")
     with jax.named_scope("coefficient"):
-        *coefficient, turned_mine, turned_other = small_call(
+        coefficient = small_call(
             coefficient_kernel,
             "coefficient",
             [((CORE_ROWS, 512), jnp.bfloat16)] * 2,
@@ -287,8 +326,6 @@
             stats,
             head_mine,
             head_other,
-            far_outs=[((512, CORE_ROWS), jnp.bfloat16)] * 2,
-            scratch=[pltpu.VMEM((2, 512, CORE_ROWS), jnp.bfloat16), pltpu.SemaphoreType.DMA((2,))],
         )
         *coefficient, own, far = lax.optimization_barrier((*coefficient, own, far))
     with jax.named_scope("hidden_grad"):
@@ -298,13 +335,20 @@
         ours = lax.optimization_barrier([product(coefficient[0], half) for half in halves])
         chip = jnp.stack([(a + b).astype(jnp.bfloat16) for a, b in zip(ours, theirs)])
     with jax.named_scope("hidden_grad"):
+        (turned,) = small_call(
+            turn_kernel,
+            "turn",
+            [],
+            *coefficient,
+            far_outs=[((512, ROWS), jnp.bfloat16)],
+            scratch=[pltpu.VMEM((512, ROWS), jnp.bfloat16), pltpu.SemaphoreType.DMA],
+        )
+        chip, turned = lax.optimization_barrier((chip, turned))
         plane = exchange(chip.reshape(16, 24, HALF), "yl", "yh", "x")
-        plane, turned_mine, turned_other, own, far = lax.optimization_barrier(
-            (plane, turned_mine, turned_other, own, far)
-        )
+        plane, turned, own, far = lax.optimization_barrier((plane, turned, own, far))
         (plane,) = small_call(plane_kernel, "plane_sum", [((16, 3, HALF), jnp.bfloat16)], plane)
         last = exchange(plane, "yl", "z")
-        table_grad = table_grad_call(at, turned_mine, turned_other, placed, mine, other, own, far)
+        table_grad = table_grad_call(at, turned, placed, mine, other, own, far)
         last, table_grad = lax.optimization_barrier((last, table_grad))
         last = jnp.sum(last.reshape(2, 8, 3, HALF).astype(jnp.float32), axis=1)
         hidden_grad = last.transpose(1, 0, 2).reshape(3, D).astype(jnp.bfloat16)

time: 148 us -> 147 us (level)
    pallas_call x5 -> x7, Pallas kernels: 5.27 us -> 5.54 us  [small_call(): pl.pallas_call(kernel, in_specs=[SCALARS if a.ndim == 1 else BLOCK for a...]
  transfers between devices with their start and end apart: 15 -> 15, of which waited for: 3 -> 2; matrix products, arithmetic and copies ran while one was open for 4% -> 4% of each run, Pallas kernels for 12% -> 11%
where the time goes in v4:
time: 147 us; the launch traced here: 146 us
  blocking collectives  72.9 us (50%)
  starting transfers between devices  26.4 us (18%)
  Pallas kernels  17.1 us (12%)
  waiting for transfers between devices  16.9 us (11%)
  matrix products  6.23 us (4%)
  local copies, waits for them, and re-layouts  3.58 us (2%)
  other arithmetic  1.47 us (1%)
    all_to_all x4, blocking collectives, exchange(): lax.all_to_all(blocks, AXES, 0, 0, axis_index_groups=groups(*axes), tiled...  72.9 us
    ppermute x3, waiting for transfers between devices, from_x(): return lax.ppermute(array, AXES, pairs)  16.9 us
    all_to_all x2, starting transfers between devices, exchange(): lax.all_to_all(blocks, AXES, 0, 0, axis_index_groups=groups(*axes), tiled...  14.1 us
    pallas_call x1, Pallas kernels, table_grad_call(): pl.pallas_call(table_grad_kernel, in_specs=[SCALARS] + [pl.BlockSpec(memo...  9.18 us
    ppermute x3, starting transfers between devices, from_x(): return lax.ppermute(array, AXES, pairs)  5.68 us
    pallas_call x7, Pallas kernels, small_call(): pl.pallas_call(kernel, in_specs=[SCALARS if a.ndim == 1 else BLOCK for a...  5.54 us
    ppermute x3, starting transfers between devices, from_y(): return lax.ppermute(array, AXES, pairs)  4.78 us
    dot_general x4, matrix products, shards(): lax.dot_general(rows[i], half, (((1,), (1,)), ((), ())), preferred_elemen...  3.65 us
  transfers between devices with their start and end apart: 15, of which 2 were waited for; matrix products, arithmetic and copies ran while one was open for 4% of the time, Pallas kernels for 11%

profile of v4, /device:TPU:8, one launch (start us, length us, event | category | flops | bytes accessed | tf_op | source)
XLA Modules:
  0.0 145.6 jit_solution(12820933639095446724)
XLA Ops:
  0.6 0.8 copy-done
  1.4 19.7 %all_to_all.30 = bf16[16,3,2304]{2,1,0:T(4,128)(2,1)S(1)} all-to-all(bf16[16,3,2304]{2,1,0:T(4,128)(2,1)S(1)} %first_blocks.1), channel_id=1, replica_groups={{0,4,8,12,16,20,24,28,128,132,136,140,144,148,152,156},{1,5,9,13,17,21,..., dimensions={0} | all-to-all | bytes 442368 | tf_op jit(solution)/shard_map/rows_lz/all_to_all | solution.py:40
  21.1 0.1 fusion.47
  21.2 0.1 squeeze.21
  21.3 1.3 broadcast_in_dim.3
  22.6 7.7 %all-to-all-start.1 = ((bf16[16,24,2304]{2,1,0:T(8,128)(2,1)}), bf16[16,24,2304]{2,1,0:T(8,128)(2,1)S(1)}, u32[]{:S(2)}, u32[]{:S(2)}) async-start(bf16[16,24,2304]{2,1,0:T(8,128)(2,1)} %broadcast_in_dim.3), calls=%async_computation.1 | async-start | bytes 3538944 | tf_op jit(solution)/shard_map/hidden_xy/all_to_all | solution.py:40
  30.4 0.1 squeeze.22
  30.5 1.5 %collective-permute-start.2 = (bf16[24,2304]{1,0:T(8,128)(2,1)S(1)}, bf16[24,2304]{1,0:T(8,128)(2,1)S(1)}, u32[]{:S(2)}, u32[]{:S(2)}) collective-permute-start(bf16[24,2304]{1,0:T(8,128)(2,1)S(1)} %squeeze.22), channel_id=1, source_target_pairs={{3,0},{0,1},{1,2},{2,3},{7,4},{4,5},{5,6},{6,7},{11,8},{8,9},{9,10... | collective-permute-start | bytes 331784 | tf_op jit(solution)/shard_map/cotangent_x/ppermute | solution.py:53
  32.1 2.7 %collective-permute-start.1 = (bf16[24,2304]{1,0:T(8,128)(2,1)S(1)}, bf16[24,2304]{1,0:T(8,128)(2,1)S(1)}, u32[]{:S(2)}, u32[]{:S(2)}) collective-permute-start(bf16[24,2304]{1,0:T(8,128)(2,1)S(1)} %squeeze.22), channel_id=1, source_target_pairs={{2,0},{3,1},{0,2},{1,3},{6,4},{7,5},{4,6},{5,7},{10,8},{11,9},{8,1... | collective-permute-start | bytes 331784 | tf_op jit(solution)/shard_map/cotangent_x/ppermute | solution.py:53
  34.7 1.5 %collective-permute-start = (bf16[24,2304]{1,0:T(8,128)(2,1)S(1)}, bf16[24,2304]{1,0:T(8,128)(2,1)S(1)}, u32[]{:S(2)}, u32[]{:S(2)}) collective-permute-start(bf16[24,2304]{1,0:T(8,128)(2,1)S(1)} %squeeze.22), channel_id=1, source_target_pairs={{1,0},{2,1},{3,2},{0,3},{5,4},{6,5},{7,6},{4,7},{9,8},{10,9},{11,1... | collective-permute-start | bytes 331784 | tf_op jit(solution)/shard_map/cotangent_x/ppermute | solution.py:53
  36.2 0.1 pad_add_fusion.1.at
  36.3 1.5 %onehots.1 = (bf16[512,192]{1,0:T(8,128)(2,1)S(1)}, bf16[512,192]{1,0:T(8,128)(2,1)S(1)}, bf16[2,512,384]{2,1,0:T(8,128)(2,1)S(1)}) custom-call(s32[3]{0:T(128)S(1)} %pad_add_fusion.1.at, s32[2,384]{1,0:T(2,128)S(1)} %copy-done.1, s32[2,192]{1,0:T(2,128)S(1)} %fusion.31.head_orders, s32[2,384]{1,0:T(2,128)S(1)} %pad_add_fusion.input_orders), custom_call_target="tpu_custom_call" | custom-call | tf_op jit(solution)/shard_map/hidden_xy/onehots/pallas_call | solution.py:177
  37.8 0.9 copy-done.2
  38.6 15.3 %collective-permute-done.2 = bf16[24,2304]{1,0:T(8,128)(2,1)S(1)} collective-permute-done((bf16[24,2304]{1,0:T(8,128)(2,1)S(1)}, bf16[24,2304]{1,0:T(8,128)(2,1)S(1)}, u32[]{:S(2)}, u32[]{:S(2)}) %collective-permute-start.2) | collective-permute-done | bytes 110624 | tf_op jit(solution)/shard_map/cotangent_x/ppermute | solution.py:53
  54.0 1.6 %collective-permute-done.1 = bf16[24,2304]{1,0:T(8,128)(2,1)S(1)} collective-permute-done((bf16[24,2304]{1,0:T(8,128)(2,1)S(1)}, bf16[24,2304]{1,0:T(8,128)(2,1)S(1)}, u32[]{:S(2)}, u32[]{:S(2)}) %collective-permute-start.1) | collective-permute-done | bytes 110624 | tf_op jit(solution)/shard_map/cotangent_x/ppermute | solution.py:53
  55.6 0.1 collective-permute-start.3
  55.7 0.6 collective-permute-start.4
  56.3 2.4 %collective-permute-start.5 = (bf16[96,2304]{1,0:T(8,128)(2,1)S(1)}, bf16[96,2304]{1,0:T(8,128)(2,1)S(1)}, u32[]{:S(2)}, u32[]{:S(2)}) collective-permute-start(bf16[96,2304]{1,0:T(8,128)(2,1)S(1)} %pad_maximum_fusion.1.refs_0_), channel_id=1, source_target_pairs={{64,0},{65,1},{66,2},{67,3},{68,4},{69,5},{70,6},{71,7},{72,8},{73... | collective-permute-start | bytes 1327112 | tf_op jit(solution)/shard_map/cotangent_y/ppermute | solution.py:62
  58.7 1.8 %collective-permute-start.6 = (bf16[96,2304]{1,0:T(8,128)(2,1)S(1)}, bf16[96,2304]{1,0:T(8,128)(2,1)S(1)}, u32[]{:S(2)}, u32[]{:S(2)}) collective-permute-start(bf16[96,2304]{1,0:T(8,128)(2,1)S(1)} %pad_maximum_fusion.1.refs_0_), channel_id=1, source_target_pairs={{192,0},{193,1},{194,2},{195,3},{196,4},{197,5},{198,6},{199,7},{2... | collective-permute-start | bytes 1327112 | tf_op jit(solution)/shard_map/cotangent_y/ppermute | solution.py:62
  60.5 2.3 %hold.1 = bf16[512,4608]{1,0:T(8,128)(2,1)S(1)} custom-call(bf16[512,4608]{1,0:T(8,128)(2,1)} %source), custom_call_target="tpu_custom_call" | custom-call | tf_op jit(solution)/shard_map/hidden_xy/hold/pallas_call | solution.py:88
  62.8 0.9 fusion.5
  63.7 0.9 fusion.14.mine
  64.7 0.9 fusion.3
  65.6 0.3 copy-done.5
  65.9 0.9 fusion.17.other
  66.8 1.0 stats.1
  67.8 14.1 %all_to_all.31.parts = f32[16,4,192]{2,1,0:T(4,128)S(1)} all-to-all(f32[16,4,192]{2,1,0:T(4,128)S(1)} %stats.1), channel_id=1, replica_groups={{0,32,4,36,8,40,12,44,16,48,20,52,24,56,28,60},{1,33,5,37,9,41,13,45,17..., dimensions={0} | all-to-all | bytes 98304 | tf_op jit(solution)/shard_map/stats/all_to_all | solution.py:40
  82.0 0.4 collective-permute-start.7
  82.4 0.2 collective-permute-start.8
  82.6 0.3 collective-permute-start.9
  82.9 0.2 collective-permute-start.10
  83.1 11.2 %all_to_all.32.parts = f32[16,4,192]{2,1,0:T(4,128)S(1)} all-to-all(f32[16,4,192]{2,1,0:T(4,128)S(1)} %merge.1), channel_id=1, replica_groups={{0,1,2,3,64,65,66,67,128,129,130,131,192,193,194,195},{4,5,6,7,68,69,70..., dimensions={0} | all-to-all | bytes 98304 | tf_op jit(solution)/shard_map/stats/all_to_all | solution.py:40
  94.3 1.0 coefficient.1
  95.4 0.6 convolution_convert_fusion
  96.1 0.1 collective-permute-start.12
  96.2 0.6 convolution_convert_fusion.1
  96.9 0.6 collective-permute-start.11
  97.5 0.6 fusion.8
  98.2 0.6 fusion.1
  98.8 1.0 turn.1.turned
  99.8 0.1 fusion.21
  99.9 0.2 fusion.20
  100.1 0.2 pad_maximum_fusion
  100.3 28.0 %all_to_all.33.blocks = bf16[16,24,2304]{2,1,0:T(8,128)(2,1)S(1)} all-to-all(bf16[16,24,2304]{2,1,0:T(8,128)(2,1)S(1)} %bitcast.30), channel_id=1, replica_groups={{0,1,2,3,64,65,66,67,128,129,130,131,192,193,194,195},{4,5,6,7,68,69,70..., dimensions={0} | all-to-all | bytes 3538944 | tf_op jit(solution)/shard_map/hidden_grad/all_to_all | solution.py:40
  128.3 1.0 plane_sum.1
  129.3 6.4 %all-to-all-start.5 = ((bf16[16,3,2304]{2,1,0:T(4,128)(2,1)}), bf16[16,3,2304]{2,1,0:T(4,128)(2,1)S(1)}, u32[]{:S(2)}, u32[]{:S(2)}) async-start(bf16[16,3,2304]{2,1,0:T(4,128)(2,1)} %plane_sum.1), calls=%async_computation.5 | async-start | bytes 589824 | tf_op jit(solution)/shard_map/hidden_grad/all_to_all | solution.py:40
  135.7 9.2 %table_grad.1 = bf16[512,4608]{1,0:T(8,128)(2,1)} custom-call(s32[3]{0:T(128)S(1)} %pad_add_fusion.1.at, bf16[512,384]{1,0:T(8,128)(2,1)} %turn.1.turned, bf16[2,512,384]{2,1,0:T(8,128)(2,1)} %copy-done.2, bf16[2,192,2304]{2,1,0:T(8,128)(2,1)} %bitcast.34, bf16[2,192,2304]{2,1,0:T(8,128)(2,1)} %copy-done.5, bf16[96,2304]{1,0:T(8,128)(2,1)} %copy-done.4, ...), custom_call_target="tpu_custom_call" | custom-call | flops 3623878656 | bytes 13000000 | tf_op jit(solution)/shard_map/hidden_grad/table_grad/pallas_call | solution.py:242
  144.9 0.7 bitcast_reduce_fusion
  (42 shorter events, 0.3 us)
Async XLA Ops:
  0.6 0.8 copy-start
  22.6 13.7 %copy-start.1 = (s32[2,384]{1,0:T(2,128)S(1)}, s32[2,384]{1,0:T(2,128)}, u32[]{:S(2)}) copy-start(s32[2,384]{1,0:T(2,128)} %ids.1) | copy-start | bytes 9220
  22.6 33.0 %all-to-all-start.1 = ((bf16[16,24,2304]{2,1,0:T(8,128)(2,1)}), bf16[16,24,2304]{2,1,0:T(8,128)(2,1)S(1)}, u32[]{:S(2)}, u32[]{:S(2)}) async-start(bf16[16,24,2304]{2,1,0:T(8,128)(2,1)} %broadcast_in_dim.3), calls=%async_computation.1 | async-start | bytes 3538944 | tf_op jit(solution)/shard_map/hidden_xy/all_to_all | solution.py:40
  30.5 23.4 %collective-permute-start.2 = (bf16[24,2304]{1,0:T(8,128)(2,1)S(1)}, bf16[24,2304]{1,0:T(8,128)(2,1)S(1)}, u32[]{:S(2)}, u32[]{:S(2)}) collective-permute-start(bf16[24,2304]{1,0:T(8,128)(2,1)S(1)} %squeeze.22), channel_id=1, source_target_pairs={{3,0},{0,1},{1,2},{2,3},{7,4},{4,5},{5,6},{6,7},{11,8},{8,9},{9,10... | collective-permute-start | bytes 331784 | tf_op jit(solution)/shard_map/cotangent_x/ppermute | solution.py:53
  32.1 23.5 %collective-permute-start.1 = (bf16[24,2304]{1,0:T(8,128)(2,1)S(1)}, bf16[24,2304]{1,0:T(8,128)(2,1)S(1)}, u32[]{:S(2)}, u32[]{:S(2)}) collective-permute-start(bf16[24,2304]{1,0:T(8,128)(2,1)S(1)} %squeeze.22), channel_id=1, source_target_pairs={{2,0},{3,1},{0,2},{1,3},{6,4},{7,5},{4,6},{5,7},{10,8},{11,9},{8,1... | collective-permute-start | bytes 331784 | tf_op jit(solution)/shard_map/cotangent_x/ppermute | solution.py:53
  34.7 20.8 %collective-permute-start = (bf16[24,2304]{1,0:T(8,128)(2,1)S(1)}, bf16[24,2304]{1,0:T(8,128)(2,1)S(1)}, u32[]{:S(2)}, u32[]{:S(2)}) collective-permute-start(bf16[24,2304]{1,0:T(8,128)(2,1)S(1)} %squeeze.22), channel_id=1, source_target_pairs={{1,0},{2,1},{3,2},{0,3},{5,4},{6,5},{7,6},{4,7},{9,8},{10,9},{11,1... | collective-permute-start | bytes 331784 | tf_op jit(solution)/shard_map/cotangent_x/ppermute | solution.py:53
  37.8 0.9 copy-start.2
  55.6 26.4 %copy-start.4 = (bf16[96,2304]{1,0:T(8,128)(2,1)}, bf16[96,2304]{1,0:T(8,128)(2,1)S(1)}, u32[]{:S(2)}) copy-start(bf16[96,2304]{1,0:T(8,128)(2,1)S(1)} %pad_maximum_fusion.1.refs_0_) | copy-start | bytes 1327108
  55.6 8.2 %copy-start.3 = (bf16[16,24,2304]{2,1,0:T(8,128)(2,1)}, bf16[16,24,2304]{2,1,0:T(8,128)(2,1)S(1)}, u32[]{:S(2)}) copy-start(bf16[16,24,2304]{2,1,0:T(8,128)(2,1)S(1)} %all-to-all-done.1) | copy-start | bytes 5308420
  55.6 9.1 %collective-permute-start.3 = (bf16[2,192,2304]{2,1,0:T(8,128)(2,1)S(1)}, bf16[2,192,2304]{2,1,0:T(8,128)(2,1)S(1)}, u32[]{:S(2)}, u32[]{:S(2)}) collective-permute-start(bf16[2,192,2304]{2,1,0:T(8,128)(2,1)S(1)} %bitcast.31), channel_id=1, source_target_pairs={{0,32},{32,0},{1,33},{33,1},{2,34},{34,2},{3,35},{35,3},{4,36},{36... | collective-permute-start | bytes 5308424 | tf_op jit(solution)/shard_map/hidden_core/ppermute | solution.py:45
  55.7 26.2 %collective-permute-start.4 = (bf16[96,2304]{1,0:T(8,128)(2,1)S(1)}, bf16[96,2304]{1,0:T(8,128)(2,1)S(1)}, u32[]{:S(2)}, u32[]{:S(2)}) collective-permute-start(bf16[96,2304]{1,0:T(8,128)(2,1)S(1)} %pad_maximum_fusion.1.refs_0_), channel_id=1, source_target_pairs={{128,0},{129,1},{130,2},{131,3},{132,4},{133,5},{134,6},{135,7},{1... | collective-permute-start | bytes 1327112 | tf_op jit(solution)/shard_map/cotangent_y/ppermute | solution.py:62
  56.3 25.6 %collective-permute-start.5 = (bf16[96,2304]{1,0:T(8,128)(2,1)S(1)}, bf16[96,2304]{1,0:T(8,128)(2,1)S(1)}, u32[]{:S(2)}, u32[]{:S(2)}) collective-permute-start(bf16[96,2304]{1,0:T(8,128)(2,1)S(1)} %pad_maximum_fusion.1.refs_0_), channel_id=1, source_target_pairs={{64,0},{65,1},{66,2},{67,3},{68,4},{69,5},{70,6},{71,7},{72,8},{73... | collective-permute-start | bytes 1327112 | tf_op jit(solution)/shard_map/cotangent_y/ppermute | solution.py:62
  58.7 23.3 %collective-permute-start.6 = (bf16[96,2304]{1,0:T(8,128)(2,1)S(1)}, bf16[96,2304]{1,0:T(8,128)(2,1)S(1)}, u32[]{:S(2)}, u32[]{:S(2)}) collective-permute-start(bf16[96,2304]{1,0:T(8,128)(2,1)S(1)} %pad_maximum_fusion.1.refs_0_), channel_id=1, source_target_pairs={{192,0},{193,1},{194,2},{195,3},{196,4},{197,5},{198,6},{199,7},{2... | collective-permute-start | bytes 1327112 | tf_op jit(solution)/shard_map/cotangent_y/ppermute | solution.py:62
  64.7 1.2 copy-start.5
  81.9 14.2 %copy-start.6 = (bf16[96,2304]{1,0:T(8,128)(2,1)}, bf16[96,2304]{1,0:T(8,128)(2,1)S(1)}, u32[]{:S(2)}) copy-start(bf16[96,2304]{1,0:T(8,128)(2,1)S(1)} %collective-permute-done.4.refs_1_) | copy-start | bytes 1327108
  82.0 14.2 %copy-start.7 = (bf16[96,2304]{1,0:T(8,128)(2,1)}, bf16[96,2304]{1,0:T(8,128)(2,1)S(1)}, u32[]{:S(2)}) copy-start(bf16[96,2304]{1,0:T(8,128)(2,1)S(1)} %collective-permute-done.5.refs_2_) | copy-start | bytes 1327108
  82.0 14.1 %copy-start.8 = (bf16[96,2304]{1,0:T(8,128)(2,1)}, bf16[96,2304]{1,0:T(8,128)(2,1)S(1)}, u32[]{:S(2)}) copy-start(bf16[96,2304]{1,0:T(8,128)(2,1)S(1)} %collective-permute-done.6.refs_3_) | copy-start | bytes 1327108
  82.0 13.4 %collective-permute-start.7 = (bf16[96,2304]{1,0:T(8,128)(2,1)S(1)}, bf16[96,2304]{1,0:T(8,128)(2,1)S(1)}, u32[]{:S(2)}, u32[]{:S(2)}) collective-permute-start(bf16[96,2304]{1,0:T(8,128)(2,1)S(1)} %pad_maximum_fusion.1.refs_0_), channel_id=1, source_target_pairs={{0,32},{32,0},{1,33},{33,1},{2,34},{34,2},{3,35},{35,3},{4,36},{36... | collective-permute-start | bytes 1327112 | tf_op jit(solution)/shard_map/stats/ppermute | solution.py:45
  82.4 13.0 %collective-permute-start.8 = (bf16[96,2304]{1,0:T(8,128)(2,1)S(1)}, bf16[96,2304]{1,0:T(8,128)(2,1)S(1)}, u32[]{:S(2)}, u32[]{:S(2)}) collective-permute-start(bf16[96,2304]{1,0:T(8,128)(2,1)S(1)} %collective-permute-done.4.refs_1_), channel_id=1, source_target_pairs={{0,32},{32,0},{1,33},{33,1},{2,34},{34,2},{3,35},{35,3},{4,36},{36... | collective-permute-start | bytes 1327112 | tf_op jit(solution)/shard_map/stats/ppermute | solution.py:45
  82.6 12.8 %collective-permute-start.9 = (bf16[96,2304]{1,0:T(8,128)(2,1)S(1)}, bf16[96,2304]{1,0:T(8,128)(2,1)S(1)}, u32[]{:S(2)}, u32[]{:S(2)}) collective-permute-start(bf16[96,2304]{1,0:T(8,128)(2,1)S(1)} %collective-permute-done.5.refs_2_), channel_id=1, source_target_pairs={{0,32},{32,0},{1,33},{33,1},{2,34},{34,2},{3,35},{35,3},{4,36},{36... | collective-permute-start | bytes 1327112 | tf_op jit(solution)/shard_map/stats/ppermute | solution.py:45
  82.9 12.5 %collective-permute-start.10 = (bf16[96,2304]{1,0:T(8,128)(2,1)S(1)}, bf16[96,2304]{1,0:T(8,128)(2,1)S(1)}, u32[]{:S(2)}, u32[]{:S(2)}) collective-permute-start(bf16[96,2304]{1,0:T(8,128)(2,1)S(1)} %collective-permute-done.6.refs_3_), channel_id=1, source_target_pairs={{0,32},{32,0},{1,33},{33,1},{2,34},{34,2},{3,35},{35,3},{4,36},{36... | collective-permute-start | bytes 1327112 | tf_op jit(solution)/shard_map/stats/ppermute | solution.py:45
  95.4 1.5 %copy-start.9 = (bf16[96,2304]{1,0:T(8,128)(2,1)}, bf16[96,2304]{1,0:T(8,128)(2,1)S(1)}, u32[]{:S(2)}) copy-start(bf16[96,2304]{1,0:T(8,128)(2,1)S(1)} %collective-permute-done.7.refs_4_) | copy-start | bytes 1327108
  95.4 1.5 %copy-start.10 = (bf16[96,2304]{1,0:T(8,128)(2,1)}, bf16[96,2304]{1,0:T(8,128)(2,1)S(1)}, u32[]{:S(2)}) copy-start(bf16[96,2304]{1,0:T(8,128)(2,1)S(1)} %collective-permute-done.8.refs_5_) | copy-start | bytes 1327108
  95.4 1.5 %copy-start.11 = (bf16[96,2304]{1,0:T(8,128)(2,1)}, bf16[96,2304]{1,0:T(8,128)(2,1)S(1)}, u32[]{:S(2)}) copy-start(bf16[96,2304]{1,0:T(8,128)(2,1)S(1)} %collective-permute-done.9.refs_6_) | copy-start | bytes 1327108
  95.4 1.5 %copy-start.12 = (bf16[96,2304]{1,0:T(8,128)(2,1)}, bf16[96,2304]{1,0:T(8,128)(2,1)S(1)}, u32[]{:S(2)}) copy-start(bf16[96,2304]{1,0:T(8,128)(2,1)S(1)} %collective-permute-done.10.refs_7_) | copy-start | bytes 1327108
  96.1 3.6 %collective-permute-start.12 = (bf16[192,2304]{1,0:T(8,128)(2,1)S(1)}, bf16[192,2304]{1,0:T(8,128)(2,1)S(1)}, u32[]{:S(2)}, u32[]{:S(2)}) collective-permute-start(bf16[192,2304]{1,0:T(8,128)(2,1)S(1)} %convolution_convert_fusion), channel_id=1, source_target_pairs={{0,32},{32,0},{1,33},{33,1},{2,34},{34,2},{3,35},{35,3},{4,36},{36... | collective-permute-start | bytes 2654216 | tf_op jit(solution)/shard_map/hidden_grad/ppermute | solution.py:45
  96.9 3.0 %collective-permute-start.11 = (bf16[192,2304]{1,0:T(8,128)(2,1)S(1)}, bf16[192,2304]{1,0:T(8,128)(2,1)S(1)}, u32[]{:S(2)}, u32[]{:S(2)}) collective-permute-start(bf16[192,2304]{1,0:T(8,128)(2,1)S(1)} %convolution_convert_fusion.1), channel_id=1, source_target_pairs={{0,32},{32,0},{1,33},{33,1},{2,34},{34,2},{3,35},{35,3},{4,36},{36... | collective-permute-start | bytes 2654216 | tf_op jit(solution)/shard_map/hidden_grad/ppermute | solution.py:45
  129.3 15.6 %all-to-all-start.5 = ((bf16[16,3,2304]{2,1,0:T(4,128)(2,1)}), bf16[16,3,2304]{2,1,0:T(4,128)(2,1)S(1)}, u32[]{:S(2)}, u32[]{:S(2)}) async-start(bf16[16,3,2304]{2,1,0:T(4,128)(2,1)} %plane_sum.1), calls=%async_computation.5 | async-start | bytes 589824 | tf_op jit(solution)/shard_map/hidden_grad/all_to_all | solution.py:40

commit v5 on v4

--- a/solution.py
+++ b/solution.py
@@ -79,9 +79,13 @@
 
 
 def hold_kernel(source, held, arrived):
-    copy = pltpu.make_async_copy(source, held, arrived)
-    copy.start()
-    copy.wait()
+    copies = []
+    for i in range(8):
+        rows = slice(64 * i, 64 * i + 64)
+        copies.append(pltpu.make_async_copy(source.at[rows, :], held.at[rows, :], arrived.at[i]))
+        copies[-1].start()
+    for copy in copies:
+        copy.wait()
 
 
 def hold(array):
@@ -90,7 +94,7 @@
         in_specs=[pl.BlockSpec(memory_space=pltpu.MemorySpace.HBM)],
         out_specs=pl.BlockSpec(memory_space=pltpu.VMEM),
         out_shape=pltpu.VMEM(array.shape, array.dtype),
-        scratch_shapes=[pltpu.SemaphoreType.DMA],
+        scratch_shapes=[pltpu.SemaphoreType.DMA((8,))],
         compiler_params=params(),
         name="hold",
     )(in_hbm(array))
@@ -109,11 +113,41 @@
 BLOCK = pl.BlockSpec(memory_space=pltpu.VMEM)
 
 
+def fold(rows):
+    top = jnp.concatenate([rows[0:1], rows[1:2, : HALF // 2]], axis=1)
+    return jnp.concatenate([top, jnp.concatenate([rows[1:2, HALF // 2 :], rows[2:3]], axis=1)], axis=0)
+
+
+def unfold(pair):
+    middle = jnp.concatenate([pair[0:1, HALF:], pair[1:2, : HALF // 2]], axis=1)
+    return jnp.concatenate([pair[0:1, :HALF], middle, pair[1:2, HALF // 2 :]], axis=0)
+
+
 def first_kernel(rows, out):
     for i in range(2):
-        half = rows[0, :, i * HALF : (i + 1) * HALF]
+        half = fold(rows[0, :, i * HALF : (i + 1) * HALF].astype(jnp.float32)).astype(jnp.bfloat16)
         for k in range(8):
             out[8 * i + k] = half
+
+
+def last_kernel(blocks, out):
+    for i in range(2):
+        total = blocks[8 * i].astype(jnp.float32)
+        for k in range(1, 8):
+            total += blocks[8 * i + k].astype(jnp.float32)
+        out[:, i * HALF : (i + 1) * HALF] = unfold(total).astype(jnp.bfloat16)
+
+
+def rows_kernel(got, cotangent, blocks, hidden, sent):
+    merge = lambda begin: jnp.concatenate([unfold(got[begin + k].astype(jnp.float32)) for k in range(8)], axis=0)
+    hidden[...] = merge(8).astype(jnp.bfloat16)
+    copies = []
+    for i in range(16):
+        copies.append(pltpu.make_async_copy(hidden, blocks.at[i], sent.at[i]))
+        copies[-1].start()
+    cotangent[...] = merge(0).astype(jnp.bfloat16)
+    for copy in copies:
+        copy.wait()
 
 
 def stats_kernel(at, mine, other, out):
@@ -168,7 +202,7 @@
     for i in range(1, blocks.shape[0]):
         total += blocks[i].astype(jnp.float32)
     for k in range(8):
-        rows = total[3 * k : 3 * k + 3].astype(jnp.bfloat16)
+        rows = fold(total[3 * k : 3 * k + 3]).astype(jnp.bfloat16)
         out[k] = rows
         out[8 + k] = rows
 
@@ -275,12 +309,19 @@
         )
 
     with jax.named_scope("rows_lz"):
-        (blocks,) = small_call(first_kernel, "first_blocks", [((16, 3, HALF), jnp.bfloat16)], stacked_rows)
-        got = exchange(blocks, "yl", "z").reshape(2, 24, HALF)
+        (blocks,) = small_call(first_kernel, "first_blocks", [((16, 2, 3 * HALF // 2), jnp.bfloat16)], stacked_rows)
+        cotangent, blocks = small_call(
+            rows_kernel,
+            "rows",
+            [((24, HALF), jnp.bfloat16)],
+            exchange(blocks, "yl", "z"),
+            far_outs=[((16, 24, HALF), jnp.bfloat16)],
+            scratch=[pltpu.VMEM((24, HALF), jnp.bfloat16), pltpu.SemaphoreType.DMA((16,))],
+        )
     with jax.named_scope("cotangent_x"):
-        line = [got[0]] + [from_x(got[0], offset) for offset in (1, 2, 3)]
+        line = [cotangent] + [from_x(cotangent, offset) for offset in (1, 2, 3)]
     with jax.named_scope("hidden_xy"):
-        mine = exchange(jnp.broadcast_to(got[1], (16, 24, HALF)), "yl", "yh", "x").reshape(2, CORE_ROWS, HALF)
+        mine = exchange(blocks, "yl", "yh", "x").reshape(2, CORE_ROWS, HALF)
         line = jnp.concatenate(line, axis=0)
         head_mine, head_other, placed = small_call(
             onehots_kernel,
@@ -346,12 +387,11 @@
         chip, turned = lax.optimization_barrier((chip, turned))
         plane = exchange(chip.reshape(16, 24, HALF), "yl", "yh", "x")
         plane, turned, own, far = lax.optimization_barrier((plane, turned, own, far))
-        (plane,) = small_call(plane_kernel, "plane_sum", [((16, 3, HALF), jnp.bfloat16)], plane)
+        (plane,) = small_call(plane_kernel, "plane_sum", [((16, 2, 3 * HALF // 2), jnp.bfloat16)], plane)
         last = exchange(plane, "yl", "z")
         table_grad = table_grad_call(at, turned, placed, mine, other, own, far)
         last, table_grad = lax.optimization_barrier((last, table_grad))
-        last = jnp.sum(last.reshape(2, 8, 3, HALF).astype(jnp.float32), axis=1)
-        hidden_grad = last.transpose(1, 0, 2).reshape(3, D).astype(jnp.bfloat16)
+        (hidden_grad,) = small_call(last_kernel, "last_sum", [((3, D), jnp.bfloat16)], last)
     return (table_grad, hidden_grad)
 
 

time: 147 us -> 144 us (0.980)
  Pallas kernels: 17.1 us -> 19.4 us
  local copies, waits for them, and re-layouts: 3.58 us -> 1.96 us
    pallas_call x7 -> x9, Pallas kernels: 5.54 us -> 7.79 us  [small_call(): pl.pallas_call(kernel, in_specs=[SCALARS if a.ndim == 1 else BLOCK for a...]
where the time goes in v5:
time: 144 us
  blocking collectives  71.7 us (50%)
  starting transfers between devices  26.1 us (18%)
  Pallas kernels  19.4 us (13%)
  waiting for transfers between devices  16.7 us (12%)
  matrix products  6.23 us (4%)
  local copies, waits for them, and re-layouts  1.96 us (1%)
    all_to_all x4, blocking collectives, exchange(): lax.all_to_all(blocks, AXES, 0, 0, axis_index_groups=groups(*axes), tiled...  71.7 us
    ppermute x3, waiting for transfers between devices, from_x(): return lax.ppermute(array, AXES, pairs)  16.7 us
    all_to_all x2, starting transfers between devices, exchange(): lax.all_to_all(blocks, AXES, 0, 0, axis_index_groups=groups(*axes), tiled...  13.8 us
    pallas_call x1, Pallas kernels, table_grad_call(): pl.pallas_call(table_grad_kernel, in_specs=[SCALARS] + [pl.BlockSpec(memo...  9.22 us
    pallas_call x9, Pallas kernels, small_call(): pl.pallas_call(kernel, in_specs=[SCALARS if a.ndim == 1 else BLOCK for a...  7.79 us
    ppermute x3, starting transfers between devices, from_x(): return lax.ppermute(array, AXES, pairs)  5.68 us
    ppermute x3, starting transfers between devices, from_y(): return lax.ppermute(array, AXES, pairs)  4.78 us
    dot_general x4, matrix products, shards(): lax.dot_general(rows[i], half, (((1,), (1,)), ((), ())), preferred_elemen...  3.65 us
  transfers between devices with their start and end apart: 15, of which 2 were waited for; matrix products, arithmetic and copies ran while one was open for 4% of the time, Pallas kernels for 11%

profile of v5, /device:TPU:8, one launch (start us, length us, event | category | flops | bytes accessed | tf_op | source)
XLA Modules:
  0.0 143.9 jit_solution(15841246748291643856)
XLA Ops:
  0.6 0.8 copy-done
  1.4 18.5 %all_to_all.30.got = bf16[16,2,3456]{2,1,0:T(2,128)(2,1)S(1)} all-to-all(bf16[16,2,3456]{2,1,0:T(2,128)(2,1)S(1)} %first_blocks.1), channel_id=1, replica_groups={{0,4,8,12,16,20,24,28,128,132,136,140,144,148,152,156},{1,5,9,13,17,21,..., dimensions={0} | all-to-all | bytes 442368 | tf_op jit(solution)/shard_map/rows_lz/all_to_all | solution.py:40
  19.9 1.5 %rows.3 = (bf16[24,2304]{1,0:T(8,128)(2,1)S(1)}, bf16[16,24,2304]{2,1,0:T(8,128)(2,1)}) custom-call(bf16[16,2,3456]{2,1,0:T(2,128)(2,1)S(1)} %all_to_all.30.got), custom_call_target="tpu_custom_call" | custom-call | tf_op jit(solution)/shard_map/rows_lz/rows/pallas_call | solution.py:211
  21.4 7.4 %all-to-all-start.1 = ((bf16[16,24,2304]{2,1,0:T(8,128)(2,1)}), bf16[16,24,2304]{2,1,0:T(8,128)(2,1)S(1)}, u32[]{:S(2)}, u32[]{:S(2)}) async-start(bf16[16,24,2304]{2,1,0:T(8,128)(2,1)} %get-tuple-element.47), calls=%async_computation.1 | async-start | bytes 3538944 | tf_op jit(solution)/shard_map/hidden_xy/all_to_all | solution.py:40
  28.9 0.1 multiply_add_fusion
  29.0 1.5 %collective-permute-start.2 = (bf16[24,2304]{1,0:T(8,128)(2,1)S(1)}, bf16[24,2304]{1,0:T(8,128)(2,1)S(1)}, u32[]{:S(2)}, u32[]{:S(2)}) collective-permute-start(bf16[24,2304]{1,0:T(8,128)(2,1)S(1)} %get-tuple-element.48), channel_id=1, source_target_pairs={{3,0},{0,1},{1,2},{2,3},{7,4},{4,5},{5,6},{6,7},{11,8},{8,9},{9,10... | collective-permute-start | bytes 331784 | tf_op jit(solution)/shard_map/cotangent_x/ppermute | solution.py:53
  30.5 2.7 %collective-permute-start.1 = (bf16[24,2304]{1,0:T(8,128)(2,1)S(1)}, bf16[24,2304]{1,0:T(8,128)(2,1)S(1)}, u32[]{:S(2)}, u32[]{:S(2)}) collective-permute-start(bf16[24,2304]{1,0:T(8,128)(2,1)S(1)} %get-tuple-element.48), channel_id=1, source_target_pairs={{2,0},{3,1},{0,2},{1,3},{6,4},{7,5},{4,6},{5,7},{10,8},{11,9},{8,1... | collective-permute-start | bytes 331784 | tf_op jit(solution)/shard_map/cotangent_x/ppermute | solution.py:53
  33.2 1.5 %collective-permute-start = (bf16[24,2304]{1,0:T(8,128)(2,1)S(1)}, bf16[24,2304]{1,0:T(8,128)(2,1)S(1)}, u32[]{:S(2)}, u32[]{:S(2)}) collective-permute-start(bf16[24,2304]{1,0:T(8,128)(2,1)S(1)} %get-tuple-element.48), channel_id=1, source_target_pairs={{1,0},{2,1},{3,2},{0,3},{5,4},{6,5},{7,6},{4,7},{9,8},{10,9},{11,1... | collective-permute-start | bytes 331784 | tf_op jit(solution)/shard_map/cotangent_x/ppermute | solution.py:53
  34.7 0.1 pad_add_fusion.1.at
  34.8 1.5 %onehots.1 = (bf16[512,192]{1,0:T(8,128)(2,1)S(1)}, bf16[512,192]{1,0:T(8,128)(2,1)S(1)}, bf16[2,512,384]{2,1,0:T(8,128)(2,1)S(1)}) custom-call(s32[3]{0:T(128)S(1)} %pad_add_fusion.1.at, s32[2,384]{1,0:T(2,128)S(1)} %copy-done.1, s32[2,192]{1,0:T(2,128)S(1)} %fusion.31.head_orders, s32[2,384]{1,0:T(2,128)S(1)} %pad_add_fusion.input_orders), custom_call_target="tpu_custom_call" | custom-call | tf_op jit(solution)/shard_map/hidden_xy/onehots/pallas_call | solution.py:211
  36.2 0.9 copy-done.2
  37.1 15.2 %collective-permute-done.2 = bf16[24,2304]{1,0:T(8,128)(2,1)S(1)} collective-permute-done((bf16[24,2304]{1,0:T(8,128)(2,1)S(1)}, bf16[24,2304]{1,0:T(8,128)(2,1)S(1)}, u32[]{:S(2)}, u32[]{:S(2)}) %collective-permute-start.2) | collective-permute-done | bytes 110624 | tf_op jit(solution)/shard_map/cotangent_x/ppermute | solution.py:53
  52.3 1.5 %collective-permute-done.1 = bf16[24,2304]{1,0:T(8,128)(2,1)S(1)} collective-permute-done((bf16[24,2304]{1,0:T(8,128)(2,1)S(1)}, bf16[24,2304]{1,0:T(8,128)(2,1)S(1)}, u32[]{:S(2)}, u32[]{:S(2)}) %collective-permute-start.1) | collective-permute-done | bytes 110624 | tf_op jit(solution)/shard_map/cotangent_x/ppermute | solution.py:53
  53.8 0.0 collective-permute-done
  53.9 0.0 all-to-all-done.1
  53.9 0.1 collective-permute-start.3
  54.0 0.7 collective-permute-start.4
  54.7 2.3 %collective-permute-start.5 = (bf16[96,2304]{1,0:T(8,128)(2,1)S(1)}, bf16[96,2304]{1,0:T(8,128)(2,1)S(1)}, u32[]{:S(2)}, u32[]{:S(2)}) collective-permute-start(bf16[96,2304]{1,0:T(8,128)(2,1)S(1)} %pad_maximum_fusion.1.refs_0_), channel_id=1, source_target_pairs={{64,0},{65,1},{66,2},{67,3},{68,4},{69,5},{70,6},{71,7},{72,8},{73... | collective-permute-start | bytes 1327112 | tf_op jit(solution)/shard_map/cotangent_y/ppermute | solution.py:62
  57.0 1.8 %collective-permute-start.6 = (bf16[96,2304]{1,0:T(8,128)(2,1)S(1)}, bf16[96,2304]{1,0:T(8,128)(2,1)S(1)}, u32[]{:S(2)}, u32[]{:S(2)}) collective-permute-start(bf16[96,2304]{1,0:T(8,128)(2,1)S(1)} %pad_maximum_fusion.1.refs_0_), channel_id=1, source_target_pairs={{192,0},{193,1},{194,2},{195,3},{196,4},{197,5},{198,6},{199,7},{2... | collective-permute-start | bytes 1327112 | tf_op jit(solution)/shard_map/cotangent_y/ppermute | solution.py:62
  58.8 2.4 %hold.1 = bf16[512,4608]{1,0:T(8,128)(2,1)S(1)} custom-call(bf16[512,4608]{1,0:T(8,128)(2,1)} %source), custom_call_target="tpu_custom_call" | custom-call | tf_op jit(solution)/shard_map/hidden_xy/hold/pallas_call | solution.py:92
  61.2 0.9 fusion.5
  62.1 0.9 fusion.14.mine
  63.0 0.9 fusion.3
  63.9 0.3 copy-done.5
  64.2 0.9 fusion.17.other
  65.1 1.0 stats.1
  66.1 14.0 %all_to_all.31.parts = f32[16,4,192]{2,1,0:T(4,128)S(1)} all-to-all(f32[16,4,192]{2,1,0:T(4,128)S(1)} %stats.1), channel_id=1, replica_groups={{0,32,4,36,8,40,12,44,16,48,20,52,24,56,28,60},{1,33,5,37,9,41,13,45,17..., dimensions={0} | all-to-all | bytes 98304 | tf_op jit(solution)/shard_map/stats/all_to_all | solution.py:40
  80.2 0.4 collective-permute-start.7
  80.7 0.2 collective-permute-start.8
  80.8 0.3 collective-permute-start.9
  81.2 0.2 collective-permute-start.10
  81.3 11.3 %all_to_all.32.parts = f32[16,4,192]{2,1,0:T(4,128)S(1)} all-to-all(f32[16,4,192]{2,1,0:T(4,128)S(1)} %merge.1), channel_id=1, replica_groups={{0,1,2,3,64,65,66,67,128,129,130,131,192,193,194,195},{4,5,6,7,68,69,70..., dimensions={0} | all-to-all | bytes 98304 | tf_op jit(solution)/shard_map/stats/all_to_all | solution.py:40
  92.7 1.0 coefficient.1
  93.8 0.6 convolution_convert_fusion
  94.5 0.1 collective-permute-start.12
  94.6 0.6 convolution_convert_fusion.1
  95.3 0.6 collective-permute-start.11
  95.8 0.6 fusion.8
  96.5 0.6 fusion.1
  97.1 1.0 turn.1.turned
  98.1 0.1 fusion.21
  98.3 0.2 fusion.20
  98.5 0.2 pad_maximum_fusion
  98.6 28.0 %all_to_all.33.blocks = bf16[16,24,2304]{2,1,0:T(8,128)(2,1)S(1)} all-to-all(bf16[16,24,2304]{2,1,0:T(8,128)(2,1)S(1)} %bitcast.25), channel_id=1, replica_groups={{0,1,2,3,64,65,66,67,128,129,130,131,192,193,194,195},{4,5,6,7,68,69,70..., dimensions={0} | all-to-all | bytes 3538944 | tf_op jit(solution)/shard_map/hidden_grad/all_to_all | solution.py:40
  126.6 1.0 plane_sum.1
  127.6 6.4 %all-to-all-start.5 = ((bf16[16,2,3456]{2,1,0:T(2,128)(2,1)}), bf16[16,2,3456]{2,1,0:T(2,128)(2,1)S(1)}, u32[]{:S(2)}, u32[]{:S(2)}) async-start(bf16[16,2,3456]{2,1,0:T(2,128)(2,1)} %plane_sum.1), calls=%async_computation.5 | async-start | bytes 442368 | tf_op jit(solution)/shard_map/hidden_grad/all_to_all | solution.py:40
  134.0 9.2 %table_grad.1 = bf16[512,4608]{1,0:T(8,128)(2,1)} custom-call(s32[3]{0:T(128)S(1)} %pad_add_fusion.1.at, bf16[512,384]{1,0:T(8,128)(2,1)} %turn.1.turned, bf16[2,512,384]{2,1,0:T(8,128)(2,1)} %copy-done.2, bf16[2,192,2304]{2,1,0:T(8,128)(2,1)} %bitcast.29, bf16[2,192,2304]{2,1,0:T(8,128)(2,1)} %copy-done.5, bf16[96,2304]{1,0:T(8,128)(2,1)} %copy-done.4, ...), custom_call_target="tpu_custom_call" | custom-call | flops 3623878656 | bytes 13000000 | tf_op jit(solution)/shard_map/hidden_grad/table_grad/pallas_call | solution.py:276
  143.2 0.7 last_sum.1
  (39 shorter events, 0.3 us)
Async XLA Ops:
  0.6 0.8 copy-start
  1.4 33.4 %copy-start.1 = (s32[2,384]{1,0:T(2,128)S(1)}, s32[2,384]{1,0:T(2,128)}, u32[]{:S(2)}) copy-start(s32[2,384]{1,0:T(2,128)} %ids.1) | copy-start | bytes 9220
  21.4 32.5 %all-to-all-start.1 = ((bf16[16,24,2304]{2,1,0:T(8,128)(2,1)}), bf16[16,24,2304]{2,1,0:T(8,128)(2,1)S(1)}, u32[]{:S(2)}, u32[]{:S(2)}) async-start(bf16[16,24,2304]{2,1,0:T(8,128)(2,1)} %get-tuple-element.47), calls=%async_computation.1 | async-start | bytes 3538944 | tf_op jit(solution)/shard_map/hidden_xy/all_to_all | solution.py:40
  29.0 23.3 %collective-permute-start.2 = (bf16[24,2304]{1,0:T(8,128)(2,1)S(1)}, bf16[24,2304]{1,0:T(8,128)(2,1)S(1)}, u32[]{:S(2)}, u32[]{:S(2)}) collective-permute-start(bf16[24,2304]{1,0:T(8,128)(2,1)S(1)} %get-tuple-element.48), channel_id=1, source_target_pairs={{3,0},{0,1},{1,2},{2,3},{7,4},{4,5},{5,6},{6,7},{11,8},{8,9},{9,10... | collective-permute-start | bytes 331784 | tf_op jit(solution)/shard_map/cotangent_x/ppermute | solution.py:53
  30.5 23.3 %collective-permute-start.1 = (bf16[24,2304]{1,0:T(8,128)(2,1)S(1)}, bf16[24,2304]{1,0:T(8,128)(2,1)S(1)}, u32[]{:S(2)}, u32[]{:S(2)}) collective-permute-start(bf16[24,2304]{1,0:T(8,128)(2,1)S(1)} %get-tuple-element.48), channel_id=1, source_target_pairs={{2,0},{3,1},{0,2},{1,3},{6,4},{7,5},{4,6},{5,7},{10,8},{11,9},{8,1... | collective-permute-start | bytes 331784 | tf_op jit(solution)/shard_map/cotangent_x/ppermute | solution.py:53
  33.2 20.6 %collective-permute-start = (bf16[24,2304]{1,0:T(8,128)(2,1)S(1)}, bf16[24,2304]{1,0:T(8,128)(2,1)S(1)}, u32[]{:S(2)}, u32[]{:S(2)}) collective-permute-start(bf16[24,2304]{1,0:T(8,128)(2,1)S(1)} %get-tuple-element.48), channel_id=1, source_target_pairs={{1,0},{2,1},{3,2},{0,3},{5,4},{6,5},{7,6},{4,7},{9,8},{10,9},{11,1... | collective-permute-start | bytes 331784 | tf_op jit(solution)/shard_map/cotangent_x/ppermute | solution.py:53
  36.2 0.9 copy-start.2
  53.9 26.3 %copy-start.4 = (bf16[96,2304]{1,0:T(8,128)(2,1)}, bf16[96,2304]{1,0:T(8,128)(2,1)S(1)}, u32[]{:S(2)}) copy-start(bf16[96,2304]{1,0:T(8,128)(2,1)S(1)} %pad_maximum_fusion.1.refs_0_) | copy-start | bytes 1327108
  53.9 8.2 %copy-start.3 = (bf16[16,24,2304]{2,1,0:T(8,128)(2,1)}, bf16[16,24,2304]{2,1,0:T(8,128)(2,1)S(1)}, u32[]{:S(2)}) copy-start(bf16[16,24,2304]{2,1,0:T(8,128)(2,1)S(1)} %all-to-all-done.1) | copy-start | bytes 5308420
  53.9 9.1 %collective-permute-start.3 = (bf16[2,192,2304]{2,1,0:T(8,128)(2,1)S(1)}, bf16[2,192,2304]{2,1,0:T(8,128)(2,1)S(1)}, u32[]{:S(2)}, u32[]{:S(2)}) collective-permute-start(bf16[2,192,2304]{2,1,0:T(8,128)(2,1)S(1)} %bitcast.26), channel_id=1, source_target_pairs={{0,32},{32,0},{1,33},{33,1},{2,34},{34,2},{3,35},{35,3},{4,36},{36... | collective-permute-start | bytes 5308424 | tf_op jit(solution)/shard_map/hidden_core/ppermute | solution.py:45
  54.0 26.2 %collective-permute-start.4 = (bf16[96,2304]{1,0:T(8,128)(2,1)S(1)}, bf16[96,2304]{1,0:T(8,128)(2,1)S(1)}, u32[]{:S(2)}, u32[]{:S(2)}) collective-permute-start(bf16[96,2304]{1,0:T(8,128)(2,1)S(1)} %pad_maximum_fusion.1.refs_0_), channel_id=1, source_target_pairs={{128,0},{129,1},{130,2},{131,3},{132,4},{133,5},{134,6},{135,7},{1... | collective-permute-start | bytes 1327112 | tf_op jit(solution)/shard_map/cotangent_y/ppermute | solution.py:62
  54.7 25.5 %collective-permute-start.5 = (bf16[96,2304]{1,0:T(8,128)(2,1)S(1)}, bf16[96,2304]{1,0:T(8,128)(2,1)S(1)}, u32[]{:S(2)}, u32[]{:S(2)}) collective-permute-start(bf16[96,2304]{1,0:T(8,128)(2,1)S(1)} %pad_maximum_fusion.1.refs_0_), channel_id=1, source_target_pairs={{64,0},{65,1},{66,2},{67,3},{68,4},{69,5},{70,6},{71,7},{72,8},{73... | collective-permute-start | bytes 1327112 | tf_op jit(solution)/shard_map/cotangent_y/ppermute | solution.py:62
  57.0 23.2 %collective-permute-start.6 = (bf16[96,2304]{1,0:T(8,128)(2,1)S(1)}, bf16[96,2304]{1,0:T(8,128)(2,1)S(1)}, u32[]{:S(2)}, u32[]{:S(2)}) collective-permute-start(bf16[96,2304]{1,0:T(8,128)(2,1)S(1)} %pad_maximum_fusion.1.refs_0_), channel_id=1, source_target_pairs={{192,0},{193,1},{194,2},{195,3},{196,4},{197,5},{198,6},{199,7},{2... | collective-permute-start | bytes 1327112 | tf_op jit(solution)/shard_map/cotangent_y/ppermute | solution.py:62
  63.0 1.2 copy-start.5
  80.2 14.3 %copy-start.6 = (bf16[96,2304]{1,0:T(8,128)(2,1)}, bf16[96,2304]{1,0:T(8,128)(2,1)S(1)}, u32[]{:S(2)}) copy-start(bf16[96,2304]{1,0:T(8,128)(2,1)S(1)} %collective-permute-done.4.refs_1_) | copy-start | bytes 1327108
  80.2 14.3 %copy-start.7 = (bf16[96,2304]{1,0:T(8,128)(2,1)}, bf16[96,2304]{1,0:T(8,128)(2,1)S(1)}, u32[]{:S(2)}) copy-start(bf16[96,2304]{1,0:T(8,128)(2,1)S(1)} %collective-permute-done.5.refs_2_) | copy-start | bytes 1327108
  80.2 14.2 %copy-start.8 = (bf16[96,2304]{1,0:T(8,128)(2,1)}, bf16[96,2304]{1,0:T(8,128)(2,1)S(1)}, u32[]{:S(2)}) copy-start(bf16[96,2304]{1,0:T(8,128)(2,1)S(1)} %collective-permute-done.6.refs_3_) | copy-start | bytes 1327108
  80.2 13.5 %collective-permute-start.7 = (bf16[96,2304]{1,0:T(8,128)(2,1)S(1)}, bf16[96,2304]{1,0:T(8,128)(2,1)S(1)}, u32[]{:S(2)}, u32[]{:S(2)}) collective-permute-start(bf16[96,2304]{1,0:T(8,128)(2,1)S(1)} %pad_maximum_fusion.1.refs_0_), channel_id=1, source_target_pairs={{0,32},{32,0},{1,33},{33,1},{2,34},{34,2},{3,35},{35,3},{4,36},{36... | collective-permute-start | bytes 1327112 | tf_op jit(solution)/shard_map/stats/ppermute | solution.py:45
  80.7 13.1 %collective-permute-start.8 = (bf16[96,2304]{1,0:T(8,128)(2,1)S(1)}, bf16[96,2304]{1,0:T(8,128)(2,1)S(1)}, u32[]{:S(2)}, u32[]{:S(2)}) collective-permute-start(bf16[96,2304]{1,0:T(8,128)(2,1)S(1)} %collective-permute-done.4.refs_1_), channel_id=1, source_target_pairs={{0,32},{32,0},{1,33},{33,1},{2,34},{34,2},{3,35},{35,3},{4,36},{36... | collective-permute-start | bytes 1327112 | tf_op jit(solution)/shard_map/stats/ppermute | solution.py:45
  80.8 12.9 %collective-permute-start.9 = (bf16[96,2304]{1,0:T(8,128)(2,1)S(1)}, bf16[96,2304]{1,0:T(8,128)(2,1)S(1)}, u32[]{:S(2)}, u32[]{:S(2)}) collective-permute-start(bf16[96,2304]{1,0:T(8,128)(2,1)S(1)} %collective-permute-done.5.refs_2_), channel_id=1, source_target_pairs={{0,32},{32,0},{1,33},{33,1},{2,34},{34,2},{3,35},{35,3},{4,36},{36... | collective-permute-start | bytes 1327112 | tf_op jit(solution)/shard_map/stats/ppermute | solution.py:45
  81.2 12.6 %collective-permute-start.10 = (bf16[96,2304]{1,0:T(8,128)(2,1)S(1)}, bf16[96,2304]{1,0:T(8,128)(2,1)S(1)}, u32[]{:S(2)}, u32[]{:S(2)}) collective-permute-start(bf16[96,2304]{1,0:T(8,128)(2,1)S(1)} %collective-permute-done.6.refs_3_), channel_id=1, source_target_pairs={{0,32},{32,0},{1,33},{33,1},{2,34},{34,2},{3,35},{35,3},{4,36},{36... | collective-permute-start | bytes 1327112 | tf_op jit(solution)/shard_map/stats/ppermute | solution.py:45
  93.7 1.5 %copy-start.9 = (bf16[96,2304]{1,0:T(8,128)(2,1)}, bf16[96,2304]{1,0:T(8,128)(2,1)S(1)}, u32[]{:S(2)}) copy-start(bf16[96,2304]{1,0:T(8,128)(2,1)S(1)} %collective-permute-done.7.refs_4_) | copy-start | bytes 1327108
  93.7 1.5 %copy-start.10 = (bf16[96,2304]{1,0:T(8,128)(2,1)}, bf16[96,2304]{1,0:T(8,128)(2,1)S(1)}, u32[]{:S(2)}) copy-start(bf16[96,2304]{1,0:T(8,128)(2,1)S(1)} %collective-permute-done.8.refs_5_) | copy-start | bytes 1327108
  93.7 1.5 %copy-start.11 = (bf16[96,2304]{1,0:T(8,128)(2,1)}, bf16[96,2304]{1,0:T(8,128)(2,1)S(1)}, u32[]{:S(2)}) copy-start(bf16[96,2304]{1,0:T(8,128)(2,1)S(1)} %collective-permute-done.9.refs_6_) | copy-start | bytes 1327108
  93.8 1.5 %copy-start.12 = (bf16[96,2304]{1,0:T(8,128)(2,1)}, bf16[96,2304]{1,0:T(8,128)(2,1)S(1)}, u32[]{:S(2)}) copy-start(bf16[96,2304]{1,0:T(8,128)(2,1)S(1)} %collective-permute-done.10.refs_7_) | copy-start | bytes 1327108
  94.5 3.6 %collective-permute-start.12 = (bf16[192,2304]{1,0:T(8,128)(2,1)S(1)}, bf16[192,2304]{1,0:T(8,128)(2,1)S(1)}, u32[]{:S(2)}, u32[]{:S(2)}) collective-permute-start(bf16[192,2304]{1,0:T(8,128)(2,1)S(1)} %convolution_convert_fusion), channel_id=1, source_target_pairs={{0,32},{32,0},{1,33},{33,1},{2,34},{34,2},{3,35},{35,3},{4,36},{36... | collective-permute-start | bytes 2654216 | tf_op jit(solution)/shard_map/hidden_grad/ppermute | solution.py:45
  95.3 3.0 %collective-permute-start.11 = (bf16[192,2304]{1,0:T(8,128)(2,1)S(1)}, bf16[192,2304]{1,0:T(8,128)(2,1)S(1)}, u32[]{:S(2)}, u32[]{:S(2)}) collective-permute-start(bf16[192,2304]{1,0:T(8,128)(2,1)S(1)} %convolution_convert_fusion.1), channel_id=1, source_target_pairs={{0,32},{32,0},{1,33},{33,1},{2,34},{34,2},{3,35},{35,3},{4,36},{36... | collective-permute-start | bytes 2654216 | tf_op jit(solution)/shard_map/hidden_grad/ppermute | solution.py:45
  127.6 15.6 %all-to-all-start.5 = ((bf16[16,2,3456]{2,1,0:T(2,128)(2,1)}), bf16[16,2,3456]{2,1,0:T(2,128)(2,1)S(1)}, u32[]{:S(2)}, u32[]{:S(2)}) async-start(bf16[16,2,3456]{2,1,0:T(2,128)(2,1)} %plane_sum.1), calls=%async_computation.5 | async-start | bytes 442368 | tf_op jit(solution)/shard_map/hidden_grad/all_to_all | solution.py:40

commit v6 on v5

--- a/solution.py
+++ b/solution.py
@@ -250,11 +250,11 @@
 
     steps = 2 * PER_HALF
     loads, stores = [load(step) for step in range(steps)], [store(step) for step in range(steps)]
-    for copy in lefts[:2] + loads[0] + lefts[2:]:
+    for copy in lefts[:2] + loads[0]:
         copy.start()
     for step in range(steps):
         if step + 1 < steps:
-            for copy in loads[step + 1]:
+            for copy in loads[step + 1] + (lefts[2:] if step == 1 else []):
                 copy.start()
         part, slot = step // PER_HALF, step % 2
         if step % PER_HALF == 0:

time: 144 us -> 145 us (level)
  no operation moved by 1% of the time
where the time goes in v6:
time: 145 us; the launch traced here: 144 us
  blocking collectives  71.7 us (49%)
  starting transfers between devices  26.1 us (18%)
  Pallas kernels  19.4 us (13%)
  waiting for transfers between devices  16.7 us (12%)
  matrix products  6.23 us (4%)
  local copies, waits for them, and re-layouts  1.96 us (1%)
    all_to_all x4, blocking collectives, exchange(): lax.all_to_all(blocks, AXES, 0, 0, axis_index_groups=groups(*axes), tiled...  71.7 us
    ppermute x3, waiting for transfers between devices, from_x(): return lax.ppermute(array, AXES, pairs)  16.7 us
    all_to_all x2, starting transfers between devices, exchange(): lax.all_to_all(blocks, AXES, 0, 0, axis_index_groups=groups(*axes), tiled...  13.8 us
    pallas_call x1, Pallas kernels, table_grad_call(): pl.pallas_call(table_grad_kernel, in_specs=[SCALARS] + [pl.BlockSpec(memo...  9.27 us
    pallas_call x9, Pallas kernels, small_call(): pl.pallas_call(kernel, in_specs=[SCALARS if a.ndim == 1 else BLOCK for a...  7.79 us
    ppermute x3, starting transfers between devices, from_x(): return lax.ppermute(array, AXES, pairs)  5.68 us
    ppermute x3, starting transfers between devices, from_y(): return lax.ppermute(array, AXES, pairs)  4.78 us
    dot_general x4, matrix products, shards(): lax.dot_general(rows[i], half, (((1,), (1,)), ((), ())), preferred_elemen...  3.65 us
  transfers between devices with their start and end apart: 15, of which 2 were waited for; matrix products, arithmetic and copies ran while one was open for 4% of the time, Pallas kernels for 11%

profile of v6, /device:TPU:8, one launch (start us, length us, event | category | flops | bytes accessed | tf_op | source)
XLA Modules:
  0.0 144.0 jit_solution(1411022452218180016)
XLA Ops:
  0.6 0.8 copy-done
  1.4 18.5 %all_to_all.30.got = bf16[16,2,3456]{2,1,0:T(2,128)(2,1)S(1)} all-to-all(bf16[16,2,3456]{2,1,0:T(2,128)(2,1)S(1)} %first_blocks.1), channel_id=1, replica_groups={{0,4,8,12,16,20,24,28,128,132,136,140,144,148,152,156},{1,5,9,13,17,21,..., dimensions={0} | all-to-all | bytes 442368 | tf_op jit(solution)/shard_map/rows_lz/all_to_all | solution.py:40
  19.9 1.5 %rows.3 = (bf16[24,2304]{1,0:T(8,128)(2,1)S(1)}, bf16[16,24,2304]{2,1,0:T(8,128)(2,1)}) custom-call(bf16[16,2,3456]{2,1,0:T(2,128)(2,1)S(1)} %all_to_all.30.got), custom_call_target="tpu_custom_call" | custom-call | tf_op jit(solution)/shard_map/rows_lz/rows/pallas_call | solution.py:211
  21.4 7.4 %all-to-all-start.1 = ((bf16[16,24,2304]{2,1,0:T(8,128)(2,1)}), bf16[16,24,2304]{2,1,0:T(8,128)(2,1)S(1)}, u32[]{:S(2)}, u32[]{:S(2)}) async-start(bf16[16,24,2304]{2,1,0:T(8,128)(2,1)} %get-tuple-element.47), calls=%async_computation.1 | async-start | bytes 3538944 | tf_op jit(solution)/shard_map/hidden_xy/all_to_all | solution.py:40
  28.9 0.1 multiply_add_fusion
  29.0 1.5 %collective-permute-start.2 = (bf16[24,2304]{1,0:T(8,128)(2,1)S(1)}, bf16[24,2304]{1,0:T(8,128)(2,1)S(1)}, u32[]{:S(2)}, u32[]{:S(2)}) collective-permute-start(bf16[24,2304]{1,0:T(8,128)(2,1)S(1)} %get-tuple-element.48), channel_id=1, source_target_pairs={{3,0},{0,1},{1,2},{2,3},{7,4},{4,5},{5,6},{6,7},{11,8},{8,9},{9,10... | collective-permute-start | bytes 331784 | tf_op jit(solution)/shard_map/cotangent_x/ppermute | solution.py:53
  30.5 2.7 %collective-permute-start.1 = (bf16[24,2304]{1,0:T(8,128)(2,1)S(1)}, bf16[24,2304]{1,0:T(8,128)(2,1)S(1)}, u32[]{:S(2)}, u32[]{:S(2)}) collective-permute-start(bf16[24,2304]{1,0:T(8,128)(2,1)S(1)} %get-tuple-element.48), channel_id=1, source_target_pairs={{2,0},{3,1},{0,2},{1,3},{6,4},{7,5},{4,6},{5,7},{10,8},{11,9},{8,1... | collective-permute-start | bytes 331784 | tf_op jit(solution)/shard_map/cotangent_x/ppermute | solution.py:53
  33.2 1.5 %collective-permute-start = (bf16[24,2304]{1,0:T(8,128)(2,1)S(1)}, bf16[24,2304]{1,0:T(8,128)(2,1)S(1)}, u32[]{:S(2)}, u32[]{:S(2)}) collective-permute-start(bf16[24,2304]{1,0:T(8,128)(2,1)S(1)} %get-tuple-element.48), channel_id=1, source_target_pairs={{1,0},{2,1},{3,2},{0,3},{5,4},{6,5},{7,6},{4,7},{9,8},{10,9},{11,1... | collective-permute-start | bytes 331784 | tf_op jit(solution)/shard_map/cotangent_x/ppermute | solution.py:53
  34.7 0.1 pad_add_fusion.1.at
  34.8 1.5 %onehots.1 = (bf16[512,192]{1,0:T(8,128)(2,1)S(1)}, bf16[512,192]{1,0:T(8,128)(2,1)S(1)}, bf16[2,512,384]{2,1,0:T(8,128)(2,1)S(1)}) custom-call(s32[3]{0:T(128)S(1)} %pad_add_fusion.1.at, s32[2,384]{1,0:T(2,128)S(1)} %copy-done.1, s32[2,192]{1,0:T(2,128)S(1)} %fusion.31.head_orders, s32[2,384]{1,0:T(2,128)S(1)} %pad_add_fusion.input_orders), custom_call_target="tpu_custom_call" | custom-call | tf_op jit(solution)/shard_map/hidden_xy/onehots/pallas_call | solution.py:211
  36.2 0.9 copy-done.2
  37.1 15.2 %collective-permute-done.2 = bf16[24,2304]{1,0:T(8,128)(2,1)S(1)} collective-permute-done((bf16[24,2304]{1,0:T(8,128)(2,1)S(1)}, bf16[24,2304]{1,0:T(8,128)(2,1)S(1)}, u32[]{:S(2)}, u32[]{:S(2)}) %collective-permute-start.2) | collective-permute-done | bytes 110624 | tf_op jit(solution)/shard_map/cotangent_x/ppermute | solution.py:53
  52.3 1.5 %collective-permute-done.1 = bf16[24,2304]{1,0:T(8,128)(2,1)S(1)} collective-permute-done((bf16[24,2304]{1,0:T(8,128)(2,1)S(1)}, bf16[24,2304]{1,0:T(8,128)(2,1)S(1)}, u32[]{:S(2)}, u32[]{:S(2)}) %collective-permute-start.1) | collective-permute-done | bytes 110624 | tf_op jit(solution)/shard_map/cotangent_x/ppermute | solution.py:53
  53.8 0.0 collective-permute-done
  53.9 0.0 all-to-all-done.1
  53.9 0.1 collective-permute-start.3
  54.0 0.7 collective-permute-start.4
  54.7 2.3 %collective-permute-start.5 = (bf16[96,2304]{1,0:T(8,128)(2,1)S(1)}, bf16[96,2304]{1,0:T(8,128)(2,1)S(1)}, u32[]{:S(2)}, u32[]{:S(2)}) collective-permute-start(bf16[96,2304]{1,0:T(8,128)(2,1)S(1)} %pad_maximum_fusion.1.refs_0_), channel_id=1, source_target_pairs={{64,0},{65,1},{66,2},{67,3},{68,4},{69,5},{70,6},{71,7},{72,8},{73... | collective-permute-start | bytes 1327112 | tf_op jit(solution)/shard_map/cotangent_y/ppermute | solution.py:62
  57.0 1.8 %collective-permute-start.6 = (bf16[96,2304]{1,0:T(8,128)(2,1)S(1)}, bf16[96,2304]{1,0:T(8,128)(2,1)S(1)}, u32[]{:S(2)}, u32[]{:S(2)}) collective-permute-start(bf16[96,2304]{1,0:T(8,128)(2,1)S(1)} %pad_maximum_fusion.1.refs_0_), channel_id=1, source_target_pairs={{192,0},{193,1},{194,2},{195,3},{196,4},{197,5},{198,6},{199,7},{2... | collective-permute-start | bytes 1327112 | tf_op jit(solution)/shard_map/cotangent_y/ppermute | solution.py:62
  58.8 2.4 %hold.1 = bf16[512,4608]{1,0:T(8,128)(2,1)S(1)} custom-call(bf16[512,4608]{1,0:T(8,128)(2,1)} %source), custom_call_target="tpu_custom_call" | custom-call | tf_op jit(solution)/shard_map/hidden_xy/hold/pallas_call | solution.py:92
  61.2 0.9 fusion.5
  62.1 0.9 fusion.14.mine
  63.0 0.9 fusion.3
  63.9 0.3 copy-done.5
  64.2 0.9 fusion.17.other
  65.1 1.0 stats.1
  66.1 14.0 %all_to_all.31.parts = f32[16,4,192]{2,1,0:T(4,128)S(1)} all-to-all(f32[16,4,192]{2,1,0:T(4,128)S(1)} %stats.1), channel_id=1, replica_groups={{0,32,4,36,8,40,12,44,16,48,20,52,24,56,28,60},{1,33,5,37,9,41,13,45,17..., dimensions={0} | all-to-all | bytes 98304 | tf_op jit(solution)/shard_map/stats/all_to_all | solution.py:40
  80.2 0.4 collective-permute-start.7
  80.7 0.2 collective-permute-start.8
  80.8 0.3 collective-permute-start.9
  81.2 0.2 collective-permute-start.10
  81.3 11.3 %all_to_all.32.parts = f32[16,4,192]{2,1,0:T(4,128)S(1)} all-to-all(f32[16,4,192]{2,1,0:T(4,128)S(1)} %merge.1), channel_id=1, replica_groups={{0,1,2,3,64,65,66,67,128,129,130,131,192,193,194,195},{4,5,6,7,68,69,70..., dimensions={0} | all-to-all | bytes 98304 | tf_op jit(solution)/shard_map/stats/all_to_all | solution.py:40
  92.7 1.0 coefficient.1
  93.8 0.6 convolution_convert_fusion
  94.5 0.1 collective-permute-start.12
  94.6 0.6 convolution_convert_fusion.1
  95.3 0.6 collective-permute-start.11
  95.8 0.6 fusion.8
  96.5 0.6 fusion.1
  97.1 1.0 turn.1.turned
  98.1 0.1 fusion.21
  98.3 0.2 fusion.20
  98.5 0.2 pad_maximum_fusion
  98.6 28.0 %all_to_all.33.blocks = bf16[16,24,2304]{2,1,0:T(8,128)(2,1)S(1)} all-to-all(bf16[16,24,2304]{2,1,0:T(8,128)(2,1)S(1)} %bitcast.25), channel_id=1, replica_groups={{0,1,2,3,64,65,66,67,128,129,130,131,192,193,194,195},{4,5,6,7,68,69,70..., dimensions={0} | all-to-all | bytes 3538944 | tf_op jit(solution)/shard_map/hidden_grad/all_to_all | solution.py:40
  126.6 1.0 plane_sum.1
  127.6 6.4 %all-to-all-start.5 = ((bf16[16,2,3456]{2,1,0:T(2,128)(2,1)}), bf16[16,2,3456]{2,1,0:T(2,128)(2,1)S(1)}, u32[]{:S(2)}, u32[]{:S(2)}) async-start(bf16[16,2,3456]{2,1,0:T(2,128)(2,1)} %plane_sum.1), calls=%async_computation.5 | async-start | bytes 442368 | tf_op jit(solution)/shard_map/hidden_grad/all_to_all | solution.py:40
  134.0 9.3 %table_grad.1 = bf16[512,4608]{1,0:T(8,128)(2,1)} custom-call(s32[3]{0:T(128)S(1)} %pad_add_fusion.1.at, bf16[512,384]{1,0:T(8,128)(2,1)} %turn.1.turned, bf16[2,512,384]{2,1,0:T(8,128)(2,1)} %copy-done.2, bf16[2,192,2304]{2,1,0:T(8,128)(2,1)} %bitcast.29, bf16[2,192,2304]{2,1,0:T(8,128)(2,1)} %copy-done.5, bf16[96,2304]{1,0:T(8,128)(2,1)} %copy-done.4, ...), custom_call_target="tpu_custom_call" | custom-call | flops 3623878656 | bytes 13000000 | tf_op jit(solution)/shard_map/hidden_grad/table_grad/pallas_call | solution.py:276
  143.3 0.7 last_sum.1
  (39 shorter events, 0.3 us)
Async XLA Ops:
  0.6 0.8 copy-start
  1.4 33.4 %copy-start.1 = (s32[2,384]{1,0:T(2,128)S(1)}, s32[2,384]{1,0:T(2,128)}, u32[]{:S(2)}) copy-start(s32[2,384]{1,0:T(2,128)} %ids.1) | copy-start | bytes 9220
  21.4 32.5 %all-to-all-start.1 = ((bf16[16,24,2304]{2,1,0:T(8,128)(2,1)}), bf16[16,24,2304]{2,1,0:T(8,128)(2,1)S(1)}, u32[]{:S(2)}, u32[]{:S(2)}) async-start(bf16[16,24,2304]{2,1,0:T(8,128)(2,1)} %get-tuple-element.47), calls=%async_computation.1 | async-start | bytes 3538944 | tf_op jit(solution)/shard_map/hidden_xy/all_to_all | solution.py:40
  29.0 23.3 %collective-permute-start.2 = (bf16[24,2304]{1,0:T(8,128)(2,1)S(1)}, bf16[24,2304]{1,0:T(8,128)(2,1)S(1)}, u32[]{:S(2)}, u32[]{:S(2)}) collective-permute-start(bf16[24,2304]{1,0:T(8,128)(2,1)S(1)} %get-tuple-element.48), channel_id=1, source_target_pairs={{3,0},{0,1},{1,2},{2,3},{7,4},{4,5},{5,6},{6,7},{11,8},{8,9},{9,10... | collective-permute-start | bytes 331784 | tf_op jit(solution)/shard_map/cotangent_x/ppermute | solution.py:53
  30.5 23.3 %collective-permute-start.1 = (bf16[24,2304]{1,0:T(8,128)(2,1)S(1)}, bf16[24,2304]{1,0:T(8,128)(2,1)S(1)}, u32[]{:S(2)}, u32[]{:S(2)}) collective-permute-start(bf16[24,2304]{1,0:T(8,128)(2,1)S(1)} %get-tuple-element.48), channel_id=1, source_target_pairs={{2,0},{3,1},{0,2},{1,3},{6,4},{7,5},{4,6},{5,7},{10,8},{11,9},{8,1... | collective-permute-start | bytes 331784 | tf_op jit(solution)/shard_map/cotangent_x/ppermute | solution.py:53
  33.2 20.6 %collective-permute-start = (bf16[24,2304]{1,0:T(8,128)(2,1)S(1)}, bf16[24,2304]{1,0:T(8,128)(2,1)S(1)}, u32[]{:S(2)}, u32[]{:S(2)}) collective-permute-start(bf16[24,2304]{1,0:T(8,128)(2,1)S(1)} %get-tuple-element.48), channel_id=1, source_target_pairs={{1,0},{2,1},{3,2},{0,3},{5,4},{6,5},{7,6},{4,7},{9,8},{10,9},{11,1... | collective-permute-start | bytes 331784 | tf_op jit(solution)/shard_map/cotangent_x/ppermute | solution.py:53
  36.2 0.9 copy-start.2
  53.9 26.3 %copy-start.4 = (bf16[96,2304]{1,0:T(8,128)(2,1)}, bf16[96,2304]{1,0:T(8,128)(2,1)S(1)}, u32[]{:S(2)}) copy-start(bf16[96,2304]{1,0:T(8,128)(2,1)S(1)} %pad_maximum_fusion.1.refs_0_) | copy-start | bytes 1327108
  53.9 8.2 %copy-start.3 = (bf16[16,24,2304]{2,1,0:T(8,128)(2,1)}, bf16[16,24,2304]{2,1,0:T(8,128)(2,1)S(1)}, u32[]{:S(2)}) copy-start(bf16[16,24,2304]{2,1,0:T(8,128)(2,1)S(1)} %all-to-all-done.1) | copy-start | bytes 5308420
  53.9 9.1 %collective-permute-start.3 = (bf16[2,192,2304]{2,1,0:T(8,128)(2,1)S(1)}, bf16[2,192,2304]{2,1,0:T(8,128)(2,1)S(1)}, u32[]{:S(2)}, u32[]{:S(2)}) collective-permute-start(bf16[2,192,2304]{2,1,0:T(8,128)(2,1)S(1)} %bitcast.26), channel_id=1, source_target_pairs={{0,32},{32,0},{1,33},{33,1},{2,34},{34,2},{3,35},{35,3},{4,36},{36... | collective-permute-start | bytes 5308424 | tf_op jit(solution)/shard_map/hidden_core/ppermute | solution.py:45
  54.0 26.2 %collective-permute-start.4 = (bf16[96,2304]{1,0:T(8,128)(2,1)S(1)}, bf16[96,2304]{1,0:T(8,128)(2,1)S(1)}, u32[]{:S(2)}, u32[]{:S(2)}) collective-permute-start(bf16[96,2304]{1,0:T(8,128)(2,1)S(1)} %pad_maximum_fusion.1.refs_0_), channel_id=1, source_target_pairs={{128,0},{129,1},{130,2},{131,3},{132,4},{133,5},{134,6},{135,7},{1... | collective-permute-start | bytes 1327112 | tf_op jit(solution)/shard_map/cotangent_y/ppermute | solution.py:62
  54.7 25.5 %collective-permute-start.5 = (bf16[96,2304]{1,0:T(8,128)(2,1)S(1)}, bf16[96,2304]{1,0:T(8,128)(2,1)S(1)}, u32[]{:S(2)}, u32[]{:S(2)}) collective-permute-start(bf16[96,2304]{1,0:T(8,128)(2,1)S(1)} %pad_maximum_fusion.1.refs_0_), channel_id=1, source_target_pairs={{64,0},{65,1},{66,2},{67,3},{68,4},{69,5},{70,6},{71,7},{72,8},{73... | collective-permute-start | bytes 1327112 | tf_op jit(solution)/shard_map/cotangent_y/ppermute | solution.py:62
  57.0 23.2 %collective-permute-start.6 = (bf16[96,2304]{1,0:T(8,128)(2,1)S(1)}, bf16[96,2304]{1,0:T(8,128)(2,1)S(1)}, u32[]{:S(2)}, u32[]{:S(2)}) collective-permute-start(bf16[96,2304]{1,0:T(8,128)(2,1)S(1)} %pad_maximum_fusion.1.refs_0_), channel_id=1, source_target_pairs={{192,0},{193,1},{194,2},{195,3},{196,4},{197,5},{198,6},{199,7},{2... | collective-permute-start | bytes 1327112 | tf_op jit(solution)/shard_map/cotangent_y/ppermute | solution.py:62
  63.0 1.2 copy-start.5
  80.2 14.3 %copy-start.6 = (bf16[96,2304]{1,0:T(8,128)(2,1)}, bf16[96,2304]{1,0:T(8,128)(2,1)S(1)}, u32[]{:S(2)}) copy-start(bf16[96,2304]{1,0:T(8,128)(2,1)S(1)} %collective-permute-done.4.refs_1_) | copy-start | bytes 1327108
  80.2 14.3 %copy-start.7 = (bf16[96,2304]{1,0:T(8,128)(2,1)}, bf16[96,2304]{1,0:T(8,128)(2,1)S(1)}, u32[]{:S(2)}) copy-start(bf16[96,2304]{1,0:T(8,128)(2,1)S(1)} %collective-permute-done.5.refs_2_) | copy-start | bytes 1327108
  80.2 14.2 %copy-start.8 = (bf16[96,2304]{1,0:T(8,128)(2,1)}, bf16[96,2304]{1,0:T(8,128)(2,1)S(1)}, u32[]{:S(2)}) copy-start(bf16[96,2304]{1,0:T(8,128)(2,1)S(1)} %collective-permute-done.6.refs_3_) | copy-start | bytes 1327108
  80.2 13.5 %collective-permute-start.7 = (bf16[96,2304]{1,0:T(8,128)(2,1)S(1)}, bf16[96,2304]{1,0:T(8,128)(2,1)S(1)}, u32[]{:S(2)}, u32[]{:S(2)}) collective-permute-start(bf16[96,2304]{1,0:T(8,128)(2,1)S(1)} %pad_maximum_fusion.1.refs_0_), channel_id=1, source_target_pairs={{0,32},{32,0},{1,33},{33,1},{2,34},{34,2},{3,35},{35,3},{4,36},{36... | collective-permute-start | bytes 1327112 | tf_op jit(solution)/shard_map/stats/ppermute | solution.py:45
  80.7 13.1 %collective-permute-start.8 = (bf16[96,2304]{1,0:T(8,128)(2,1)S(1)}, bf16[96,2304]{1,0:T(8,128)(2,1)S(1)}, u32[]{:S(2)}, u32[]{:S(2)}) collective-permute-start(bf16[96,2304]{1,0:T(8,128)(2,1)S(1)} %collective-permute-done.4.refs_1_), channel_id=1, source_target_pairs={{0,32},{32,0},{1,33},{33,1},{2,34},{34,2},{3,35},{35,3},{4,36},{36... | collective-permute-start | bytes 1327112 | tf_op jit(solution)/shard_map/stats/ppermute | solution.py:45
  80.8 12.9 %collective-permute-start.9 = (bf16[96,2304]{1,0:T(8,128)(2,1)S(1)}, bf16[96,2304]{1,0:T(8,128)(2,1)S(1)}, u32[]{:S(2)}, u32[]{:S(2)}) collective-permute-start(bf16[96,2304]{1,0:T(8,128)(2,1)S(1)} %collective-permute-done.5.refs_2_), channel_id=1, source_target_pairs={{0,32},{32,0},{1,33},{33,1},{2,34},{34,2},{3,35},{35,3},{4,36},{36... | collective-permute-start | bytes 1327112 | tf_op jit(solution)/shard_map/stats/ppermute | solution.py:45
  81.2 12.6 %collective-permute-start.10 = (bf16[96,2304]{1,0:T(8,128)(2,1)S(1)}, bf16[96,2304]{1,0:T(8,128)(2,1)S(1)}, u32[]{:S(2)}, u32[]{:S(2)}) collective-permute-start(bf16[96,2304]{1,0:T(8,128)(2,1)S(1)} %collective-permute-done.6.refs_3_), channel_id=1, source_target_pairs={{0,32},{32,0},{1,33},{33,1},{2,34},{34,2},{3,35},{35,3},{4,36},{36... | collective-permute-start | bytes 1327112 | tf_op jit(solution)/shard_map/stats/ppermute | solution.py:45
  93.7 1.5 %copy-start.9 = (bf16[96,2304]{1,0:T(8,128)(2,1)}, bf16[96,2304]{1,0:T(8,128)(2,1)S(1)}, u32[]{:S(2)}) copy-start(bf16[96,2304]{1,0:T(8,128)(2,1)S(1)} %collective-permute-done.7.refs_4_) | copy-start | bytes 1327108
  93.7 1.5 %copy-start.10 = (bf16[96,2304]{1,0:T(8,128)(2,1)}, bf16[96,2304]{1,0:T(8,128)(2,1)S(1)}, u32[]{:S(2)}) copy-start(bf16[96,2304]{1,0:T(8,128)(2,1)S(1)} %collective-permute-done.8.refs_5_) | copy-start | bytes 1327108
  93.7 1.5 %copy-start.11 = (bf16[96,2304]{1,0:T(8,128)(2,1)}, bf16[96,2304]{1,0:T(8,128)(2,1)S(1)}, u32[]{:S(2)}) copy-start(bf16[96,2304]{1,0:T(8,128)(2,1)S(1)} %collective-permute-done.9.refs_6_) | copy-start | bytes 1327108
  93.8 1.5 %copy-start.12 = (bf16[96,2304]{1,0:T(8,128)(2,1)}, bf16[96,2304]{1,0:T(8,128)(2,1)S(1)}, u32[]{:S(2)}) copy-start(bf16[96,2304]{1,0:T(8,128)(2,1)S(1)} %collective-permute-done.10.refs_7_) | copy-start | bytes 1327108
  94.5 3.6 %collective-permute-start.12 = (bf16[192,2304]{1,0:T(8,128)(2,1)S(1)}, bf16[192,2304]{1,0:T(8,128)(2,1)S(1)}, u32[]{:S(2)}, u32[]{:S(2)}) collective-permute-start(bf16[192,2304]{1,0:T(8,128)(2,1)S(1)} %convolution_convert_fusion), channel_id=1, source_target_pairs={{0,32},{32,0},{1,33},{33,1},{2,34},{34,2},{3,35},{35,3},{4,36},{36... | collective-permute-start | bytes 2654216 | tf_op jit(solution)/shard_map/hidden_grad/ppermute | solution.py:45
  95.3 3.0 %collective-permute-start.11 = (bf16[192,2304]{1,0:T(8,128)(2,1)S(1)}, bf16[192,2304]{1,0:T(8,128)(2,1)S(1)}, u32[]{:S(2)}, u32[]{:S(2)}) collective-permute-start(bf16[192,2304]{1,0:T(8,128)(2,1)S(1)} %convolution_convert_fusion.1), channel_id=1, source_target_pairs={{0,32},{32,0},{1,33},{33,1},{2,34},{34,2},{3,35},{35,3},{4,36},{36... | collective-permute-start | bytes 2654216 | tf_op jit(solution)/shard_map/hidden_grad/ppermute | solution.py:45
  127.6 15.6 %all-to-all-start.5 = ((bf16[16,2,3456]{2,1,0:T(2,128)(2,1)}), bf16[16,2,3456]{2,1,0:T(2,128)(2,1)S(1)}, u32[]{:S(2)}, u32[]{:S(2)}) async-start(bf16[16,2,3456]{2,1,0:T(2,128)(2,1)} %plane_sum.1), calls=%async_computation.5 | async-start | bytes 442368 | tf_op jit(solution)/shard_map/hidden_grad/all_to_all | solution.py:40

commit v7 on v5

--- a/solution.py
+++ b/solution.py
@@ -123,7 +123,10 @@
     return jnp.concatenate([pair[0:1, :HALF], middle, pair[1:2, HALF // 2 :]], axis=0)
 
 
-def first_kernel(rows, out):
+def first_kernel(source, out, rows, arrived):
+    copy = pltpu.make_async_copy(source, rows, arrived)
+    copy.start()
+    copy.wait()
     for i in range(2):
         half = fold(rows[0, :, i * HALF : (i + 1) * HALF].astype(jnp.float32)).astype(jnp.bfloat16)
         for k in range(8):
@@ -309,7 +312,15 @@
         )
 
     with jax.named_scope("rows_lz"):
-        (blocks,) = small_call(first_kernel, "first_blocks", [((16, 2, 3 * HALF // 2), jnp.bfloat16)], stacked_rows)
+        blocks = pl.pallas_call(
+            first_kernel,
+            in_specs=[pl.BlockSpec(memory_space=HBM)],
+            out_specs=BLOCK,
+            out_shape=jax.ShapeDtypeStruct((16, 2, 3 * HALF // 2), jnp.bfloat16),
+            scratch_shapes=[pltpu.VMEM((1, 3, D), jnp.bfloat16), pltpu.SemaphoreType.DMA],
+            compiler_params=params(),
+            name="first_blocks",
+        )(in_hbm(stacked_rows))
         cotangent, blocks = small_call(
             rows_kernel,
             "rows",

time: 144 us -> 144 us (level)
    pallas_call x9 -> x8, Pallas kernels: 7.79 us -> 7.74 us  [small_call(): pl.pallas_call(kernel, in_specs=[SCALARS if a.ndim == 1 else BLOCK for a...]
where the time goes in v7:
time: 144 us
  blocking collectives  71.7 us (50%)
  starting transfers between devices  26.1 us (18%)
  Pallas kernels  20.1 us (14%)
  waiting for transfers between devices  16.7 us (12%)
  matrix products  6.23 us (4%)
    all_to_all x4, blocking collectives, exchange(): lax.all_to_all(blocks, AXES, 0, 0, axis_index_groups=groups(*axes), tiled...  71.7 us
    ppermute x3, waiting for transfers between devices, from_x(): return lax.ppermute(array, AXES, pairs)  16.7 us
    all_to_all x2, starting transfers between devices, exchange(): lax.all_to_all(blocks, AXES, 0, 0, axis_index_groups=groups(*axes), tiled...  13.8 us
    pallas_call x1, Pallas kernels, table_grad_call(): pl.pallas_call(table_grad_kernel, in_specs=[SCALARS] + [pl.BlockSpec(memo...  9.17 us
    pallas_call x8, Pallas kernels, small_call(): pl.pallas_call(kernel, in_specs=[SCALARS if a.ndim == 1 else BLOCK for a...  7.74 us
    ppermute x3, starting transfers between devices, from_x(): return lax.ppermute(array, AXES, pairs)  5.68 us
    ppermute x3, starting transfers between devices, from_y(): return lax.ppermute(array, AXES, pairs)  4.78 us
    dot_general x4, matrix products, shards(): lax.dot_general(rows[i], half, (((1,), (1,)), ((), ())), preferred_elemen...  3.65 us
  transfers between devices with their start and end apart: 15, of which 2 were waited for; matrix products, arithmetic and copies ran while one was open for 4% of the time, Pallas kernels for 11%

profile of v7, /device:TPU:8, one launch (start us, length us, event | category | flops | bytes accessed | tf_op | source)
XLA Modules:
  0.0 143.9 jit_solution(1620333547535429568)
XLA Ops:
  0.6 0.8 first_blocks.1
  1.5 18.5 %all_to_all.30.got = bf16[16,2,3456]{2,1,0:T(2,128)(2,1)S(1)} all-to-all(bf16[16,2,3456]{2,1,0:T(2,128)(2,1)S(1)} %first_blocks.1), channel_id=1, replica_groups={{0,4,8,12,16,20,24,28,128,132,136,140,144,148,152,156},{1,5,9,13,17,21,..., dimensions={0} | all-to-all | bytes 442368 | tf_op jit(solution)/shard_map/rows_lz/all_to_all | solution.py:40
  19.9 1.5 %rows.1 = (bf16[24,2304]{1,0:T(8,128)(2,1)S(1)}, bf16[16,24,2304]{2,1,0:T(8,128)(2,1)}) custom-call(bf16[16,2,3456]{2,1,0:T(2,128)(2,1)S(1)} %all_to_all.30.got), custom_call_target="tpu_custom_call" | custom-call | tf_op jit(solution)/shard_map/rows_lz/rows/pallas_call | solution.py:214
  21.4 7.4 %all-to-all-start.1 = ((bf16[16,24,2304]{2,1,0:T(8,128)(2,1)}), bf16[16,24,2304]{2,1,0:T(8,128)(2,1)S(1)}, u32[]{:S(2)}, u32[]{:S(2)}) async-start(bf16[16,24,2304]{2,1,0:T(8,128)(2,1)} %get-tuple-element.47), calls=%async_computation.1 | async-start | bytes 3538944 | tf_op jit(solution)/shard_map/hidden_xy/all_to_all | solution.py:40
  28.9 0.1 multiply_add_fusion
  29.0 1.5 %collective-permute-start.2 = (bf16[24,2304]{1,0:T(8,128)(2,1)S(1)}, bf16[24,2304]{1,0:T(8,128)(2,1)S(1)}, u32[]{:S(2)}, u32[]{:S(2)}) collective-permute-start(bf16[24,2304]{1,0:T(8,128)(2,1)S(1)} %get-tuple-element.48), channel_id=1, source_target_pairs={{3,0},{0,1},{1,2},{2,3},{7,4},{4,5},{5,6},{6,7},{11,8},{8,9},{9,10... | collective-permute-start | bytes 331784 | tf_op jit(solution)/shard_map/cotangent_x/ppermute | solution.py:53
  30.6 2.7 %collective-permute-start.1 = (bf16[24,2304]{1,0:T(8,128)(2,1)S(1)}, bf16[24,2304]{1,0:T(8,128)(2,1)S(1)}, u32[]{:S(2)}, u32[]{:S(2)}) collective-permute-start(bf16[24,2304]{1,0:T(8,128)(2,1)S(1)} %get-tuple-element.48), channel_id=1, source_target_pairs={{2,0},{3,1},{0,2},{1,3},{6,4},{7,5},{4,6},{5,7},{10,8},{11,9},{8,1... | collective-permute-start | bytes 331784 | tf_op jit(solution)/shard_map/cotangent_x/ppermute | solution.py:53
  33.2 1.5 %collective-permute-start = (bf16[24,2304]{1,0:T(8,128)(2,1)S(1)}, bf16[24,2304]{1,0:T(8,128)(2,1)S(1)}, u32[]{:S(2)}, u32[]{:S(2)}) collective-permute-start(bf16[24,2304]{1,0:T(8,128)(2,1)S(1)} %get-tuple-element.48), channel_id=1, source_target_pairs={{1,0},{2,1},{3,2},{0,3},{5,4},{6,5},{7,6},{4,7},{9,8},{10,9},{11,1... | collective-permute-start | bytes 331784 | tf_op jit(solution)/shard_map/cotangent_x/ppermute | solution.py:53
  34.7 0.1 pad_add_fusion.1.at
  34.8 1.5 %onehots.1 = (bf16[512,192]{1,0:T(8,128)(2,1)S(1)}, bf16[512,192]{1,0:T(8,128)(2,1)S(1)}, bf16[2,512,384]{2,1,0:T(8,128)(2,1)S(1)}) custom-call(s32[3]{0:T(128)S(1)} %pad_add_fusion.1.at, s32[2,384]{1,0:T(2,128)S(1)} %copy-done, s32[2,192]{1,0:T(2,128)S(1)} %fusion.31.head_orders, s32[2,384]{1,0:T(2,128)S(1)} %pad_add_fusion.input_orders), custom_call_target="tpu_custom_call" | custom-call | tf_op jit(solution)/shard_map/hidden_xy/onehots/pallas_call | solution.py:214
  36.3 0.9 copy-done.1
  37.2 15.1 %collective-permute-done.2 = bf16[24,2304]{1,0:T(8,128)(2,1)S(1)} collective-permute-done((bf16[24,2304]{1,0:T(8,128)(2,1)S(1)}, bf16[24,2304]{1,0:T(8,128)(2,1)S(1)}, u32[]{:S(2)}, u32[]{:S(2)}) %collective-permute-start.2) | collective-permute-done | bytes 110624 | tf_op jit(solution)/shard_map/cotangent_x/ppermute | solution.py:53
  52.3 1.5 %collective-permute-done.1 = bf16[24,2304]{1,0:T(8,128)(2,1)S(1)} collective-permute-done((bf16[24,2304]{1,0:T(8,128)(2,1)S(1)}, bf16[24,2304]{1,0:T(8,128)(2,1)S(1)}, u32[]{:S(2)}, u32[]{:S(2)}) %collective-permute-start.1) | collective-permute-done | bytes 110624 | tf_op jit(solution)/shard_map/cotangent_x/ppermute | solution.py:53
  53.8 0.0 collective-permute-done
  53.9 0.1 collective-permute-start.3
  54.0 0.7 collective-permute-start.4
  54.7 2.3 %collective-permute-start.5 = (bf16[96,2304]{1,0:T(8,128)(2,1)S(1)}, bf16[96,2304]{1,0:T(8,128)(2,1)S(1)}, u32[]{:S(2)}, u32[]{:S(2)}) collective-permute-start(bf16[96,2304]{1,0:T(8,128)(2,1)S(1)} %pad_maximum_fusion.1.refs_0_), channel_id=1, source_target_pairs={{64,0},{65,1},{66,2},{67,3},{68,4},{69,5},{70,6},{71,7},{72,8},{73... | collective-permute-start | bytes 1327112 | tf_op jit(solution)/shard_map/cotangent_y/ppermute | solution.py:62
  57.0 1.8 %collective-permute-start.6 = (bf16[96,2304]{1,0:T(8,128)(2,1)S(1)}, bf16[96,2304]{1,0:T(8,128)(2,1)S(1)}, u32[]{:S(2)}, u32[]{:S(2)}) collective-permute-start(bf16[96,2304]{1,0:T(8,128)(2,1)S(1)} %pad_maximum_fusion.1.refs_0_), channel_id=1, source_target_pairs={{192,0},{193,1},{194,2},{195,3},{196,4},{197,5},{198,6},{199,7},{2... | collective-permute-start | bytes 1327112 | tf_op jit(solution)/shard_map/cotangent_y/ppermute | solution.py:62
  58.8 2.4 %hold.1 = bf16[512,4608]{1,0:T(8,128)(2,1)S(1)} custom-call(bf16[512,4608]{1,0:T(8,128)(2,1)} %source.2), custom_call_target="tpu_custom_call" | custom-call | tf_op jit(solution)/shard_map/hidden_xy/hold/pallas_call | solution.py:92
  61.2 0.9 fusion.5
  62.1 0.9 fusion.14.mine
  63.0 0.9 fusion.3
  64.0 0.3 copy-done.4
  64.2 0.9 fusion.17.other
  65.2 1.0 stats.1
  66.2 14.0 %all_to_all.31.parts = f32[16,4,192]{2,1,0:T(4,128)S(1)} all-to-all(f32[16,4,192]{2,1,0:T(4,128)S(1)} %stats.1), channel_id=1, replica_groups={{0,32,4,36,8,40,12,44,16,48,20,52,24,56,28,60},{1,33,5,37,9,41,13,45,17..., dimensions={0} | all-to-all | bytes 98304 | tf_op jit(solution)/shard_map/stats/all_to_all | solution.py:40
  80.2 0.0 collective-permute-done.4.refs_1_
  80.3 0.4 collective-permute-start.7
  80.7 0.2 collective-permute-start.8
  80.9 0.3 collective-permute-start.9
  81.2 0.2 collective-permute-start.10
  81.4 11.3 %all_to_all.32.parts = f32[16,4,192]{2,1,0:T(4,128)S(1)} all-to-all(f32[16,4,192]{2,1,0:T(4,128)S(1)} %merge.1), channel_id=1, replica_groups={{0,1,2,3,64,65,66,67,128,129,130,131,192,193,194,195},{4,5,6,7,68,69,70..., dimensions={0} | all-to-all | bytes 98304 | tf_op jit(solution)/shard_map/stats/all_to_all | solution.py:40
  92.7 1.0 coefficient.1
  93.8 0.6 convolution_convert_fusion
  94.5 0.1 collective-permute-start.12
  94.6 0.6 convolution_convert_fusion.1
  95.3 0.6 collective-permute-start.11
  95.9 0.6 fusion.8
  96.5 0.6 fusion.1
  97.2 1.0 turn.1.turned
  98.1 0.1 fusion.21
  98.3 0.2 fusion.20
  98.5 0.2 pad_maximum_fusion
  98.7 28.0 %all_to_all.33.blocks = bf16[16,24,2304]{2,1,0:T(8,128)(2,1)S(1)} all-to-all(bf16[16,24,2304]{2,1,0:T(8,128)(2,1)S(1)} %bitcast.25), channel_id=1, replica_groups={{0,1,2,3,64,65,66,67,128,129,130,131,192,193,194,195},{4,5,6,7,68,69,70..., dimensions={0} | all-to-all | bytes 3538944 | tf_op jit(solution)/shard_map/hidden_grad/all_to_all | solution.py:40
  126.6 1.0 plane_sum.1
  127.7 6.3 %all-to-all-start.5 = ((bf16[16,2,3456]{2,1,0:T(2,128)(2,1)}), bf16[16,2,3456]{2,1,0:T(2,128)(2,1)S(1)}, u32[]{:S(2)}, u32[]{:S(2)}) async-start(bf16[16,2,3456]{2,1,0:T(2,128)(2,1)} %plane_sum.1), calls=%async_computation.5 | async-start | bytes 442368 | tf_op jit(solution)/shard_map/hidden_grad/all_to_all | solution.py:40
  134.0 9.2 %table_grad.1 = bf16[512,4608]{1,0:T(8,128)(2,1)} custom-call(s32[3]{0:T(128)S(1)} %pad_add_fusion.1.at, bf16[512,384]{1,0:T(8,128)(2,1)} %turn.1.turned, bf16[2,512,384]{2,1,0:T(8,128)(2,1)} %copy-done.1, bf16[2,192,2304]{2,1,0:T(8,128)(2,1)} %bitcast.29, bf16[2,192,2304]{2,1,0:T(8,128)(2,1)} %copy-done.4, bf16[96,2304]{1,0:T(8,128)(2,1)} %copy-done.3, ...), custom_call_target="tpu_custom_call" | custom-call | flops 3623878656 | bytes 13000000 | tf_op jit(solution)/shard_map/hidden_grad/table_grad/pallas_call | solution.py:279
  143.2 0.7 last_sum.1
  (37 shorter events, 0.2 us)
Async XLA Ops:
  0.6 34.1 %copy-start = (s32[2,384]{1,0:T(2,128)S(1)}, s32[2,384]{1,0:T(2,128)}, u32[]{:S(2)}) copy-start(s32[2,384]{1,0:T(2,128)} %ids.1) | copy-start | bytes 9220
  21.4 32.5 %all-to-all-start.1 = ((bf16[16,24,2304]{2,1,0:T(8,128)(2,1)}), bf16[16,24,2304]{2,1,0:T(8,128)(2,1)S(1)}, u32[]{:S(2)}, u32[]{:S(2)}) async-start(bf16[16,24,2304]{2,1,0:T(8,128)(2,1)} %get-tuple-element.47), calls=%async_computation.1 | async-start | bytes 3538944 | tf_op jit(solution)/shard_map/hidden_xy/all_to_all | solution.py:40
  29.0 23.3 %collective-permute-start.2 = (bf16[24,2304]{1,0:T(8,128)(2,1)S(1)}, bf16[24,2304]{1,0:T(8,128)(2,1)S(1)}, u32[]{:S(2)}, u32[]{:S(2)}) collective-permute-start(bf16[24,2304]{1,0:T(8,128)(2,1)S(1)} %get-tuple-element.48), channel_id=1, source_target_pairs={{3,0},{0,1},{1,2},{2,3},{7,4},{4,5},{5,6},{6,7},{11,8},{8,9},{9,10... | collective-permute-start | bytes 331784 | tf_op jit(solution)/shard_map/cotangent_x/ppermute | solution.py:53
  30.6 23.3 %collective-permute-start.1 = (bf16[24,2304]{1,0:T(8,128)(2,1)S(1)}, bf16[24,2304]{1,0:T(8,128)(2,1)S(1)}, u32[]{:S(2)}, u32[]{:S(2)}) collective-permute-start(bf16[24,2304]{1,0:T(8,128)(2,1)S(1)} %get-tuple-element.48), channel_id=1, source_target_pairs={{2,0},{3,1},{0,2},{1,3},{6,4},{7,5},{4,6},{5,7},{10,8},{11,9},{8,1... | collective-permute-start | bytes 331784 | tf_op jit(solution)/shard_map/cotangent_x/ppermute | solution.py:53
  33.2 20.6 %collective-permute-start = (bf16[24,2304]{1,0:T(8,128)(2,1)S(1)}, bf16[24,2304]{1,0:T(8,128)(2,1)S(1)}, u32[]{:S(2)}, u32[]{:S(2)}) collective-permute-start(bf16[24,2304]{1,0:T(8,128)(2,1)S(1)} %get-tuple-element.48), channel_id=1, source_target_pairs={{1,0},{2,1},{3,2},{0,3},{5,4},{6,5},{7,6},{4,7},{9,8},{10,9},{11,1... | collective-permute-start | bytes 331784 | tf_op jit(solution)/shard_map/cotangent_x/ppermute | solution.py:53
  36.3 0.9 copy-start.1
  53.9 26.4 %copy-start.3 = (bf16[96,2304]{1,0:T(8,128)(2,1)}, bf16[96,2304]{1,0:T(8,128)(2,1)S(1)}, u32[]{:S(2)}) copy-start(bf16[96,2304]{1,0:T(8,128)(2,1)S(1)} %pad_maximum_fusion.1.refs_0_) | copy-start | bytes 1327108
  53.9 8.2 %copy-start.2 = (bf16[16,24,2304]{2,1,0:T(8,128)(2,1)}, bf16[16,24,2304]{2,1,0:T(8,128)(2,1)S(1)}, u32[]{:S(2)}) copy-start(bf16[16,24,2304]{2,1,0:T(8,128)(2,1)S(1)} %all-to-all-done.1) | copy-start | bytes 5308420
  53.9 9.1 %collective-permute-start.3 = (bf16[2,192,2304]{2,1,0:T(8,128)(2,1)S(1)}, bf16[2,192,2304]{2,1,0:T(8,128)(2,1)S(1)}, u32[]{:S(2)}, u32[]{:S(2)}) collective-permute-start(bf16[2,192,2304]{2,1,0:T(8,128)(2,1)S(1)} %bitcast.26), channel_id=1, source_target_pairs={{0,32},{32,0},{1,33},{33,1},{2,34},{34,2},{3,35},{35,3},{4,36},{36... | collective-permute-start | bytes 5308424 | tf_op jit(solution)/shard_map/hidden_core/ppermute | solution.py:45
  54.0 26.2 %collective-permute-start.4 = (bf16[96,2304]{1,0:T(8,128)(2,1)S(1)}, bf16[96,2304]{1,0:T(8,128)(2,1)S(1)}, u32[]{:S(2)}, u32[]{:S(2)}) collective-permute-start(bf16[96,2304]{1,0:T(8,128)(2,1)S(1)} %pad_maximum_fusion.1.refs_0_), channel_id=1, source_target_pairs={{128,0},{129,1},{130,2},{131,3},{132,4},{133,5},{134,6},{135,7},{1... | collective-permute-start | bytes 1327112 | tf_op jit(solution)/shard_map/cotangent_y/ppermute | solution.py:62
  54.7 25.5 %collective-permute-start.5 = (bf16[96,2304]{1,0:T(8,128)(2,1)S(1)}, bf16[96,2304]{1,0:T(8,128)(2,1)S(1)}, u32[]{:S(2)}, u32[]{:S(2)}) collective-permute-start(bf16[96,2304]{1,0:T(8,128)(2,1)S(1)} %pad_maximum_fusion.1.refs_0_), channel_id=1, source_target_pairs={{64,0},{65,1},{66,2},{67,3},{68,4},{69,5},{70,6},{71,7},{72,8},{73... | collective-permute-start | bytes 1327112 | tf_op jit(solution)/shard_map/cotangent_y/ppermute | solution.py:62
  57.0 23.2 %collective-permute-start.6 = (bf16[96,2304]{1,0:T(8,128)(2,1)S(1)}, bf16[96,2304]{1,0:T(8,128)(2,1)S(1)}, u32[]{:S(2)}, u32[]{:S(2)}) collective-permute-start(bf16[96,2304]{1,0:T(8,128)(2,1)S(1)} %pad_maximum_fusion.1.refs_0_), channel_id=1, source_target_pairs={{192,0},{193,1},{194,2},{195,3},{196,4},{197,5},{198,6},{199,7},{2... | collective-permute-start | bytes 1327112 | tf_op jit(solution)/shard_map/cotangent_y/ppermute | solution.py:62
  63.0 1.2 copy-start.4
  80.2 14.3 %copy-start.5 = (bf16[96,2304]{1,0:T(8,128)(2,1)}, bf16[96,2304]{1,0:T(8,128)(2,1)S(1)}, u32[]{:S(2)}) copy-start(bf16[96,2304]{1,0:T(8,128)(2,1)S(1)} %collective-permute-done.4.refs_1_) | copy-start | bytes 1327108
  80.2 14.3 %copy-start.6 = (bf16[96,2304]{1,0:T(8,128)(2,1)}, bf16[96,2304]{1,0:T(8,128)(2,1)S(1)}, u32[]{:S(2)}) copy-start(bf16[96,2304]{1,0:T(8,128)(2,1)S(1)} %collective-permute-done.5.refs_2_) | copy-start | bytes 1327108
  80.2 14.2 %copy-start.7 = (bf16[96,2304]{1,0:T(8,128)(2,1)}, bf16[96,2304]{1,0:T(8,128)(2,1)S(1)}, u32[]{:S(2)}) copy-start(bf16[96,2304]{1,0:T(8,128)(2,1)S(1)} %collective-permute-done.6.refs_3_) | copy-start | bytes 1327108
  80.3 13.5 %collective-permute-start.7 = (bf16[96,2304]{1,0:T(8,128)(2,1)S(1)}, bf16[96,2304]{1,0:T(8,128)(2,1)S(1)}, u32[]{:S(2)}, u32[]{:S(2)}) collective-permute-start(bf16[96,2304]{1,0:T(8,128)(2,1)S(1)} %pad_maximum_fusion.1.refs_0_), channel_id=1, source_target_pairs={{0,32},{32,0},{1,33},{33,1},{2,34},{34,2},{3,35},{35,3},{4,36},{36... | collective-permute-start | bytes 1327112 | tf_op jit(solution)/shard_map/stats/ppermute | solution.py:45
  80.7 13.1 %collective-permute-start.8 = (bf16[96,2304]{1,0:T(8,128)(2,1)S(1)}, bf16[96,2304]{1,0:T(8,128)(2,1)S(1)}, u32[]{:S(2)}, u32[]{:S(2)}) collective-permute-start(bf16[96,2304]{1,0:T(8,128)(2,1)S(1)} %collective-permute-done.4.refs_1_), channel_id=1, source_target_pairs={{0,32},{32,0},{1,33},{33,1},{2,34},{34,2},{3,35},{35,3},{4,36},{36... | collective-permute-start | bytes 1327112 | tf_op jit(solution)/shard_map/stats/ppermute | solution.py:45
  80.9 12.9 %collective-permute-start.9 = (bf16[96,2304]{1,0:T(8,128)(2,1)S(1)}, bf16[96,2304]{1,0:T(8,128)(2,1)S(1)}, u32[]{:S(2)}, u32[]{:S(2)}) collective-permute-start(bf16[96,2304]{1,0:T(8,128)(2,1)S(1)} %collective-permute-done.5.refs_2_), channel_id=1, source_target_pairs={{0,32},{32,0},{1,33},{33,1},{2,34},{34,2},{3,35},{35,3},{4,36},{36... | collective-permute-start | bytes 1327112 | tf_op jit(solution)/shard_map/stats/ppermute | solution.py:45
  81.2 12.6 %collective-permute-start.10 = (bf16[96,2304]{1,0:T(8,128)(2,1)S(1)}, bf16[96,2304]{1,0:T(8,128)(2,1)S(1)}, u32[]{:S(2)}, u32[]{:S(2)}) collective-permute-start(bf16[96,2304]{1,0:T(8,128)(2,1)S(1)} %collective-permute-done.6.refs_3_), channel_id=1, source_target_pairs={{0,32},{32,0},{1,33},{33,1},{2,34},{34,2},{3,35},{35,3},{4,36},{36... | collective-permute-start | bytes 1327112 | tf_op jit(solution)/shard_map/stats/ppermute | solution.py:45
  93.7 1.5 %copy-start.8 = (bf16[96,2304]{1,0:T(8,128)(2,1)}, bf16[96,2304]{1,0:T(8,128)(2,1)S(1)}, u32[]{:S(2)}) copy-start(bf16[96,2304]{1,0:T(8,128)(2,1)S(1)} %collective-permute-done.7.refs_4_) | copy-start | bytes 1327108
  93.8 1.5 %copy-start.9 = (bf16[96,2304]{1,0:T(8,128)(2,1)}, bf16[96,2304]{1,0:T(8,128)(2,1)S(1)}, u32[]{:S(2)}) copy-start(bf16[96,2304]{1,0:T(8,128)(2,1)S(1)} %collective-permute-done.8.refs_5_) | copy-start | bytes 1327108
  93.8 1.5 %copy-start.10 = (bf16[96,2304]{1,0:T(8,128)(2,1)}, bf16[96,2304]{1,0:T(8,128)(2,1)S(1)}, u32[]{:S(2)}) copy-start(bf16[96,2304]{1,0:T(8,128)(2,1)S(1)} %collective-permute-done.9.refs_6_) | copy-start | bytes 1327108
  93.8 1.5 %copy-start.11 = (bf16[96,2304]{1,0:T(8,128)(2,1)}, bf16[96,2304]{1,0:T(8,128)(2,1)S(1)}, u32[]{:S(2)}) copy-start(bf16[96,2304]{1,0:T(8,128)(2,1)S(1)} %collective-permute-done.10.refs_7_) | copy-start | bytes 1327108
  94.5 3.6 %collective-permute-start.12 = (bf16[192,2304]{1,0:T(8,128)(2,1)S(1)}, bf16[192,2304]{1,0:T(8,128)(2,1)S(1)}, u32[]{:S(2)}, u32[]{:S(2)}) collective-permute-start(bf16[192,2304]{1,0:T(8,128)(2,1)S(1)} %convolution_convert_fusion), channel_id=1, source_target_pairs={{0,32},{32,0},{1,33},{33,1},{2,34},{34,2},{3,35},{35,3},{4,36},{36... | collective-permute-start | bytes 2654216 | tf_op jit(solution)/shard_map/hidden_grad/ppermute | solution.py:45
  95.3 3.0 %collective-permute-start.11 = (bf16[192,2304]{1,0:T(8,128)(2,1)S(1)}, bf16[192,2304]{1,0:T(8,128)(2,1)S(1)}, u32[]{:S(2)}, u32[]{:S(2)}) collective-permute-start(bf16[192,2304]{1,0:T(8,128)(2,1)S(1)} %convolution_convert_fusion.1), channel_id=1, source_target_pairs={{0,32},{32,0},{1,33},{33,1},{2,34},{34,2},{3,35},{35,3},{4,36},{36... | collective-permute-start | bytes 2654216 | tf_op jit(solution)/shard_map/hidden_grad/ppermute | solution.py:45
  127.7 15.5 %all-to-all-start.5 = ((bf16[16,2,3456]{2,1,0:T(2,128)(2,1)}), bf16[16,2,3456]{2,1,0:T(2,128)(2,1)S(1)}, u32[]{:S(2)}, u32[]{:S(2)}) async-start(bf16[16,2,3456]{2,1,0:T(2,128)(2,1)} %plane_sum.1), calls=%async_computation.5 | async-start | bytes 442368 | tf_op jit(solution)/shard_map/hidden_grad/all_to_all | solution.py:40
